TPU v7x, 256 devices: a whole 4x4x8 slice. The times are simulated.
256 devices in a mesh: ctx: 16 (over z, y_hi), head: 16 (over y_lo, x, core).
Axes of the slice: x: 4, y: 4 (y_hi: 2, y_lo: 2; y = y_hi * 2 + y_lo), z: 8, core: 2. Of those that a mesh axis runs over, the one named last changes fastest.
Arguments:
- main_query: bfloat16 [4096, 128, 576], P('ctx', 'head'), may hold values from -12 to 12
- key_latent: bfloat16 [12288, 576], P('ctx'), may hold values from -6 to 6
- index_query: bfloat16 [4096, 64, 128], P('ctx', 'head'), may hold values from -0.53033009 to 0.53033009
- index_key: bfloat16 [12288, 128], P('ctx'), may hold values from -6 to 6
- index_weight: float32 [4096, 64], P('ctx', 'head'), may hold values from -1.6 to 1.6
- selection: int32 [16, 16], replicated, may hold values from 0 to 95, as said below
- loss_grad: float32 [4096], P('ctx'), may hold values from 8 to 64
Outputs:
- query_grad: float32 [4096, 64, 128], P('ctx', 'head')
- weight_grad: float32 [4096, 64], P('ctx', 'head')
- key_grad: float32 [12288, 128], P(('ctx', 'head'))
- query_loss: float32 [4096], P('ctx')
Inputs may be any that keep to these rules, and one draw needn't show every extreme that they name: `selection`: row b lists 16 different key tiles, all at or below key tile 16 * 4 + 2 * b + 1, and includes the 2 tiles from 16 * 4 + 2 * b upward. Within any aligned group of 6 tiles (the keys of one device) a row names at most 3 tiles; in every draw one group that lies below all queries is named exactly 3 times by every row.
All inputs are finite; a program needn't handle non-finite values.
Results may differ from a plain program's by a relative error of at most 0.012.
Values may be sent and summed in bfloat16 or wider, within the bound.
No kernel may reach another device: no remote copies, remote signals or barrier semaphores. Data moves between devices by JAX's collectives and lax.ppermute only.
A program may use at most 128 MiB of HBM per device.

v0:
```python
import functools
import math

import jax
import jax.numpy as jnp
from jax import lax
from jax.experimental import pallas as pl
from jax.experimental.pallas import tpu as pltpu
from jax.sharding import Mesh, PartitionSpec as P

TILE = 128
MLA_HEADS = 128
OWNER_MOST = 3
QROWS = 16
STRIPE = 8
VMEM = 60 * 1024 * 1024

SLOTS, CORE, FIRST = 16, 18, 19

CTX = ("z", "yh")
HEAD = ("yl", "x", "core")
ROWS = ("core", "yl", "x")
exp_scale = 192.0 ** (-0.5) * math.log2(math.e)
far_below = -1e30


def allowed_keys(query_first, key_pos):
    rows = lax.broadcasted_iota(jnp.int32, (QROWS, key_pos.shape[1]), 0)
    return key_pos <= rows + query_first


def stripes_kernel(where, selection, index_key, key_latent, send):
    ctx, lane = where[0], where[1]
    rows, (blocks, slots) = send.shape[0], selection.shape
    per_block = OWNER_MOST * STRIPE
    tiles = index_key.shape[0] // TILE
    row = lax.broadcasted_iota(jnp.int32, (rows, slots), 0)
    slot = lax.broadcasted_iota(jnp.int32, (rows, slots), 1)
    first = slot * per_block
    repeat = ((row >= first) & (row < first + per_block)).astype(jnp.float32)
    picked = jnp.dot(
        repeat.astype(jnp.bfloat16),
        selection[...].astype(jnp.float32).astype(jnp.bfloat16),
        preferred_element_type=jnp.float32,
    ).astype(jnp.int32)
    inner = picked - ctx * tiles
    mine = (inner >= 0) & (inner < tiles)
    a = lax.broadcasted_iota(jnp.int32, (slots, slots), 0)
    b = lax.broadcasted_iota(jnp.int32, (slots, slots), 1)
    earlier = (a < b).astype(jnp.float32).astype(jnp.bfloat16)
    rank = jnp.dot(
        mine.astype(jnp.float32).astype(jnp.bfloat16), earlier, preferred_element_type=jnp.float32
    ).astype(jnp.int32)
    block = jnp.sum(jnp.where(repeat > 0, slot, 0), axis=1, keepdims=True)
    row = lax.broadcasted_iota(jnp.int32, (rows, 1), 0)
    wanted = lax.shift_right_logical(row - block * per_block, 3)
    source = inner * TILE + lane * STRIPE + (row & (STRIPE - 1)) + 1
    source = jnp.sum(jnp.where(mine & (rank == wanted), source, 0), axis=1, keepdims=True) - 1
    spot = lax.broadcasted_iota(jnp.int32, (rows, index_key.shape[0]), 1)
    pick = (spot == source).astype(jnp.float32).astype(jnp.bfloat16)
    send[:, :TILE] = jnp.dot(pick, index_key[...], preferred_element_type=jnp.float32).astype(
        jnp.bfloat16
    )
    send[:, TILE:] = lax.dot_general(
        pick, key_latent[...], (((1,), (1,)), ((), ())), preferred_element_type=jnp.float32
    ).astype(jnp.bfloat16)


def attend_kernel(facts, *refs):
    pieces, (q_own, q_other, target, index_keys, keys, total, *raw) = refs[:16], refs[16:]
    for i, piece in enumerate(pieces):
        spot = pl.ds(pl.multiple_of(facts[i] * TILE, TILE), TILE)
        index_keys[spot, :] = piece[:, :TILE]
        keys[spot, :] = piece[:, TILE:]
    span = keys.shape[0]
    shape = (STRIPE, 2 * TILE)
    behind = lax.broadcasted_iota(jnp.int32, shape, 0) - (
        lax.broadcasted_iota(jnp.int32, shape, 1) & (TILE - 1)
    )
    behind = behind - facts[CORE] * TILE
    pairs = [(part, head) for part in (q_own, q_other) for head in range(0, part.shape[0], 2)]

    def scores(step):
        part, head = pairs[step]
        both = jnp.concatenate([part[head], part[head + 1]], axis=1)
        out = raw[step % 2]
        out[...] = jnp.dot(keys[...], both, preferred_element_type=jnp.float32)
        for tile in range(2):
            for stripe in range(span // TILE):
                spot = pl.ds(pl.multiple_of(stripe * TILE + facts[SLOTS + tile] * STRIPE, STRIPE), STRIPE)
                late = behind + (tile * TILE + stripe * STRIPE) > 0
                out[spot, :] = jnp.where(late, far_below, out[spot, :])

    def softmax(step):
        part = raw[step % 2]
        spots = [slice(i, i + TILE) for i in range(0, span, TILE)]
        folded = (TILE // 8, 8, 2 * TILE)
        top = functools.reduce(
            jnp.maximum, [jnp.max(part[spot, :].reshape(folded), axis=0) for spot in spots]
        )
        top = jnp.max(top, axis=0, keepdims=True)
        row_sum = jnp.zeros((8, 2 * TILE), jnp.float32)
        for spot in spots:
            weights = jnp.exp2((part[spot, :] - top) * exp_scale)
            part[spot, :] = weights
            row_sum = row_sum + jnp.sum(weights.reshape(folded), axis=0)
        share = 1.0 / (jnp.sum(row_sum, axis=0, keepdims=True) * MLA_HEADS)
        for spot in spots:
            weights = part[spot, :] * share
            weights = weights[:, :TILE] + weights[:, TILE:]
            if step == 0:
                total[spot, :] = weights
            else:
                total[spot, :] += weights

    for step in range(len(pairs)):
        scores(step)
        if step:
            softmax(step - 1)
    softmax(len(pairs) - 1)
    for i in range(0, span, TILE):
        target[:, i : i + TILE] = total[i : i + TILE, :].T


def row_groups(rows, heads):
    row = lax.broadcasted_iota(jnp.int32, (rows, rows * heads), 0) * heads
    both = lax.broadcasted_iota(jnp.int32, (rows, rows * heads), 1)
    return ((both >= row) & (both < row + heads)).astype(jnp.float32)


def index_logits(queries, keys, step, count):
    block = queries[step * count : (step + 1) * count, :, :TILE]
    return lax.dot_general(
        block.reshape(-1, TILE),
        keys[...],
        (((1,), (1,)), ((), ())),
        preferred_element_type=jnp.float32,
    ).reshape(count, -1, keys.shape[0])


def index_weights(queries, step, count):
    terms = queries[step * count : (step + 1) * count, :, TILE : 2 * TILE].astype(jnp.float32)
    return terms[:, :, 0:1] + terms[:, :, 1:2] + terms[:, :, 2:3]


def score_kernel(queries, keys, score):
    count = 2
    heads_rows = queries.shape[1]
    total = jnp.zeros((heads_rows, keys.shape[0]), jnp.float32)
    for step in range(queries.shape[0] // count):
        lifted = jnp.maximum(index_logits(queries, keys, step, count), 0.0)
        total = total + jnp.sum(lifted * index_weights(queries, step, count), axis=0)
    score[...] = jnp.dot(
        row_groups(QROWS, heads_rows // QROWS),
        total,
        precision=lax.Precision.HIGHEST,
        preferred_element_type=jnp.float32,
    )


def grad_kernel(
    facts, target_parts, score, queries, keys, key_pos, loss_grad,
    query_grad, weight_grad, key_grad, loss, coef
):
    allowed = allowed_keys(facts[FIRST], key_pos[...])
    target = jnp.sum(target_parts[...], axis=0)
    masked = jnp.where(allowed, score[...], far_below)
    shifted = masked - jnp.max(masked, axis=-1, keepdims=True)
    weights = jnp.where(allowed, jnp.exp(shifted), 0.0)
    row_sum = jnp.sum(weights, axis=-1, keepdims=True)
    log_prob = shifted - jnp.log(row_sum)
    positive = target > 0
    self_term = jnp.where(positive, target * jnp.log(jnp.where(positive, target, 1.0)), 0.0)
    loss[...] = jnp.sum(
        jnp.where(allowed, self_term - target * log_prob, 0.0), axis=-1, keepdims=True
    )
    score_grad = loss_grad[...] * jnp.where(allowed, weights / row_sum - target, 0.0)
    count = 2
    sources, heads_rows = queries.shape[:2]
    score_grad = lax.dot_general(
        row_groups(QROWS, heads_rows // QROWS),
        score_grad,
        (((0,), (0,)), ((), ())),
        precision=lax.Precision.HIGHEST,
        preferred_element_type=jnp.float32,
    )[None]
    rows = count * heads_rows
    for step in range(sources // count):
        spot = slice(step * rows, (step + 1) * rows)
        logits = index_logits(queries, keys, step, count)
        scaled = score_grad * index_weights(queries, step, count)
        scaled = jnp.where(logits > 0, scaled, 0.0).reshape(rows, -1)
        coef[spot, :] = scaled.astype(jnp.bfloat16)
        lifted = score_grad * jnp.maximum(logits, 0.0)
        weight_grad[spot, :] = jnp.sum(lifted, axis=-1, keepdims=True).reshape(rows, 1)
    query_grad[...] = jnp.dot(coef[...], keys[...], preferred_element_type=jnp.float32)
    flat = queries[:, :, :TILE].reshape(sources * heads_rows, TILE)
    flat = lax.dot_general(
        flat, coef[...], (((0,), (0,)), ((), ())), preferred_element_type=jnp.float32
    )
    for lane in range(key_grad.shape[0] * key_grad.shape[1]):
        key_grad[lane % 2, lane // 2] = flat[:, lane * TILE : (lane + 1) * TILE]


def whole(shape):
    return pl.BlockSpec(shape, lambda *_: (0,) * len(shape))


def one_hot_rows(table, block):
    a, b = table.shape
    eye = jnp.eye(block, dtype=table.dtype)
    return (table[:, None, :, None] * eye[None, :, None, :]).reshape(a * block, b * block)


def body(main_query, key_latent, index_query, index_key, index_weight, selection, loss_grad):
    bf16, f32 = jnp.bfloat16, jnp.float32
    ctx_index = lax.axis_index(CTX)
    ctx_count = lax.axis_size(CTX)
    lane = lax.axis_index(HEAD)
    lanes = lax.axis_size(HEAD)
    yl, x, core = lax.axis_index("yl"), lax.axis_index("x"), lax.axis_index("core")
    x_count = lax.axis_size("x")
    query_rows, main_local, lat_width = main_query.shape
    index_local, idx_width = index_query.shape[1:]
    key_tiles = key_latent.shape[0] // TILE
    sel_count = selection.shape[1]
    key_span = sel_count * TILE
    context = key_tiles * TILE * ctx_count
    width = idx_width + lat_width
    heads_all = lanes * index_local
    rows_all = heads_all * QROWS
    heads_rows = index_local * QROWS
    swap = [(0, 1), (1, 0)]
    params = pltpu.CompilerParams(vmem_limit_bytes=VMEM)
    vmem = pl.BlockSpec(memory_space=pltpu.VMEM)
    smem = pl.BlockSpec(memory_space=pltpu.SMEM)

    def shifted(value, shift):
        ring = [(i, (i + shift) % x_count) for i in range(x_count)]
        return lax.ppermute(value, "x", ring)

    send = pl.pallas_call(
        stripes_kernel,
        in_specs=[smem, vmem, vmem, vmem],
        out_shape=jax.ShapeDtypeStruct((ctx_count * OWNER_MOST * STRIPE, width), bf16),
        compiler_params=params,
        name="stripes",
    )(jnp.stack([ctx_index, lane]).astype(jnp.int32), selection, index_key, key_latent.T)
    arrived = lax.all_to_all(send, CTX, 0, 0, tiled=True)

    queries = jnp.transpose(main_query, (1, 2, 0))
    q_other = lax.dynamic_slice_in_dim(queries, (1 - core) * TILE, TILE, 2)
    q_other = lax.ppermute(q_other, "core", swap)

    first_term = lax.reduce_precision(index_weight, 8, 7)
    rest = index_weight - first_term
    second_term = lax.reduce_precision(rest, 8, 7)
    terms = jnp.stack([first_term, second_term, rest - second_term], axis=-1).astype(bf16)
    iq = jnp.concatenate(
        [index_query, jnp.pad(terms, ((0, 0), (0, 0), (0, idx_width - 3)))], axis=-1
    ).reshape(lanes, heads_rows, 2 * idx_width)

    owner = selection // key_tiles
    inner = selection % key_tiles
    earlier = jnp.tril(jnp.ones((sel_count, sel_count), jnp.int32), -1)
    rank = jnp.sum((owner[:, :, None] == owner[:, None, :]) * earlier[None], axis=2)
    ranks = jnp.arange(OWNER_MOST)
    picked = lax.dynamic_index_in_dim(selection, ctx_index, 0, keepdims=False)
    my_owner = lax.dynamic_index_in_dim(owner, ctx_index, 0, keepdims=False)
    my_rank = lax.dynamic_index_in_dim(rank, ctx_index, 0, keepdims=False)
    sent = jnp.any(
        (owner[:, None, :, None] == ctx_index)
        & (rank[:, None, :, None] == ranks[None, :, None, None])
        & (inner[:, None, :, None] == jnp.arange(key_tiles)[None, None, None, :]),
        axis=2,
    ).reshape(ctx_count * OWNER_MOST, key_tiles)
    got = (
        (my_owner[:, None, None] == jnp.arange(ctx_count)[None, :, None])
        & (my_rank[:, None, None] == ranks[None, None, :])
    ).reshape(sel_count, ctx_count * OWNER_MOST)
    got_rows = one_hot_rows(got.astype(bf16), STRIPE)
    sent_rows = one_hot_rows(sent.astype(bf16), STRIPE)
    chunk = core * (lanes // 2) + yl * x_count + x
    grad_rows = lax.dynamic_slice_in_dim(loss_grad, chunk * QROWS, QROWS, 0).reshape(QROWS, 1)
    key_pos = (
        jnp.arange(lanes)[:, None, None] * STRIPE
        + picked[None, :, None] * TILE
        + jnp.arange(STRIPE)[None, None, :]
    ).reshape(1, key_span)
    place = [
        ((yl ^ j) * x_count + (x - shift) % x_count) * 2 + (core ^ k)
        for k in range(2)
        for j in range(2)
        for shift in (0, 1, 3, 2)
    ]
    block_first = context - query_rows * ctx_count + ctx_index * query_rows
    own = block_first // TILE + jnp.arange(2)
    slots = jnp.argmax(picked[None, :] == own[:, None], axis=1)
    facts = jnp.concatenate(
        [jnp.stack(place), slots, jnp.stack([core, block_first + chunk * QROWS])]
    ).astype(jnp.int32)
    arrived, got_rows, sent_rows, key_pos, grad_rows, facts, iq = lax.optimization_barrier(
        (arrived, got_rows, sent_rows, key_pos, grad_rows, facts, iq)
    )
    stripe = jnp.dot(got_rows, arrived, preferred_element_type=bf16)

    other = lax.ppermute(stripe, "yl", swap)
    pieces = [stripe] + [shifted(stripe, shift) for shift in (1, 3, 2)]
    iq, *pieces = lax.optimization_barrier((iq, *pieces))
    iq = lax.all_to_all(iq, ROWS, 0, 0, tiled=True)
    pieces += [other] + [shifted(other, shift) for shift in (1, 3, 2)]
    pieces += [lax.ppermute(piece, "core", swap) for piece in pieces]

    count = 2 * main_local * TILE
    target_part, index_keys = pl.pallas_call(
        attend_kernel,
        grid_spec=pltpu.PrefetchScalarGridSpec(
            num_scalar_prefetch=1,
            grid=(1,),
            in_specs=[whole((TILE, width))] * 16
            + [
                pl.BlockSpec((main_local, lat_width, TILE), lambda i, facts: (0, 0, facts[CORE])),
                whole((main_local, lat_width, TILE)),
            ],
            out_specs=[whole((TILE, key_span)), whole((key_span, idx_width))],
            scratch_shapes=[
                pltpu.VMEM((key_span, lat_width), bf16),
                pltpu.VMEM((key_span, TILE), f32),
                pltpu.VMEM((key_span, 2 * TILE), f32),
                pltpu.VMEM((key_span, 2 * TILE), f32),
            ],
        ),
        out_shape=[
            jax.ShapeDtypeStruct((TILE, key_span), f32),
            jax.ShapeDtypeStruct((key_span, idx_width), bf16),
        ],
        compiler_params=params,
        cost_estimate=pl.CostEstimate(
            flops=2 * count * key_span * lat_width,
            bytes_accessed=8 * 2**20,
            transcendentals=count * key_span,
        ),
        name="attend",
    )(facts, *pieces, queries, q_other)
    target_parts = lax.all_to_all(target_part, ("yl", "x"), 0, 0, tiled=True)
    target_parts = target_parts.reshape(lanes // 2, QROWS, key_span)

    score = pl.pallas_call(
        score_kernel,
        grid=(1,),
        in_specs=[whole(iq.shape), whole((key_span, idx_width))],
        out_specs=whole((QROWS, key_span)),
        out_shape=jax.ShapeDtypeStruct((QROWS, key_span), f32),
        compiler_params=params,
        cost_estimate=pl.CostEstimate(
            flops=2 * rows_all * key_span * idx_width, bytes_accessed=2**20, transcendentals=0
        ),
        name="score",
    )(iq, index_keys)

    query_grad, weight_grad, key_part, loss = pl.pallas_call(
        grad_kernel,
        grid=(1,),
        in_specs=[smem]
        + [whole((lanes // 2, QROWS, key_span)), whole((QROWS, key_span))]
        + [whole(iq.shape), whole((key_span, idx_width)), whole((1, key_span)), whole((QROWS, 1))],
        out_specs=[
            whole((rows_all, idx_width)),
            whole((rows_all, 1)),
            whole((2, lanes // 2, idx_width, TILE)),
            whole((QROWS, 1)),
        ],
        out_shape=[
            jax.ShapeDtypeStruct((rows_all, idx_width), f32),
            jax.ShapeDtypeStruct((rows_all, 1), f32),
            jax.ShapeDtypeStruct((2, lanes // 2, idx_width, TILE), f32),
            jax.ShapeDtypeStruct((QROWS, 1), f32),
        ],
        scratch_shapes=[pltpu.VMEM((rows_all, key_span), bf16)],
        compiler_params=params,
        cost_estimate=pl.CostEstimate(
            flops=6 * rows_all * key_span * idx_width, bytes_accessed=4 * 2**20, transcendentals=0
        ),
        name="grad",
    )(facts, target_parts, score, iq, index_keys, key_pos, grad_rows)

    exact = lax.Precision.HIGHEST
    key_keep = lax.dynamic_index_in_dim(key_part, core, 0, keepdims=False)
    key_give = lax.dynamic_index_in_dim(key_part, 1 - core, 0, keepdims=False)
    key_sum = key_keep + lax.ppermute(key_give, "core", swap)
    key_sum = jnp.sum(
        lax.all_to_all(key_sum, ("yl", "x"), 0, 0, tiled=True), axis=0
    )
    back = lax.dot_general(
        got_rows.astype(f32), key_sum, (((0,), (1,)), ((), ())), precision=exact
    )
    back = lax.all_to_all(back, CTX, 0, 0, tiled=True)
    own_blocks = lax.dot_general(
        sent_rows.astype(f32), back, (((0,), (0,)), ((), ())), precision=exact
    ).reshape(key_tiles, STRIPE, idx_width)
    order = jnp.arange(lanes)
    natural = order % (lanes // 2) * 2 + order // (lanes // 2)
    goes = (jnp.arange(key_tiles)[None, :] * lanes + lane) // key_tiles == natural[:, None]
    key_send = jnp.sum(jnp.where(goes[:, :, None, None], own_blocks[None], 0.0), axis=1)

    small = jnp.concatenate(
        [
            weight_grad.reshape(lanes, heads_rows),
            jnp.broadcast_to(loss.reshape(1, QROWS), (lanes, QROWS)),
            jnp.zeros((lanes, idx_width - heads_rows - QROWS), f32),
        ],
        axis=1,
    ).reshape(lanes, 1, idx_width)
    packed = jnp.concatenate(
        [query_grad.reshape(lanes, heads_rows, idx_width), key_send, small], axis=1
    )
    packed = lax.all_to_all(packed, ROWS, 0, 0, tiled=True)
    query_out = packed[:, :heads_rows].reshape(query_rows, index_local, idx_width)
    blocks = packed[:, heads_rows : heads_rows + STRIPE]
    source = (lane * key_tiles + jnp.arange(key_tiles)) % lanes
    source = source % 2 * (lanes // 2) + source // 2
    comes = source[:, None] == order[None, :]
    key_out = jnp.sum(jnp.where(comes[:, :, None, None], blocks[None], 0.0), axis=1)
    key_out = key_out.reshape(key_tiles * STRIPE, idx_width)
    small = packed[:, heads_rows + STRIPE]
    weight_out = small[:, :heads_rows].reshape(query_rows, index_local)
    loss_out = small[:, heads_rows : heads_rows + QROWS].reshape(query_rows)
    return (query_out, weight_out, key_out, loss_out)


def solution(mesh):
    fine = Mesh(mesh.devices.reshape(8, 2, 2, 4, 2), CTX + HEAD)
    return jax.shard_map(
        body,
        mesh=fine,
        in_specs=(
            P(CTX, HEAD, None),
            P(CTX, None),
            P(CTX, HEAD, None),
            P(CTX, None),
            P(CTX, HEAD),
            P(),
            P(CTX),
        ),
        out_specs=(P(CTX, HEAD, None), P(CTX, HEAD), P(CTX + HEAD, None), P(CTX)),
        check_vma=False,
    )
```

profile of v0, /device:TPU:1, one launch (start us, length us, event | category | flops | bytes accessed | tf_op | source)
XLA Modules:
  0.0 171.0 jit_solution(6388957238114530612)
XLA Ops:
  1.3 3.4 %stripes.1 = bf16[384,704]{1,0:T(8,128)(2,1)} custom-call(s32[2]{0:T(128)} %pad_add_fusion.where, s32[16,16]{1,0:T(8,128)} %selection.1, bf16[768,128]{1,0:T(8,128)(2,1)} %index_key.1, bf16[576,768]{1,0:T(8,128)(2,1)} %bitcast.84), custom_call_target="tpu_custom_call" | custom-call | tf_op jit(solution)/shard_map/stripes/pallas_call | solution.py:242
  4.7 11.9 %all-to-all-start = ((bf16[16,24,704]{2,1,0:T(8,128)(2,1)}), bf16[16,24,704]{2,1,0:T(8,128)(2,1)S(1)}, u32[]{:S(2)}, u32[]{:S(2)}) async-start(bf16[16,24,704]{2,1,0:T(8,128)(2,1)} %bitcast.82), calls=%async_computation | async-start | bytes 1179648 | tf_op jit(solution)/shard_map/all_to_all | solution.py:249
  20.8 1.8 %mul.166 = bf16[128,384]{1,0:T(8,128)(2,1)S(1)} reshape(bf16[16,8,48,8]{3,2,1,0:T(8,128)(2,1)S(1)} %broadcast_multiply_fusion) | data formatting | bytes 196608 | tf_op jit(solution)/shard_map/mul | solution.py:212
  27.7 7.2 %all-to-all-done = bf16[16,24,704]{2,1,0:T(8,128)(2,1)S(1)} async-done(((bf16[16,24,704]{2,1,0:T(8,128)(2,1)}), bf16[16,24,704]{2,1,0:T(8,128)(2,1)S(1)}, u32[]{:S(2)}, u32[]{:S(2)}) %all-to-all-start) | async-done | bytes 540704 | tf_op jit(solution)/shard_map/all_to_all | solution.py:249
  38.2 1.5 collective-permute-start.2
  41.3 4.0 %collective-permute-done.2.refs_3_ = bf16[128,704]{1,0:T(8,128)(2,1)S(1)} collective-permute-done((bf16[128,704]{1,0:T(8,128)(2,1)S(1)}, bf16[128,704]{1,0:T(8,128)(2,1)S(1)}, u32[]{:S(2)}, u32[]{:S(2)}) %collective-permute-start.2) | collective-permute-done | bytes 180256 | tf_op jit(solution)/shard_map/ppermute | solution.py:240
  45.4 4.1 %collective-permute-start.7 = (bf16[128,704]{1,0:T(8,128)(2,1)S(1)}, bf16[128,704]{1,0:T(8,128)(2,1)S(1)}, u32[]{:S(2)}, u32[]{:S(2)}) collective-permute-start(bf16[128,704]{1,0:T(8,128)(2,1)S(1)} %copy.77.refs_0_), channel_id=1, source_target_pairs={{0,1},{1,0},{2,3},{3,2},{4,5},{5,4},{6,7},{7,6},{8,9},{9,8},{10,11... | collective-permute-start | bytes 540680 | tf_op jit(solution)/shard_map/ppermute | solution.py:312
  50.9 1.8 %collective-permute-start.5 = (bf16[128,704]{1,0:T(8,128)(2,1)S(1)}, bf16[128,704]{1,0:T(8,128)(2,1)S(1)}, u32[]{:S(2)}, u32[]{:S(2)}) collective-permute-start(bf16[128,704]{1,0:T(8,128)(2,1)S(1)} %collective-permute-done.3.refs_4_), channel_id=1, source_target_pairs={{0,6},{2,0},{4,2},{6,4},{1,7},{3,1},{5,3},{7,5},{8,14},{10,8},{12,... | collective-permute-start | bytes 540680 | tf_op jit(solution)/shard_map/ppermute | solution.py:240
  54.2 3.3 %collective-permute-done.4.refs_5_ = bf16[128,704]{1,0:T(8,128)(2,1)S(1)} collective-permute-done((bf16[128,704]{1,0:T(8,128)(2,1)S(1)}, bf16[128,704]{1,0:T(8,128)(2,1)S(1)}, u32[]{:S(2)}, u32[]{:S(2)}) %collective-permute-start.4) | collective-permute-done | bytes 180256 | tf_op jit(solution)/shard_map/ppermute | solution.py:240
  57.5 1.5 collective-permute-start.12
  59.1 3.0 %collective-permute-start.13 = (bf16[128,704]{1,0:T(8,128)(2,1)S(1)}, bf16[128,704]{1,0:T(8,128)(2,1)}, u32[]{:S(2)}, u32[]{:S(2)}) collective-permute-start(bf16[128,704]{1,0:T(8,128)(2,1)S(1)} %collective-permute-done.5.refs_6_), channel_id=1, source_target_pairs={{0,1},{1,0},{2,3},{3,2},{4,5},{5,4},{6,7},{7,6},{8,9},{9,8},{10,11... | collective-permute-start | bytes 540680 | tf_op jit(solution)/shard_map/ppermute | solution.py:312
  63.0 4.7 %all-to-all-start.2 = ((bf16[16,64,256]{2,1,0:T(8,128)(2,1)}), bf16[16,64,256]{2,1,0:T(8,128)(2,1)S(1)}, u32[]{:S(2)}, u32[]{:S(2)}) async-start(bf16[16,64,256]{2,1,0:T(8,128)(2,1)} %reshape.394), calls=%async_computation.2 | async-start | bytes 1048576 | tf_op jit(solution)/shard_map/all_to_all | solution.py:310
  68.4 15.1 %attend.1 = (f32[128,2048]{1,0:T(8,128)}, bf16[2048,128]{1,0:T(8,128)(2,1)}) custom-call(s32[20]{0:T(128)} %concatenate.12.facts, bf16[128,704]{1,0:T(8,128)(2,1)} %copy-done.7, bf16[128,704]{1,0:T(8,128)(2,1)} %copy-done.11, bf16[128,704]{1,0:T(8,128)(2,1)} %copy-done.12, bf16[128,704]{1,0:T(8,128)(2,1)} %copy-done.13, bf16[128,704]{1,0:T(8,128)(2,1)} %copy-done.14, ...), custom_call_target="tpu_custom_call" | custom-call | flops 4831838208 | bytes 8388608 | tf_op jit(solution)/shard_map/attend/pallas_call | solution.py:315
  83.5 5.1 %all-to-all-start.1 = ((f32[8,16,2048]{2,1,0:T(8,128)}), f32[8,16,2048]{2,1,0:T(8,128)S(1)}, u32[]{:S(2)}, u32[]{:S(2)}) async-start(f32[8,16,2048]{2,1,0:T(8,128)} %bitcast.83), calls=%async_computation.1 | async-start | bytes 2097152 | tf_op jit(solution)/shard_map/all_to_all | solution.py:345
  89.3 3.5 %score.1 = f32[16,2048]{1,0:T(8,128)} custom-call(bf16[16,64,256]{2,1,0:T(8,128)(2,1)} %copy-done.5, bf16[2048,128]{1,0:T(8,128)(2,1)} %get-tuple-element.34.keys), custom_call_target="tpu_custom_call" | custom-call | flops 536870912 | bytes 1048576 | tf_op jit(solution)/shard_map/score/pallas_call | solution.py:348
  92.7 11.7 %all-to-all-done.1.target_parts = f32[8,16,2048]{2,1,0:T(8,128)S(1)} async-done(((f32[8,16,2048]{2,1,0:T(8,128)}), f32[8,16,2048]{2,1,0:T(8,128)S(1)}, u32[]{:S(2)}, u32[]{:S(2)}) %all-to-all-start.1) | async-done | bytes 1048608 | tf_op jit(solution)/shard_map/all_to_all | solution.py:345
  105.5 6.5 %grad.1 = (f32[1024,128]{1,0:T(8,128)}, f32[1024,1]{1,0:T(8,128)}, f32[2,8,128,128]{3,2,1,0:T(8,128)}, f32[16,1]{1,0:T(8,128)}) custom-call(s32[20]{0:T(128)} %concatenate.12.facts, f32[8,16,2048]{2,1,0:T(8,128)} %copy-done.1, f32[16,2048]{1,0:T(8,128)} %score.1, bf16[16,64,256]{2,1,0:T(8,128)(2,1)} %copy-done.5, bf16[2048,128]{1,0:T(8,128)(2,1)} %get-tuple-element.34.keys, ...), custom_call_target="tpu_custom_call" | custom-call | flops 1610612736 | bytes 4194304 | tf_op jit(solution)/shard_map/grad/pallas_call | solution.py:361
  115.5 1.9 %bitcast_add_fusion = f32[8,128,128]{2,1,0:T(8,128)} fusion(f32[8,128,128]{2,1,0:T(8,128)S(1)} %collective-permute-done.16, f32[2,8,128,128]{3,2,1,0:T(8,128)} %get-tuple-element.39, s32[]{:T(128)S(6)} %select_n.167), kind=kLoop, calls=%fused_computation.8 | loop fusion | flops 131072 | bytes 1572868 | tf_op jit(solution)/shard_map/add | solution.py:390
  117.4 3.6 %all-to-all-start.3 = ((f32[8,128,128]{2,1,0:T(8,128)}), f32[8,128,128]{2,1,0:T(8,128)S(1)}, u32[]{:S(2)}, u32[]{:S(2)}) async-start(f32[8,128,128]{2,1,0:T(8,128)} %bitcast_add_fusion), calls=%async_computation.3 | async-start | bytes 1048576 | tf_op jit(solution)/shard_map/all_to_all | solution.py:392
  121.3 10.0 %all-to-all-done.3 = f32[8,128,128]{2,1,0:T(8,128)S(1)} async-done(((f32[8,128,128]{2,1,0:T(8,128)}), f32[8,128,128]{2,1,0:T(8,128)S(1)}, u32[]{:S(2)}, u32[]{:S(2)}) %all-to-all-start.3) | async-done | bytes 524320 | tf_op jit(solution)/shard_map/all_to_all | solution.py:392
  132.2 5.5 %all-to-all-start.4 = ((f32[16,24,128]{2,1,0:T(8,128)}), f32[16,24,128]{2,1,0:T(8,128)S(1)}, u32[]{:S(2)}, u32[]{:S(2)}) async-start(f32[16,24,128]{2,1,0:T(8,128)} %fusion.5), calls=%async_computation.4 | async-start | bytes 393216 | tf_op jit(solution)/shard_map/all_to_all | solution.py:397
  138.3 10.1 %all-to-all-done.4 = f32[16,24,128]{2,1,0:T(8,128)S(1)} async-done(((f32[16,24,128]{2,1,0:T(8,128)}), f32[16,24,128]{2,1,0:T(8,128)S(1)}, u32[]{:S(2)}, u32[]{:S(2)}) %all-to-all-start.4) | async-done | bytes 196640 | tf_op jit(solution)/shard_map/all_to_all | solution.py:397
  149.8 6.1 %all-to-all-start.5 = ((f32[16,73,128]{2,1,0:T(8,128)}), f32[16,73,128]{2,1,0:T(8,128)S(1)}, u32[]{:S(2)}, u32[]{:S(2)}) async-start(f32[16,73,128]{2,1,0:T(8,128)} %pad_maximum_fusion), calls=%async_computation.5 | async-start | bytes 1310720 | tf_op jit(solution)/shard_map/all_to_all | solution.py:417
  156.0 11.9 %all-to-all-done.5 = f32[16,73,128]{2,1,0:T(8,128)S(1)} async-done(((f32[16,73,128]{2,1,0:T(8,128)}), f32[16,73,128]{2,1,0:T(8,128)S(1)}, u32[]{:S(2)}, u32[]{:S(2)}) %all-to-all-start.5) | async-done | bytes 598048 | tf_op jit(solution)/shard_map/all_to_all | solution.py:417
  (142 shorter events, 30.3 us)
Async XLA Ops:
  4.7 30.3 %all-to-all-start = ((bf16[16,24,704]{2,1,0:T(8,128)(2,1)}), bf16[16,24,704]{2,1,0:T(8,128)(2,1)S(1)}, u32[]{:S(2)}, u32[]{:S(2)}) async-start(bf16[16,24,704]{2,1,0:T(8,128)(2,1)} %bitcast.82), calls=%async_computation | async-start | bytes 1179648 | tf_op jit(solution)/shard_map/all_to_all | solution.py:249
  17.8 33.1 %collective-permute-start.15 = (bf16[8,576,128]{2,1,0:T(8,128)(2,1)}, bf16[8,576,128]{2,1,0:T(8,128)(2,1)}, u32[]{:S(2)}, u32[]{:S(2)}) collective-permute-start(bf16[8,576,128]{2,1,0:T(8,128)(2,1)} %dynamic-slice_bitcast_fusion), channel_id=1, source_target_pairs={{0,1},{1,0},{2,3},{3,2},{4,5},{5,4},{6,7},{7,6},{8,9},{9,8},{10,11... | collective-permute-start | bytes 3538952 | tf_op jit(solution)/shard_map/ppermute | solution.py:253
  35.5 5.8 %collective-permute-start = (bf16[128,704]{1,0:T(8,128)(2,1)S(1)}, bf16[128,704]{1,0:T(8,128)(2,1)S(1)}, u32[]{:S(2)}, u32[]{:S(2)}) collective-permute-start(bf16[128,704]{1,0:T(8,128)(2,1)S(1)} %copy.72), channel_id=1, source_target_pairs={{0,2},{2,4},{4,6},{6,0},{1,3},{3,5},{5,7},{7,1},{8,10},{10,12},{12... | collective-permute-start | bytes 540680 | tf_op jit(solution)/shard_map/ppermute | solution.py:240
  36.8 4.5 %collective-permute-start.1 = (bf16[128,704]{1,0:T(8,128)(2,1)S(1)}, bf16[128,704]{1,0:T(8,128)(2,1)S(1)}, u32[]{:S(2)}, u32[]{:S(2)}) collective-permute-start(bf16[128,704]{1,0:T(8,128)(2,1)S(1)} %copy.72), channel_id=1, source_target_pairs={{0,6},{2,0},{4,2},{6,4},{1,7},{3,1},{5,3},{7,5},{8,14},{10,8},{12,... | collective-permute-start | bytes 540680 | tf_op jit(solution)/shard_map/ppermute | solution.py:240
  38.2 7.0 %collective-permute-start.2 = (bf16[128,704]{1,0:T(8,128)(2,1)S(1)}, bf16[128,704]{1,0:T(8,128)(2,1)S(1)}, u32[]{:S(2)}, u32[]{:S(2)}) collective-permute-start(bf16[128,704]{1,0:T(8,128)(2,1)S(1)} %copy.72), channel_id=1, source_target_pairs={{0,4},{2,6},{4,0},{6,2},{1,5},{3,7},{5,1},{7,3},{8,12},{10,14},{12... | collective-permute-start | bytes 540680 | tf_op jit(solution)/shard_map/ppermute | solution.py:240
  39.8 10.3 %collective-permute-start.3 = (bf16[128,704]{1,0:T(8,128)(2,1)S(1)}, bf16[128,704]{1,0:T(8,128)(2,1)S(1)}, u32[]{:S(2)}, u32[]{:S(2)}) collective-permute-start(bf16[128,704]{1,0:T(8,128)(2,1)S(1)} %copy.72), channel_id=1, source_target_pairs={{0,8},{8,0},{1,9},{9,1},{2,10},{10,2},{3,11},{11,3},{4,12},{12,4},... | collective-permute-start | bytes 540680 | tf_op jit(solution)/shard_map/ppermute | solution.py:307
  45.4 7.3 %collective-permute-start.7 = (bf16[128,704]{1,0:T(8,128)(2,1)S(1)}, bf16[128,704]{1,0:T(8,128)(2,1)S(1)}, u32[]{:S(2)}, u32[]{:S(2)}) collective-permute-start(bf16[128,704]{1,0:T(8,128)(2,1)S(1)} %copy.77.refs_0_), channel_id=1, source_target_pairs={{0,1},{1,0},{2,3},{3,2},{4,5},{5,4},{6,7},{7,6},{8,9},{9,8},{10,11... | collective-permute-start | bytes 540680 | tf_op jit(solution)/shard_map/ppermute | solution.py:312
  49.5 3.5 %collective-permute-start.10 = (bf16[128,704]{1,0:T(8,128)(2,1)S(1)}, bf16[128,704]{1,0:T(8,128)(2,1)S(1)}, u32[]{:S(2)}, u32[]{:S(2)}) collective-permute-start(bf16[128,704]{1,0:T(8,128)(2,1)S(1)} %collective-permute-done.2.refs_3_), channel_id=1, source_target_pairs={{0,1},{1,0},{2,3},{3,2},{4,5},{5,4},{6,7},{7,6},{8,9},{9,8},{10,11... | collective-permute-start | bytes 540680 | tf_op jit(solution)/shard_map/ppermute | solution.py:312
  49.6 4.4 %collective-permute-start.8 = (bf16[128,704]{1,0:T(8,128)(2,1)S(1)}, bf16[128,704]{1,0:T(8,128)(2,1)S(1)}, u32[]{:S(2)}, u32[]{:S(2)}) collective-permute-start(bf16[128,704]{1,0:T(8,128)(2,1)S(1)} %collective-permute-done.refs_1_), channel_id=1, source_target_pairs={{0,1},{1,0},{2,3},{3,2},{4,5},{5,4},{6,7},{7,6},{8,9},{9,8},{10,11... | collective-permute-start | bytes 540680 | tf_op jit(solution)/shard_map/ppermute | solution.py:312
  50.1 7.5 %collective-permute-start.4 = (bf16[128,704]{1,0:T(8,128)(2,1)S(1)}, bf16[128,704]{1,0:T(8,128)(2,1)S(1)}, u32[]{:S(2)}, u32[]{:S(2)}) collective-permute-start(bf16[128,704]{1,0:T(8,128)(2,1)S(1)} %collective-permute-done.3.refs_4_), channel_id=1, source_target_pairs={{0,2},{2,4},{4,6},{6,0},{1,3},{3,5},{5,7},{7,1},{8,10},{10,12},{12... | collective-permute-start | bytes 540680 | tf_op jit(solution)/shard_map/ppermute | solution.py:240
  50.9 8.1 %collective-permute-start.5 = (bf16[128,704]{1,0:T(8,128)(2,1)S(1)}, bf16[128,704]{1,0:T(8,128)(2,1)S(1)}, u32[]{:S(2)}, u32[]{:S(2)}) collective-permute-start(bf16[128,704]{1,0:T(8,128)(2,1)S(1)} %collective-permute-done.3.refs_4_), channel_id=1, source_target_pairs={{0,6},{2,0},{4,2},{6,4},{1,7},{3,1},{5,3},{7,5},{8,14},{10,8},{12,... | collective-permute-start | bytes 540680 | tf_op jit(solution)/shard_map/ppermute | solution.py:240
  52.7 9.4 %collective-permute-start.6 = (bf16[128,704]{1,0:T(8,128)(2,1)S(1)}, bf16[128,704]{1,0:T(8,128)(2,1)S(1)}, u32[]{:S(2)}, u32[]{:S(2)}) collective-permute-start(bf16[128,704]{1,0:T(8,128)(2,1)S(1)} %collective-permute-done.3.refs_4_), channel_id=1, source_target_pairs={{0,4},{2,6},{4,0},{6,2},{1,5},{3,7},{5,1},{7,3},{8,12},{10,14},{12... | collective-permute-start | bytes 540680 | tf_op jit(solution)/shard_map/ppermute | solution.py:240
  53.0 14.6 %collective-permute-start.9 = (bf16[128,704]{1,0:T(8,128)(2,1)S(1)}, bf16[128,704]{1,0:T(8,128)(2,1)S(1)}, u32[]{:S(2)}, u32[]{:S(2)}) collective-permute-start(bf16[128,704]{1,0:T(8,128)(2,1)S(1)} %collective-permute-done.1.refs_2_), channel_id=1, source_target_pairs={{0,1},{1,0},{2,3},{3,2},{4,5},{5,4},{6,7},{7,6},{8,9},{9,8},{10,11... | collective-permute-start | bytes 540680 | tf_op jit(solution)/shard_map/ppermute | solution.py:312
  54.1 13.6 %collective-permute-start.11 = (bf16[128,704]{1,0:T(8,128)(2,1)S(1)}, bf16[128,704]{1,0:T(8,128)(2,1)}, u32[]{:S(2)}, u32[]{:S(2)}) collective-permute-start(bf16[128,704]{1,0:T(8,128)(2,1)S(1)} %collective-permute-done.3.refs_4_), channel_id=1, source_target_pairs={{0,1},{1,0},{2,3},{3,2},{4,5},{5,4},{6,7},{7,6},{8,9},{9,8},{10,11... | collective-permute-start | bytes 540680 | tf_op jit(solution)/shard_map/ppermute | solution.py:312
  57.5 10.2 %collective-permute-start.12 = (bf16[128,704]{1,0:T(8,128)(2,1)S(1)}, bf16[128,704]{1,0:T(8,128)(2,1)}, u32[]{:S(2)}, u32[]{:S(2)}) collective-permute-start(bf16[128,704]{1,0:T(8,128)(2,1)S(1)} %collective-permute-done.4.refs_5_), channel_id=1, source_target_pairs={{0,1},{1,0},{2,3},{3,2},{4,5},{5,4},{6,7},{7,6},{8,9},{9,8},{10,11... | collective-permute-start | bytes 540680 | tf_op jit(solution)/shard_map/ppermute | solution.py:312
  59.1 8.7 %collective-permute-start.13 = (bf16[128,704]{1,0:T(8,128)(2,1)S(1)}, bf16[128,704]{1,0:T(8,128)(2,1)}, u32[]{:S(2)}, u32[]{:S(2)}) collective-permute-start(bf16[128,704]{1,0:T(8,128)(2,1)S(1)} %collective-permute-done.5.refs_6_), channel_id=1, source_target_pairs={{0,1},{1,0},{2,3},{3,2},{4,5},{5,4},{6,7},{7,6},{8,9},{9,8},{10,11... | collective-permute-start | bytes 540680 | tf_op jit(solution)/shard_map/ppermute | solution.py:312
  62.1 5.6 %collective-permute-start.14 = (bf16[128,704]{1,0:T(8,128)(2,1)S(1)}, bf16[128,704]{1,0:T(8,128)(2,1)}, u32[]{:S(2)}, u32[]{:S(2)}) collective-permute-start(bf16[128,704]{1,0:T(8,128)(2,1)S(1)} %collective-permute-done.6.refs_7_), channel_id=1, source_target_pairs={{0,1},{1,0},{2,3},{3,2},{4,5},{5,4},{6,7},{7,6},{8,9},{9,8},{10,11... | collective-permute-start | bytes 540680 | tf_op jit(solution)/shard_map/ppermute | solution.py:312
  63.0 20.5 %all-to-all-start.2 = ((bf16[16,64,256]{2,1,0:T(8,128)(2,1)}), bf16[16,64,256]{2,1,0:T(8,128)(2,1)S(1)}, u32[]{:S(2)}, u32[]{:S(2)}) async-start(bf16[16,64,256]{2,1,0:T(8,128)(2,1)} %reshape.394), calls=%async_computation.2 | async-start | bytes 1048576 | tf_op jit(solution)/shard_map/all_to_all | solution.py:310
  83.5 20.9 %all-to-all-start.1 = ((f32[8,16,2048]{2,1,0:T(8,128)}), f32[8,16,2048]{2,1,0:T(8,128)S(1)}, u32[]{:S(2)}, u32[]{:S(2)}) async-start(f32[8,16,2048]{2,1,0:T(8,128)} %bitcast.83), calls=%async_computation.1 | async-start | bytes 2097152 | tf_op jit(solution)/shard_map/all_to_all | solution.py:345
  113.1 2.4 %collective-permute-start.16 = (f32[8,128,128]{2,1,0:T(8,128)S(1)}, f32[8,128,128]{2,1,0:T(8,128)S(1)}, u32[]{:S(2)}, u32[]{:S(2)}) collective-permute-start(f32[8,128,128]{2,1,0:T(8,128)S(1)} %dynamic-slice_bitcast_fusion.1), channel_id=1, source_target_pairs={{0,1},{1,0},{2,3},{3,2},{4,5},{5,4},{6,7},{7,6},{8,9},{9,8},{10,11... | collective-permute-start | bytes 1572872 | tf_op jit(solution)/shard_map/ppermute | solution.py:390
  117.4 31.4 %copy-start.4 = (f32[1024,128]{1,0:T(8,128)S(1)}, f32[1024,128]{1,0:T(8,128)}, u32[]{:S(2)}) copy-start(f32[1024,128]{1,0:T(8,128)} %get-tuple-element.37) | copy-start | bytes 1572868
  117.4 13.9 %all-to-all-start.3 = ((f32[8,128,128]{2,1,0:T(8,128)}), f32[8,128,128]{2,1,0:T(8,128)S(1)}, u32[]{:S(2)}, u32[]{:S(2)}) async-start(f32[8,128,128]{2,1,0:T(8,128)} %bitcast_add_fusion), calls=%async_computation.3 | async-start | bytes 1048576 | tf_op jit(solution)/shard_map/all_to_all | solution.py:392
  132.2 16.2 %all-to-all-start.4 = ((f32[16,24,128]{2,1,0:T(8,128)}), f32[16,24,128]{2,1,0:T(8,128)S(1)}, u32[]{:S(2)}, u32[]{:S(2)}) async-start(f32[16,24,128]{2,1,0:T(8,128)} %fusion.5), calls=%async_computation.4 | async-start | bytes 393216 | tf_op jit(solution)/shard_map/all_to_all | solution.py:397
  149.8 18.1 %all-to-all-start.5 = ((f32[16,73,128]{2,1,0:T(8,128)}), f32[16,73,128]{2,1,0:T(8,128)S(1)}, u32[]{:S(2)}, u32[]{:S(2)}) async-start(f32[16,73,128]{2,1,0:T(8,128)} %pad_maximum_fusion), calls=%async_computation.5 | async-start | bytes 1310720 | tf_op jit(solution)/shard_map/all_to_all | solution.py:417
  (21 other events, 296.3 us)
where the time goes:
time: 172 us; the launch traced here: 171 us
  waiting for transfers between devices  60.9 us (35%)
  starting transfers between devices  57.6 us (33%)
  Pallas kernels  28.5 us (17%)
  local copies, waits for them, and re-layouts  13.6 us (8%)
  other arithmetic  7.57 us (4%)
    pallas_call x1, Pallas kernels, body(): pl.pallas_call(attend_kernel, grid_spec=pltpu.PrefetchScalarGridSpec(num_...  15.1 us
    all_to_all x1, waiting for transfers between devices, body(): packed = lax.all_to_all(packed, ROWS, 0, 0, tiled=True)  11.9 us
    all_to_all x1, starting transfers between devices, body(): arrived = lax.all_to_all(send, CTX, 0, 0, tiled=True)  11.9 us
    all_to_all x1, waiting for transfers between devices, body(): target_parts = lax.all_to_all(target_part, ('yl', 'x'), 0, 0, tiled=True)  11.7 us
    ppermute x8, starting transfers between devices, body(): pieces += [lax.ppermute(piece, 'core', swap) for piece in pieces]  11.3 us
    all_to_all x1, waiting for transfers between devices, body(): back = lax.all_to_all(back, CTX, 0, 0, tiled=True)  10.1 us
    all_to_all x1, waiting for transfers between devices, body(): lax.all_to_all(key_sum, ('yl', 'x'), 0, 0, tiled=True)  9.98 us
    ppermute x6, waiting for transfers between devices, shifted(): return lax.ppermute(value, 'x', ring)  8.39 us
  transfers between devices with their start and end apart: 23, of which 9 were waited for; matrix products, arithmetic and copies ran while one was open for 7% of the time, Pallas kernels for 11%

commit v1 on v0

--- a/solution.py
+++ b/solution.py
@@ -128,28 +128,30 @@
     return ((both >= row) & (both < row + heads)).astype(jnp.float32)
 
 
-def index_logits(queries, keys, step, count):
-    block = queries[step * count : (step + 1) * count, :, :TILE]
+def index_logits(block, keys):
     return lax.dot_general(
-        block.reshape(-1, TILE),
+        block[:, :, :TILE].reshape(-1, TILE),
         keys[...],
         (((1,), (1,)), ((), ())),
         preferred_element_type=jnp.float32,
-    ).reshape(count, -1, keys.shape[0])
-
-
-def index_weights(queries, step, count):
-    terms = queries[step * count : (step + 1) * count, :, TILE : 2 * TILE].astype(jnp.float32)
+    ).reshape(*block.shape[:2], keys.shape[0])
+
+
+def index_weights(block):
+    terms = block[:, :, TILE : 2 * TILE].astype(jnp.float32)
     return terms[:, :, 0:1] + terms[:, :, 1:2] + terms[:, :, 2:3]
 
 
+def source_blocks(queries, count):
+    return [queries.at[i : i + count] for i in range(0, queries.shape[0], count)]
+
+
 def score_kernel(queries, keys, score):
-    count = 2
     heads_rows = queries.shape[1]
     total = jnp.zeros((heads_rows, keys.shape[0]), jnp.float32)
-    for step in range(queries.shape[0] // count):
-        lifted = jnp.maximum(index_logits(queries, keys, step, count), 0.0)
-        total = total + jnp.sum(lifted * index_weights(queries, step, count), axis=0)
+    for block in source_blocks(queries, 2):
+        lifted = jnp.maximum(index_logits(block, keys), 0.0)
+        total = total + jnp.sum(lifted * index_weights(block), axis=0)
     score[...] = jnp.dot(
         row_groups(QROWS, heads_rows // QROWS),
         total,
@@ -158,9 +160,15 @@
     )
 
 
-def grad_kernel(
+def index_coefs(block, keys, score_grad):
+    logits = index_logits(block, keys)
+    scaled = jnp.where(logits > 0, score_grad[None] * index_weights(block), 0.0)
+    return logits, scaled.astype(jnp.bfloat16).reshape(-1, logits.shape[-1])
+
+
+def key_grad_kernel(
     facts, target_parts, score, queries, keys, key_pos, loss_grad,
-    query_grad, weight_grad, key_grad, loss, coef
+    score_grad, loss, key_grad, coef
 ):
     allowed = allowed_keys(facts[FIRST], key_pos[...])
     target = jnp.sum(target_parts[...], axis=0)
@@ -174,32 +182,51 @@
     loss[...] = jnp.sum(
         jnp.where(allowed, self_term - target * log_prob, 0.0), axis=-1, keepdims=True
     )
-    score_grad = loss_grad[...] * jnp.where(allowed, weights / row_sum - target, 0.0)
-    count = 2
-    sources, heads_rows = queries.shape[:2]
-    score_grad = lax.dot_general(
+    rows_grad = loss_grad[...] * jnp.where(allowed, weights / row_sum - target, 0.0)
+    heads_rows = queries.shape[1]
+    score_grad[...] = lax.dot_general(
         row_groups(QROWS, heads_rows // QROWS),
-        score_grad,
+        rows_grad,
         (((0,), (0,)), ((), ())),
         precision=lax.Precision.HIGHEST,
         preferred_element_type=jnp.float32,
-    )[None]
+    )
+    count = 2
     rows = count * heads_rows
-    for step in range(sources // count):
-        spot = slice(step * rows, (step + 1) * rows)
-        logits = index_logits(queries, keys, step, count)
-        scaled = score_grad * index_weights(queries, step, count)
-        scaled = jnp.where(logits > 0, scaled, 0.0).reshape(rows, -1)
-        coef[spot, :] = scaled.astype(jnp.bfloat16)
-        lifted = score_grad * jnp.maximum(logits, 0.0)
-        weight_grad[spot, :] = jnp.sum(lifted, axis=-1, keepdims=True).reshape(rows, 1)
-    query_grad[...] = jnp.dot(coef[...], keys[...], preferred_element_type=jnp.float32)
-    flat = queries[:, :, :TILE].reshape(sources * heads_rows, TILE)
+    for step, block in enumerate(source_blocks(queries, count)):
+        coef[step * rows : (step + 1) * rows, :] = index_coefs(block, keys, score_grad[...])[1]
+    flat = queries[:, :, :TILE].reshape(-1, TILE)
     flat = lax.dot_general(
         flat, coef[...], (((0,), (0,)), ((), ())), preferred_element_type=jnp.float32
-    )
-    for lane in range(key_grad.shape[0] * key_grad.shape[1]):
-        key_grad[lane % 2, lane // 2] = flat[:, lane * TILE : (lane + 1) * TILE]
+    ).astype(jnp.bfloat16)
+    for lane in range(key_grad.shape[0]):
+        key_grad[lane] = flat[:, lane * TILE : (lane + 1) * TILE]
+
+
+def as_row(column):
+    n = column.shape[0]
+    here = lax.broadcasted_iota(jnp.int32, (n, n), 0) == lax.broadcasted_iota(
+        jnp.int32, (n, n), 1
+    )
+    return jnp.sum(jnp.where(here, column, 0.0), axis=0, keepdims=True)
+
+
+def query_grad_kernel(score_grad, loss, queries, keys, packed):
+    count = 2
+    heads_rows = queries.shape[1]
+    losses = as_row(loss[...])
+    blank = jnp.zeros((1, packed.shape[2] - heads_rows - QROWS), jnp.float32)
+    rest = jnp.zeros((packed.shape[1] - heads_rows - STRIPE - 1, packed.shape[2]), jnp.float32)
+    for step, block in enumerate(source_blocks(queries, count)):
+        logits, coef = index_coefs(block, keys, score_grad[...])
+        query = jnp.dot(coef, keys[...], preferred_element_type=jnp.float32)
+        query = query.reshape(count, heads_rows, TILE)
+        lifted = jnp.sum(score_grad[...][None] * jnp.maximum(logits, 0.0), axis=-1, keepdims=True)
+        for i in range(count):
+            place = step * count + i
+            packed[place, :heads_rows] = query[i]
+            last = jnp.concatenate([as_row(lifted[i]), losses, blank], axis=1)
+            packed[place, heads_rows + STRIPE :] = jnp.concatenate([last, rest], axis=0)
 
 
 def whole(shape):
@@ -246,6 +273,9 @@
         compiler_params=params,
         name="stripes",
     )(jnp.stack([ctx_index, lane]).astype(jnp.int32), selection, index_key, key_latent.T)
+    send, index_query, index_weight, main_query = lax.optimization_barrier(
+        (send, index_query, index_weight, main_query)
+    )
     arrived = lax.all_to_all(send, CTX, 0, 0, tiled=True)
 
     queries = jnp.transpose(main_query, (1, 2, 0))
@@ -358,39 +388,49 @@
         name="score",
     )(iq, index_keys)
 
-    query_grad, weight_grad, key_part, loss = pl.pallas_call(
-        grad_kernel,
+    score_grad, loss, key_part = pl.pallas_call(
+        key_grad_kernel,
         grid=(1,),
         in_specs=[smem]
         + [whole((lanes // 2, QROWS, key_span)), whole((QROWS, key_span))]
-        + [whole(iq.shape), whole((key_span, idx_width)), whole((1, key_span)), whole((QROWS, 1))],
+        + [whole(iq.shape), whole((key_span, idx_width))]
+        + [whole((1, key_span)), whole((QROWS, 1))],
         out_specs=[
-            whole((rows_all, idx_width)),
-            whole((rows_all, 1)),
-            whole((2, lanes // 2, idx_width, TILE)),
+            whole((heads_rows, key_span)),
             whole((QROWS, 1)),
+            whole((lanes, idx_width, TILE)),
         ],
         out_shape=[
-            jax.ShapeDtypeStruct((rows_all, idx_width), f32),
-            jax.ShapeDtypeStruct((rows_all, 1), f32),
-            jax.ShapeDtypeStruct((2, lanes // 2, idx_width, TILE), f32),
+            jax.ShapeDtypeStruct((heads_rows, key_span), f32),
             jax.ShapeDtypeStruct((QROWS, 1), f32),
+            jax.ShapeDtypeStruct((lanes, idx_width, TILE), bf16),
         ],
         scratch_shapes=[pltpu.VMEM((rows_all, key_span), bf16)],
         compiler_params=params,
         cost_estimate=pl.CostEstimate(
-            flops=6 * rows_all * key_span * idx_width, bytes_accessed=4 * 2**20, transcendentals=0
-        ),
-        name="grad",
+            flops=4 * rows_all * key_span * idx_width, bytes_accessed=4 * 2**20, transcendentals=0
+        ),
+        name="key_grad",
     )(facts, target_parts, score, iq, index_keys, key_pos, grad_rows)
 
+    packed_shape = (lanes, heads_rows + 2 * STRIPE, idx_width)
+    packed = pl.pallas_call(
+        query_grad_kernel,
+        grid=(1,),
+        in_specs=[whole((heads_rows, key_span)), whole((QROWS, 1))]
+        + [whole(iq.shape), whole((key_span, idx_width))],
+        out_specs=whole(packed_shape),
+        out_shape=jax.ShapeDtypeStruct(packed_shape, f32),
+        compiler_params=params,
+        cost_estimate=pl.CostEstimate(
+            flops=4 * rows_all * key_span * idx_width, bytes_accessed=4 * 2**20, transcendentals=0
+        ),
+        name="query_grad",
+    )(score_grad, loss, iq, index_keys)
+
     exact = lax.Precision.HIGHEST
-    key_keep = lax.dynamic_index_in_dim(key_part, core, 0, keepdims=False)
-    key_give = lax.dynamic_index_in_dim(key_part, 1 - core, 0, keepdims=False)
-    key_sum = key_keep + lax.ppermute(key_give, "core", swap)
-    key_sum = jnp.sum(
-        lax.all_to_all(key_sum, ("yl", "x"), 0, 0, tiled=True), axis=0
-    )
+    key_sum = lax.all_to_all(key_part, HEAD, 0, 0, tiled=True)
+    key_sum = jnp.sum(key_sum.astype(f32), axis=0)
     back = lax.dot_general(
         got_rows.astype(f32), key_sum, (((0,), (1,)), ((), ())), precision=exact
     )
@@ -403,17 +443,7 @@
     goes = (jnp.arange(key_tiles)[None, :] * lanes + lane) // key_tiles == natural[:, None]
     key_send = jnp.sum(jnp.where(goes[:, :, None, None], own_blocks[None], 0.0), axis=1)
 
-    small = jnp.concatenate(
-        [
-            weight_grad.reshape(lanes, heads_rows),
-            jnp.broadcast_to(loss.reshape(1, QROWS), (lanes, QROWS)),
-            jnp.zeros((lanes, idx_width - heads_rows - QROWS), f32),
-        ],
-        axis=1,
-    ).reshape(lanes, 1, idx_width)
-    packed = jnp.concatenate(
-        [query_grad.reshape(lanes, heads_rows, idx_width), key_send, small], axis=1
-    )
+    packed = lax.dynamic_update_slice(packed, key_send, (0, heads_rows, 0))
     packed = lax.all_to_all(packed, ROWS, 0, 0, tiled=True)
     query_out = packed[:, :heads_rows].reshape(query_rows, index_local, idx_width)
     blocks = packed[:, heads_rows : heads_rows + STRIPE]

time: 172 us -> 165 us (0.959)
  waiting for transfers between devices: 60.9 us -> 54.6 us
  Pallas kernels: 28.5 us -> 31.9 us
  other arithmetic: 7.57 us -> 4.4 us
    all_to_all x1, waiting for transfers between devices: 10.1 us -> 5.53 us  [body(): back = lax.all_to_all(back, CTX, 0, 0, tiled=True)]
    pallas_call x1 -> x2, Pallas kernels: 6.54 us -> 10 us  [the longest x1 5.06 us: body(): pl.pallas_call(key_grad_kernel, grid=(1,), in_specs=[smem] + [whole((lane...]
    add x1 -> x0, other arithmetic: 1.93 us -> none  [body(): key_sum = key_keep + lax.ppermute(key_give, 'core', swap)]
  transfers between devices with their start and end apart: 23 -> 22, of which waited for: 9 -> 8; matrix products, arithmetic and copies ran while one was open for 7% -> 7% of each run, Pallas kernels for 11% -> 14%
where the time goes in v1:
time: 165 us; the launch traced here: 164 us
  starting transfers between devices  57.4 us (35%)
  waiting for transfers between devices  54.6 us (33%)
  Pallas kernels  31.9 us (19%)
  local copies, waits for them, and re-layouts  13.3 us (8%)
  other arithmetic  4.4 us (3%)
    pallas_call x1, Pallas kernels, body(): pl.pallas_call(attend_kernel, grid_spec=pltpu.PrefetchScalarGridSpec(num_...  15.1 us
    all_to_all x1, waiting for transfers between devices, body(): packed = lax.all_to_all(packed, ROWS, 0, 0, tiled=True)  11.9 us
    all_to_all x1, starting transfers between devices, body(): arrived = lax.all_to_all(send, CTX, 0, 0, tiled=True)  11.9 us
    all_to_all x1, waiting for transfers between devices, body(): target_parts = lax.all_to_all(target_part, ('yl', 'x'), 0, 0, tiled=True)  11.7 us
    ppermute x8, starting transfers between devices, body(): pieces += [lax.ppermute(piece, 'core', swap) for piece in pieces]  11.1 us
    all_to_all x1, waiting for transfers between devices, body(): key_sum = lax.all_to_all(key_part, HEAD, 0, 0, tiled=True)  9.84 us
    ppermute x6, waiting for transfers between devices, shifted(): return lax.ppermute(value, 'x', ring)  8.52 us
    ppermute x6, starting transfers between devices, shifted(): return lax.ppermute(value, 'x', ring)  7.27 us
  transfers between devices with their start and end apart: 22, of which 8 were waited for; matrix products, arithmetic and copies ran while one was open for 7% of the time, Pallas kernels for 14%

profile of v1, /device:TPU:1, one launch (start us, length us, event | category | flops | bytes accessed | tf_op | source)
XLA Modules:
  0.0 164.2 jit_solution(6329929878465851708)
XLA Ops:
  1.2 3.3 %stripes.1 = bf16[384,704]{1,0:T(8,128)(2,1)} custom-call(s32[2]{0:T(128)} %pad_add_fusion.where, s32[16,16]{1,0:T(8,128)} %selection.1, bf16[768,128]{1,0:T(8,128)(2,1)} %index_key.1, bf16[576,768]{1,0:T(8,128)(2,1)} %bitcast.76), custom_call_target="tpu_custom_call" | custom-call | tf_op jit(solution)/shard_map/stripes/pallas_call | solution.py:269
  4.6 11.9 %all-to-all-start = ((bf16[16,24,704]{2,1,0:T(8,128)(2,1)}), bf16[16,24,704]{2,1,0:T(8,128)(2,1)S(1)}, u32[]{:S(2)}, u32[]{:S(2)}) async-start(bf16[16,24,704]{2,1,0:T(8,128)(2,1)} %bitcast.74), calls=%async_computation | async-start | bytes 1179648 | tf_op jit(solution)/shard_map/all_to_all | solution.py:279
  22.2 1.8 %mul.166 = bf16[128,384]{1,0:T(8,128)(2,1)S(1)} reshape(bf16[16,8,48,8]{3,2,1,0:T(8,128)(2,1)S(1)} %broadcast_multiply_fusion) | data formatting | bytes 196608 | tf_op jit(solution)/shard_map/mul | solution.py:239
  27.8 7.1 %all-to-all-done = bf16[16,24,704]{2,1,0:T(8,128)(2,1)S(1)} async-done(((bf16[16,24,704]{2,1,0:T(8,128)(2,1)}), bf16[16,24,704]{2,1,0:T(8,128)(2,1)S(1)}, u32[]{:S(2)}, u32[]{:S(2)}) %all-to-all-start) | async-done | bytes 540704 | tf_op jit(solution)/shard_map/all_to_all | solution.py:279
  38.1 1.5 collective-permute-start.2
  41.2 4.0 %collective-permute-done.2.refs_3_ = bf16[128,704]{1,0:T(8,128)(2,1)S(1)} collective-permute-done((bf16[128,704]{1,0:T(8,128)(2,1)S(1)}, bf16[128,704]{1,0:T(8,128)(2,1)S(1)}, u32[]{:S(2)}, u32[]{:S(2)}) %collective-permute-start.2) | collective-permute-done | bytes 180256 | tf_op jit(solution)/shard_map/ppermute | solution.py:267
  45.3 4.1 %collective-permute-start.7 = (bf16[128,704]{1,0:T(8,128)(2,1)S(1)}, bf16[128,704]{1,0:T(8,128)(2,1)S(1)}, u32[]{:S(2)}, u32[]{:S(2)}) collective-permute-start(bf16[128,704]{1,0:T(8,128)(2,1)S(1)} %copy.57.refs_0_), channel_id=1, source_target_pairs={{0,1},{1,0},{2,3},{3,2},{4,5},{5,4},{6,7},{7,6},{8,9},{9,8},{10,11... | collective-permute-start | bytes 540680 | tf_op jit(solution)/shard_map/ppermute | solution.py:342
  50.8 1.8 %collective-permute-start.5 = (bf16[128,704]{1,0:T(8,128)(2,1)S(1)}, bf16[128,704]{1,0:T(8,128)(2,1)S(1)}, u32[]{:S(2)}, u32[]{:S(2)}) collective-permute-start(bf16[128,704]{1,0:T(8,128)(2,1)S(1)} %collective-permute-done.3.refs_4_), channel_id=1, source_target_pairs={{0,6},{2,0},{4,2},{6,4},{1,7},{3,1},{5,3},{7,5},{8,14},{10,8},{12,... | collective-permute-start | bytes 540680 | tf_op jit(solution)/shard_map/ppermute | solution.py:267
  54.1 3.4 %collective-permute-done.4.refs_5_ = bf16[128,704]{1,0:T(8,128)(2,1)} collective-permute-done((bf16[128,704]{1,0:T(8,128)(2,1)S(1)}, bf16[128,704]{1,0:T(8,128)(2,1)}, u32[]{:S(2)}, u32[]{:S(2)}) %collective-permute-start.4) | collective-permute-done | bytes 180256 | tf_op jit(solution)/shard_map/ppermute | solution.py:267
  57.5 1.5 collective-permute-start.12
  59.1 2.9 %collective-permute-start.13 = (bf16[128,704]{1,0:T(8,128)(2,1)S(1)}, bf16[128,704]{1,0:T(8,128)(2,1)}, u32[]{:S(2)}, u32[]{:S(2)}) collective-permute-start(bf16[128,704]{1,0:T(8,128)(2,1)S(1)} %collective-permute-done.5.refs_6_), channel_id=1, source_target_pairs={{0,1},{1,0},{2,3},{3,2},{4,5},{5,4},{6,7},{7,6},{8,9},{9,8},{10,11... | collective-permute-start | bytes 540680 | tf_op jit(solution)/shard_map/ppermute | solution.py:342
  62.9 4.7 %all-to-all-start.2 = ((bf16[16,64,256]{2,1,0:T(8,128)(2,1)}), bf16[16,64,256]{2,1,0:T(8,128)(2,1)S(1)}, u32[]{:S(2)}, u32[]{:S(2)}) async-start(bf16[16,64,256]{2,1,0:T(8,128)(2,1)} %reshape.383), calls=%async_computation.2 | async-start | bytes 1048576 | tf_op jit(solution)/shard_map/all_to_all | solution.py:340
  68.4 15.1 %attend.1 = (f32[128,2048]{1,0:T(8,128)}, bf16[2048,128]{1,0:T(8,128)(2,1)}) custom-call(s32[20]{0:T(128)} %concatenate.6.facts, bf16[128,704]{1,0:T(8,128)(2,1)} %copy-done.4, bf16[128,704]{1,0:T(8,128)(2,1)} %copy-done.7, bf16[128,704]{1,0:T(8,128)(2,1)} %copy-done.8, bf16[128,704]{1,0:T(8,128)(2,1)} %copy-done.9, bf16[128,704]{1,0:T(8,128)(2,1)} %copy-done.10, ...), custom_call_target="tpu_custom_call" | custom-call | flops 4831838208 | bytes 8388608 | tf_op jit(solution)/shard_map/attend/pallas_call | solution.py:345
  83.6 5.1 %all-to-all-start.1 = ((f32[8,16,2048]{2,1,0:T(8,128)}), f32[8,16,2048]{2,1,0:T(8,128)S(1)}, u32[]{:S(2)}, u32[]{:S(2)}) async-start(f32[8,16,2048]{2,1,0:T(8,128)} %bitcast.75), calls=%async_computation.1 | async-start | bytes 2097152 | tf_op jit(solution)/shard_map/all_to_all | solution.py:375
  89.3 3.5 %score.1 = f32[16,2048]{1,0:T(8,128)} custom-call(bf16[16,64,256]{2,1,0:T(8,128)(2,1)} %copy-done.2, bf16[2048,128]{1,0:T(8,128)(2,1)} %get-tuple-element.41.keys), custom_call_target="tpu_custom_call" | custom-call | flops 536870912 | bytes 1048576 | tf_op jit(solution)/shard_map/score/pallas_call | solution.py:378
  92.8 11.7 %all-to-all-done.1.target_parts = f32[8,16,2048]{2,1,0:T(8,128)S(1)} async-done(((f32[8,16,2048]{2,1,0:T(8,128)}), f32[8,16,2048]{2,1,0:T(8,128)S(1)}, u32[]{:S(2)}, u32[]{:S(2)}) %all-to-all-start.1) | async-done | bytes 1048608 | tf_op jit(solution)/shard_map/all_to_all | solution.py:375
  105.5 5.1 %key_grad.1 = (f32[64,2048]{1,0:T(8,128)}, f32[16,1]{1,0:T(8,128)}, bf16[16,128,128]{2,1,0:T(8,128)(2,1)}) custom-call(s32[20]{0:T(128)} %concatenate.6.facts, f32[8,16,2048]{2,1,0:T(8,128)} %copy-done.1, f32[16,2048]{1,0:T(8,128)} %score.1, bf16[16,64,256]{2,1,0:T(8,128)(2,1)} %copy-done.2, bf16[2048,128]{1,0:T(8,128)(2,1)} %get-tuple-element.41.keys, ...), custom_call_target="tpu_custom_call" | custom-call | flops 1073741824 | bytes 4194304 | tf_op jit(solution)/shard_map/key_grad/pallas_call | solution.py:391
  110.6 4.2 %all-to-all-start.3 = ((bf16[16,128,128]{2,1,0:T(8,128)(2,1)}), bf16[16,128,128]{2,1,0:T(8,128)(2,1)S(1)}, u32[]{:S(2)}, u32[]{:S(2)}) async-start(bf16[16,128,128]{2,1,0:T(8,128)(2,1)} %get-tuple-element.47), calls=%async_computation.3 | async-start | bytes 1048576 | tf_op jit(solution)/shard_map/all_to_all | solution.py:432
  114.9 9.8 %all-to-all-done.3 = bf16[16,128,128]{2,1,0:T(8,128)(2,1)S(1)} async-done(((bf16[16,128,128]{2,1,0:T(8,128)(2,1)}), bf16[16,128,128]{2,1,0:T(8,128)(2,1)S(1)}, u32[]{:S(2)}, u32[]{:S(2)}) %all-to-all-start.3) | async-done | bytes 524320 | tf_op jit(solution)/shard_map/all_to_all | solution.py:432
  125.7 5.5 %all-to-all-start.4 = ((f32[16,24,128]{2,1,0:T(8,128)}), f32[16,24,128]{2,1,0:T(8,128)S(1)}, u32[]{:S(2)}, u32[]{:S(2)}) async-start(f32[16,24,128]{2,1,0:T(8,128)} %fusion.5), calls=%async_computation.4 | async-start | bytes 393216 | tf_op jit(solution)/shard_map/all_to_all | solution.py:437
  131.4 4.9 %query_grad.1 = f32[16,80,128]{2,1,0:T(8,128)} custom-call(f32[64,2048]{1,0:T(8,128)} %get-tuple-element.44.score_grad, f32[16,1]{1,0:T(8,128)} %get-tuple-element.45.loss, bf16[16,64,256]{2,1,0:T(8,128)(2,1)} %copy-done.2, bf16[2048,128]{1,0:T(8,128)(2,1)} %get-tuple-element.41.keys), custom_call_target="tpu_custom_call" | custom-call | flops 1073741824 | bytes 4194304 | tf_op jit(solution)/shard_map/query_grad/pallas_call | solution.py:417
  136.3 5.5 %all-to-all-done.4 = f32[16,24,128]{2,1,0:T(8,128)S(1)} async-done(((f32[16,24,128]{2,1,0:T(8,128)}), f32[16,24,128]{2,1,0:T(8,128)S(1)}, u32[]{:S(2)}, u32[]{:S(2)}) %all-to-all-start.4) | async-done | bytes 196640 | tf_op jit(solution)/shard_map/all_to_all | solution.py:437
  142.9 6.2 %all-to-all-start.5 = ((f32[16,80,128]{2,1,0:T(8,128)}), f32[16,80,128]{2,1,0:T(8,128)S(1)}, u32[]{:S(2)}, u32[]{:S(2)}) async-start(f32[16,80,128]{2,1,0:T(8,128)} %constant_dynamic-update-slice_fusion), calls=%async_computation.5 | async-start | bytes 1310720 | tf_op jit(solution)/shard_map/all_to_all | solution.py:447
  149.2 11.9 %all-to-all-done.5 = f32[16,80,128]{2,1,0:T(8,128)S(1)} async-done(((f32[16,80,128]{2,1,0:T(8,128)}), f32[16,80,128]{2,1,0:T(8,128)S(1)}, u32[]{:S(2)}, u32[]{:S(2)}) %all-to-all-start.5) | async-done | bytes 655392 | tf_op jit(solution)/shard_map/all_to_all | solution.py:447
  (125 shorter events, 26.5 us)
Async XLA Ops:
  0.6 27.1 %copy-start = (f32[256]{0:T(256)S(1)}, f32[256]{0:T(256)}, u32[]{:S(2)}) copy-start(f32[256]{0:T(256)} %param.13) | copy-start | bytes 3076
  4.6 30.3 %all-to-all-start = ((bf16[16,24,704]{2,1,0:T(8,128)(2,1)}), bf16[16,24,704]{2,1,0:T(8,128)(2,1)S(1)}, u32[]{:S(2)}, u32[]{:S(2)}) async-start(bf16[16,24,704]{2,1,0:T(8,128)(2,1)} %bitcast.74), calls=%async_computation | async-start | bytes 1179648 | tf_op jit(solution)/shard_map/all_to_all | solution.py:279
  17.9 32.9 %collective-permute-start.15 = (bf16[8,576,128]{2,1,0:T(8,128)(2,1)S(1)}, bf16[8,576,128]{2,1,0:T(8,128)(2,1)}, u32[]{:S(2)}, u32[]{:S(2)}) collective-permute-start(bf16[8,576,128]{2,1,0:T(8,128)(2,1)S(1)} %dynamic-slice_bitcast_fusion), channel_id=1, source_target_pairs={{0,1},{1,0},{2,3},{3,2},{4,5},{5,4},{6,7},{7,6},{8,9},{9,8},{10,11... | collective-permute-start | bytes 3538952 | tf_op jit(solution)/shard_map/ppermute | solution.py:283
  35.4 5.8 %collective-permute-start = (bf16[128,704]{1,0:T(8,128)(2,1)S(1)}, bf16[128,704]{1,0:T(8,128)(2,1)S(1)}, u32[]{:S(2)}, u32[]{:S(2)}) collective-permute-start(bf16[128,704]{1,0:T(8,128)(2,1)S(1)} %copy.52), channel_id=1, source_target_pairs={{0,2},{2,4},{4,6},{6,0},{1,3},{3,5},{5,7},{7,1},{8,10},{10,12},{12... | collective-permute-start | bytes 540680 | tf_op jit(solution)/shard_map/ppermute | solution.py:267
  36.7 4.5 %collective-permute-start.1 = (bf16[128,704]{1,0:T(8,128)(2,1)S(1)}, bf16[128,704]{1,0:T(8,128)(2,1)S(1)}, u32[]{:S(2)}, u32[]{:S(2)}) collective-permute-start(bf16[128,704]{1,0:T(8,128)(2,1)S(1)} %copy.52), channel_id=1, source_target_pairs={{0,6},{2,0},{4,2},{6,4},{1,7},{3,1},{5,3},{7,5},{8,14},{10,8},{12,... | collective-permute-start | bytes 540680 | tf_op jit(solution)/shard_map/ppermute | solution.py:267
  38.1 7.0 %collective-permute-start.2 = (bf16[128,704]{1,0:T(8,128)(2,1)S(1)}, bf16[128,704]{1,0:T(8,128)(2,1)S(1)}, u32[]{:S(2)}, u32[]{:S(2)}) collective-permute-start(bf16[128,704]{1,0:T(8,128)(2,1)S(1)} %copy.52), channel_id=1, source_target_pairs={{0,4},{2,6},{4,0},{6,2},{1,5},{3,7},{5,1},{7,3},{8,12},{10,14},{12... | collective-permute-start | bytes 540680 | tf_op jit(solution)/shard_map/ppermute | solution.py:267
  39.7 10.3 %collective-permute-start.3 = (bf16[128,704]{1,0:T(8,128)(2,1)S(1)}, bf16[128,704]{1,0:T(8,128)(2,1)S(1)}, u32[]{:S(2)}, u32[]{:S(2)}) collective-permute-start(bf16[128,704]{1,0:T(8,128)(2,1)S(1)} %copy.52), channel_id=1, source_target_pairs={{0,8},{8,0},{1,9},{9,1},{2,10},{10,2},{3,11},{11,3},{4,12},{12,4},... | collective-permute-start | bytes 540680 | tf_op jit(solution)/shard_map/ppermute | solution.py:337
  41.2 26.5 %copy-start.8 = (bf16[128,704]{1,0:T(8,128)(2,1)}, bf16[128,704]{1,0:T(8,128)(2,1)S(1)}, u32[]{:S(2)}) copy-start(bf16[128,704]{1,0:T(8,128)(2,1)S(1)} %collective-permute-done.1.refs_2_) | copy-start | bytes 540676
  45.3 7.3 %collective-permute-start.7 = (bf16[128,704]{1,0:T(8,128)(2,1)S(1)}, bf16[128,704]{1,0:T(8,128)(2,1)S(1)}, u32[]{:S(2)}, u32[]{:S(2)}) collective-permute-start(bf16[128,704]{1,0:T(8,128)(2,1)S(1)} %copy.57.refs_0_), channel_id=1, source_target_pairs={{0,1},{1,0},{2,3},{3,2},{4,5},{5,4},{6,7},{7,6},{8,9},{9,8},{10,11... | collective-permute-start | bytes 540680 | tf_op jit(solution)/shard_map/ppermute | solution.py:342
  49.4 3.5 %collective-permute-start.10 = (bf16[128,704]{1,0:T(8,128)(2,1)S(1)}, bf16[128,704]{1,0:T(8,128)(2,1)S(1)}, u32[]{:S(2)}, u32[]{:S(2)}) collective-permute-start(bf16[128,704]{1,0:T(8,128)(2,1)S(1)} %collective-permute-done.2.refs_3_), channel_id=1, source_target_pairs={{0,1},{1,0},{2,3},{3,2},{4,5},{5,4},{6,7},{7,6},{8,9},{9,8},{10,11... | collective-permute-start | bytes 540680 | tf_op jit(solution)/shard_map/ppermute | solution.py:342
  49.5 4.4 %collective-permute-start.8 = (bf16[128,704]{1,0:T(8,128)(2,1)S(1)}, bf16[128,704]{1,0:T(8,128)(2,1)S(1)}, u32[]{:S(2)}, u32[]{:S(2)}) collective-permute-start(bf16[128,704]{1,0:T(8,128)(2,1)S(1)} %collective-permute-done.refs_1_), channel_id=1, source_target_pairs={{0,1},{1,0},{2,3},{3,2},{4,5},{5,4},{6,7},{7,6},{8,9},{9,8},{10,11... | collective-permute-start | bytes 540680 | tf_op jit(solution)/shard_map/ppermute | solution.py:342
  50.0 7.6 %collective-permute-start.4 = (bf16[128,704]{1,0:T(8,128)(2,1)S(1)}, bf16[128,704]{1,0:T(8,128)(2,1)}, u32[]{:S(2)}, u32[]{:S(2)}) collective-permute-start(bf16[128,704]{1,0:T(8,128)(2,1)S(1)} %collective-permute-done.3.refs_4_), channel_id=1, source_target_pairs={{0,2},{2,4},{4,6},{6,0},{1,3},{3,5},{5,7},{7,1},{8,10},{10,12},{12... | collective-permute-start | bytes 540680 | tf_op jit(solution)/shard_map/ppermute | solution.py:267
  50.8 8.2 %collective-permute-start.5 = (bf16[128,704]{1,0:T(8,128)(2,1)S(1)}, bf16[128,704]{1,0:T(8,128)(2,1)S(1)}, u32[]{:S(2)}, u32[]{:S(2)}) collective-permute-start(bf16[128,704]{1,0:T(8,128)(2,1)S(1)} %collective-permute-done.3.refs_4_), channel_id=1, source_target_pairs={{0,6},{2,0},{4,2},{6,4},{1,7},{3,1},{5,3},{7,5},{8,14},{10,8},{12,... | collective-permute-start | bytes 540680 | tf_op jit(solution)/shard_map/ppermute | solution.py:267
  52.6 9.4 %collective-permute-start.6 = (bf16[128,704]{1,0:T(8,128)(2,1)S(1)}, bf16[128,704]{1,0:T(8,128)(2,1)S(1)}, u32[]{:S(2)}, u32[]{:S(2)}) collective-permute-start(bf16[128,704]{1,0:T(8,128)(2,1)S(1)} %collective-permute-done.3.refs_4_), channel_id=1, source_target_pairs={{0,4},{2,6},{4,0},{6,2},{1,5},{3,7},{5,1},{7,3},{8,12},{10,14},{12... | collective-permute-start | bytes 540680 | tf_op jit(solution)/shard_map/ppermute | solution.py:267
  53.0 14.6 %collective-permute-start.9 = (bf16[128,704]{1,0:T(8,128)(2,1)S(1)}, bf16[128,704]{1,0:T(8,128)(2,1)S(1)}, u32[]{:S(2)}, u32[]{:S(2)}) collective-permute-start(bf16[128,704]{1,0:T(8,128)(2,1)S(1)} %collective-permute-done.1.refs_2_), channel_id=1, source_target_pairs={{0,1},{1,0},{2,3},{3,2},{4,5},{5,4},{6,7},{7,6},{8,9},{9,8},{10,11... | collective-permute-start | bytes 540680 | tf_op jit(solution)/shard_map/ppermute | solution.py:342
  54.0 13.6 %collective-permute-start.11 = (bf16[128,704]{1,0:T(8,128)(2,1)S(1)}, bf16[128,704]{1,0:T(8,128)(2,1)S(1)}, u32[]{:S(2)}, u32[]{:S(2)}) collective-permute-start(bf16[128,704]{1,0:T(8,128)(2,1)S(1)} %collective-permute-done.3.refs_4_), channel_id=1, source_target_pairs={{0,1},{1,0},{2,3},{3,2},{4,5},{5,4},{6,7},{7,6},{8,9},{9,8},{10,11... | collective-permute-start | bytes 540680 | tf_op jit(solution)/shard_map/ppermute | solution.py:342
  57.5 10.1 %collective-permute-start.12 = (bf16[128,704]{1,0:T(8,128)(2,1)}, bf16[128,704]{1,0:T(8,128)(2,1)S(1)}, u32[]{:S(2)}, u32[]{:S(2)}) collective-permute-start(bf16[128,704]{1,0:T(8,128)(2,1)} %collective-permute-done.4.refs_5_), channel_id=1, source_target_pairs={{0,1},{1,0},{2,3},{3,2},{4,5},{5,4},{6,7},{7,6},{8,9},{9,8},{10,11... | collective-permute-start | bytes 540680 | tf_op jit(solution)/shard_map/ppermute | solution.py:342
  59.1 8.6 %collective-permute-start.13 = (bf16[128,704]{1,0:T(8,128)(2,1)S(1)}, bf16[128,704]{1,0:T(8,128)(2,1)}, u32[]{:S(2)}, u32[]{:S(2)}) collective-permute-start(bf16[128,704]{1,0:T(8,128)(2,1)S(1)} %collective-permute-done.5.refs_6_), channel_id=1, source_target_pairs={{0,1},{1,0},{2,3},{3,2},{4,5},{5,4},{6,7},{7,6},{8,9},{9,8},{10,11... | collective-permute-start | bytes 540680 | tf_op jit(solution)/shard_map/ppermute | solution.py:342
  62.0 5.6 %collective-permute-start.14 = (bf16[128,704]{1,0:T(8,128)(2,1)S(1)}, bf16[128,704]{1,0:T(8,128)(2,1)}, u32[]{:S(2)}, u32[]{:S(2)}) collective-permute-start(bf16[128,704]{1,0:T(8,128)(2,1)S(1)} %collective-permute-done.6.refs_7_), channel_id=1, source_target_pairs={{0,1},{1,0},{2,3},{3,2},{4,5},{5,4},{6,7},{7,6},{8,9},{9,8},{10,11... | collective-permute-start | bytes 540680 | tf_op jit(solution)/shard_map/ppermute | solution.py:342
  62.9 20.7 %all-to-all-start.2 = ((bf16[16,64,256]{2,1,0:T(8,128)(2,1)}), bf16[16,64,256]{2,1,0:T(8,128)(2,1)S(1)}, u32[]{:S(2)}, u32[]{:S(2)}) async-start(bf16[16,64,256]{2,1,0:T(8,128)(2,1)} %reshape.383), calls=%async_computation.2 | async-start | bytes 1048576 | tf_op jit(solution)/shard_map/all_to_all | solution.py:340
  83.6 20.9 %all-to-all-start.1 = ((f32[8,16,2048]{2,1,0:T(8,128)}), f32[8,16,2048]{2,1,0:T(8,128)S(1)}, u32[]{:S(2)}, u32[]{:S(2)}) async-start(f32[8,16,2048]{2,1,0:T(8,128)} %bitcast.75), calls=%async_computation.1 | async-start | bytes 2097152 | tf_op jit(solution)/shard_map/all_to_all | solution.py:375
  110.6 14.1 %all-to-all-start.3 = ((bf16[16,128,128]{2,1,0:T(8,128)(2,1)}), bf16[16,128,128]{2,1,0:T(8,128)(2,1)S(1)}, u32[]{:S(2)}, u32[]{:S(2)}) async-start(bf16[16,128,128]{2,1,0:T(8,128)(2,1)} %get-tuple-element.47), calls=%async_computation.3 | async-start | bytes 1048576 | tf_op jit(solution)/shard_map/all_to_all | solution.py:432
  125.7 16.1 %all-to-all-start.4 = ((f32[16,24,128]{2,1,0:T(8,128)}), f32[16,24,128]{2,1,0:T(8,128)S(1)}, u32[]{:S(2)}, u32[]{:S(2)}) async-start(f32[16,24,128]{2,1,0:T(8,128)} %fusion.5), calls=%async_computation.4 | async-start | bytes 393216 | tf_op jit(solution)/shard_map/all_to_all | solution.py:437
  142.9 18.2 %all-to-all-start.5 = ((f32[16,80,128]{2,1,0:T(8,128)}), f32[16,80,128]{2,1,0:T(8,128)S(1)}, u32[]{:S(2)}, u32[]{:S(2)}) async-start(f32[16,80,128]{2,1,0:T(8,128)} %constant_dynamic-update-slice_fusion), calls=%async_computation.5 | async-start | bytes 1310720 | tf_op jit(solution)/shard_map/all_to_all | solution.py:447
  (17 other events, 175.7 us)

commit v2 on v1

--- a/solution.py
+++ b/solution.py
@@ -13,7 +13,7 @@
 OWNER_MOST = 3
 QROWS = 16
 STRIPE = 8
-VMEM = 60 * 1024 * 1024
+VMEM = 32 * 1024 * 1024
 
 SLOTS, CORE, FIRST = 16, 18, 19
 
@@ -78,11 +78,13 @@
         lax.broadcasted_iota(jnp.int32, shape, 1) & (TILE - 1)
     )
     behind = behind - facts[CORE] * TILE
-    pairs = [(part, head) for part in (q_own, q_other) for head in range(0, part.shape[0], 2)]
+    half = pl.ds(pl.multiple_of(facts[CORE] * TILE, TILE), TILE)
+    heads = [q_own.at[head, :, half] for head in range(q_own.shape[0])]
+    heads += [q_other.at[head] for head in range(q_other.shape[0])]
+    pairs = list(zip(heads[::2], heads[1::2]))
 
     def scores(step):
-        part, head = pairs[step]
-        both = jnp.concatenate([part[head], part[head + 1]], axis=1)
+        both = jnp.concatenate([head[...] for head in pairs[step]], axis=1)
         out = raw[step % 2]
         out[...] = jnp.dot(keys[...], both, preferred_element_type=jnp.float32)
         for tile in range(2):
@@ -227,10 +229,6 @@
             packed[place, :heads_rows] = query[i]
             last = jnp.concatenate([as_row(lifted[i]), losses, blank], axis=1)
             packed[place, heads_rows + STRIPE :] = jnp.concatenate([last, rest], axis=0)
-
-
-def whole(shape):
-    return pl.BlockSpec(shape, lambda *_: (0,) * len(shape))
 
 
 def one_hot_rows(table, block):
@@ -336,30 +334,22 @@
 
     other = lax.ppermute(stripe, "yl", swap)
     pieces = [stripe] + [shifted(stripe, shift) for shift in (1, 3, 2)]
-    iq, *pieces = lax.optimization_barrier((iq, *pieces))
+    far_pieces = [shifted(other, shift) for shift in (1, 3, 2)]
+    iq, *far_pieces = lax.optimization_barrier((iq, *far_pieces))
     iq = lax.all_to_all(iq, ROWS, 0, 0, tiled=True)
-    pieces += [other] + [shifted(other, shift) for shift in (1, 3, 2)]
+    pieces += [other] + far_pieces
     pieces += [lax.ppermute(piece, "core", swap) for piece in pieces]
 
     count = 2 * main_local * TILE
     target_part, index_keys = pl.pallas_call(
         attend_kernel,
-        grid_spec=pltpu.PrefetchScalarGridSpec(
-            num_scalar_prefetch=1,
-            grid=(1,),
-            in_specs=[whole((TILE, width))] * 16
-            + [
-                pl.BlockSpec((main_local, lat_width, TILE), lambda i, facts: (0, 0, facts[CORE])),
-                whole((main_local, lat_width, TILE)),
-            ],
-            out_specs=[whole((TILE, key_span)), whole((key_span, idx_width))],
-            scratch_shapes=[
-                pltpu.VMEM((key_span, lat_width), bf16),
-                pltpu.VMEM((key_span, TILE), f32),
-                pltpu.VMEM((key_span, 2 * TILE), f32),
-                pltpu.VMEM((key_span, 2 * TILE), f32),
-            ],
-        ),
+        in_specs=[smem] + [vmem] * 18,
+        scratch_shapes=[
+            pltpu.VMEM((key_span, lat_width), bf16),
+            pltpu.VMEM((key_span, TILE), f32),
+            pltpu.VMEM((key_span, 2 * TILE), f32),
+            pltpu.VMEM((key_span, 2 * TILE), f32),
+        ],
         out_shape=[
             jax.ShapeDtypeStruct((TILE, key_span), f32),
             jax.ShapeDtypeStruct((key_span, idx_width), bf16),
@@ -377,9 +367,7 @@
 
     score = pl.pallas_call(
         score_kernel,
-        grid=(1,),
-        in_specs=[whole(iq.shape), whole((key_span, idx_width))],
-        out_specs=whole((QROWS, key_span)),
+        in_specs=[vmem] * 2,
         out_shape=jax.ShapeDtypeStruct((QROWS, key_span), f32),
         compiler_params=params,
         cost_estimate=pl.CostEstimate(
@@ -390,16 +378,7 @@
 
     score_grad, loss, key_part = pl.pallas_call(
         key_grad_kernel,
-        grid=(1,),
-        in_specs=[smem]
-        + [whole((lanes // 2, QROWS, key_span)), whole((QROWS, key_span))]
-        + [whole(iq.shape), whole((key_span, idx_width))]
-        + [whole((1, key_span)), whole((QROWS, 1))],
-        out_specs=[
-            whole((heads_rows, key_span)),
-            whole((QROWS, 1)),
-            whole((lanes, idx_width, TILE)),
-        ],
+        in_specs=[smem] + [vmem] * 6,
         out_shape=[
             jax.ShapeDtypeStruct((heads_rows, key_span), f32),
             jax.ShapeDtypeStruct((QROWS, 1), f32),
@@ -416,10 +395,7 @@
     packed_shape = (lanes, heads_rows + 2 * STRIPE, idx_width)
     packed = pl.pallas_call(
         query_grad_kernel,
-        grid=(1,),
-        in_specs=[whole((heads_rows, key_span)), whole((QROWS, 1))]
-        + [whole(iq.shape), whole((key_span, idx_width))],
-        out_specs=whole(packed_shape),
+        in_specs=[vmem] * 4,
         out_shape=jax.ShapeDtypeStruct(packed_shape, f32),
         compiler_params=params,
         cost_estimate=pl.CostEstimate(

time: 165 us -> 173 us (1.048)
  local copies, waits for them, and re-layouts: 13.3 us -> 24.5 us
  waiting for transfers between devices: 54.6 us -> 44.2 us
  starting transfers between devices: 57.4 us -> 65.6 us
  Pallas kernels: 31.9 us -> 26 us
  other arithmetic: 4.4 us -> 7.93 us
    ppermute x6, waiting for transfers between devices: 8.52 us -> 0.02 us  [shifted(): return lax.ppermute(value, 'x', ring)]
    unnamed x39 -> x41, local copies, waits for them, and re-layouts: 2.42 us -> 9.96 us
    all_to_all x1, waiting for transfers between devices: 7.06 us -> 0.01 us  [body(): arrived = lax.all_to_all(send, CTX, 0, 0, tiled=True)]
    pallas_call x4, Pallas kernels: 28.6 us -> 23.5 us  [the longest x1 13.7 us: body(): pl.pallas_call(attend_kernel, in_specs=[smem] + [vmem] * 18, scratch_shap...]
    all_to_all x1, starting transfers between devices: 5.53 us -> 10.6 us  [body(): back = lax.all_to_all(back, CTX, 0, 0, tiled=True)]
    mul x2, local copies, waits for them, and re-layouts: 2.38 us -> 4.76 us  [one_hot_rows(): table[:, None, :, None] * eye[None, :, None, :]]
    all_to_all x1, waiting for transfers between devices: 11.7 us -> 14.1 us  [body(): target_parts = lax.all_to_all(target_part, ('yl', 'x'), 0, 0, tiled=True)]
    ppermute x6, starting transfers between devices: 7.27 us -> 9.61 us  [shifted(): return lax.ppermute(value, 'x', ring)]
  transfers between devices with their start and end apart: 22 -> 22, of which waited for: 8 -> 5; matrix products, arithmetic and copies ran while one was open for 7% -> 12% of each run, Pallas kernels for 14% -> 11%
where the time goes in v2:
time: 173 us; the launch traced here: 172 us
  starting transfers between devices  65.6 us (38%)
  waiting for transfers between devices  44.2 us (26%)
  Pallas kernels  26 us (15%)
  local copies, waits for them, and re-layouts  24.5 us (14%)
  other arithmetic  7.93 us (5%)
  matrix products  2.51 us (1%)
    all_to_all x1, waiting for transfers between devices, body(): target_parts = lax.all_to_all(target_part, ('yl', 'x'), 0, 0, tiled=True)  14.1 us
    pallas_call x1, Pallas kernels, body(): pl.pallas_call(attend_kernel, in_specs=[smem] + [vmem] * 18, scratch_shap...  13.7 us
    all_to_all x1, waiting for transfers between devices, body(): packed = lax.all_to_all(packed, ROWS, 0, 0, tiled=True)  11.9 us
    ppermute x8, starting transfers between devices, body(): pieces += [lax.ppermute(piece, 'core', swap) for piece in pieces]  11.9 us
    all_to_all x1, starting transfers between devices, body(): arrived = lax.all_to_all(send, CTX, 0, 0, tiled=True)  11.9 us
    all_to_all x1, starting transfers between devices, body(): back = lax.all_to_all(back, CTX, 0, 0, tiled=True)  10.6 us
    unnamed x41, local copies, waits for them, and re-layouts  9.96 us
    all_to_all x1, waiting for transfers between devices, body(): key_sum = lax.all_to_all(key_part, HEAD, 0, 0, tiled=True)  9.83 us
  transfers between devices with their start and end apart: 22, of which 5 were waited for; matrix products, arithmetic and copies ran while one was open for 12% of the time, Pallas kernels for 11%

profile of v2, /device:TPU:1, one launch (start us, length us, event | category | flops | bytes accessed | tf_op | source)
XLA Modules:
  0.0 171.7 jit_solution(13762182071579684448)
XLA Ops:
  3.5 2.6 %stripes.1 = bf16[384,704]{1,0:T(8,128)(2,1)} custom-call(s32[2]{0:T(128)S(1)} %pad_add_fusion.where, s32[16,16]{1,0:T(8,128)S(1)} %copy-done.4, bf16[768,128]{1,0:T(8,128)(2,1)S(1)} %copy-done.3, bf16[576,768]{1,0:T(8,128)(2,1)S(1)} %bitcast.73), custom_call_target="tpu_custom_call" | custom-call | tf_op jit(solution)/shard_map/stripes/pallas_call | solution.py:267
  6.1 11.9 %all-to-all-start = ((bf16[16,24,704]{2,1,0:T(8,128)(2,1)}), bf16[16,24,704]{2,1,0:T(8,128)(2,1)S(1)}, u32[]{:S(2)}, u32[]{:S(2)}) async-start(bf16[16,24,704]{2,1,0:T(8,128)(2,1)} %bitcast.3), calls=%async_computation | async-start | bytes 1179648 | tf_op jit(solution)/shard_map/all_to_all | solution.py:277
  24.5 2.0 %reshape.383 = bf16[16,64,256]{2,1,0:T(8,128)(2,1)} reshape(bf16[256,4,256]{2,1,0:T(4,128)(2,1)} %copy.51) | data formatting | bytes 1048576 | tf_op jit(solution)/shard_map/reshape | solution.py:289
  28.6 3.5 %mul.166 = bf16[128,384]{1,0:T(8,128)(2,1)} reshape(bf16[16,8,48,8]{3,2,1,0:T(8,128)(2,1)} %broadcast_multiply_fusion) | data formatting | bytes 196608 | tf_op jit(solution)/shard_map/mul | solution.py:237
  40.5 2.7 %collective-permute-start.2 = (bf16[128,704]{1,0:T(8,128)(2,1)S(1)}, bf16[128,704]{1,0:T(8,128)(2,1)S(1)}, u32[]{:S(2)}, u32[]{:S(2)}) collective-permute-start(bf16[128,704]{1,0:T(8,128)(2,1)S(1)} %fusion.26.refs_0_), channel_id=1, source_target_pairs={{0,4},{2,6},{4,0},{6,2},{1,5},{3,7},{5,1},{7,3},{8,12},{10,14},{12... | collective-permute-start | bytes 540680 | tf_op jit(solution)/shard_map/ppermute | solution.py:265
  43.2 1.8 %collective-permute-done.3.refs_4_ = bf16[128,704]{1,0:T(8,128)(2,1)S(1)} collective-permute-done((bf16[128,704]{1,0:T(8,128)(2,1)S(1)}, bf16[128,704]{1,0:T(8,128)(2,1)S(1)}, u32[]{:S(2)}, u32[]{:S(2)}) %collective-permute-start.3) | collective-permute-done | bytes 180256 | tf_op jit(solution)/shard_map/ppermute | solution.py:335
  47.7 1.5 collective-permute-start.6
  49.5 2.4 %collective-permute-start.1 = (bf16[128,704]{1,0:T(8,128)(2,1)S(1)}, bf16[128,704]{1,0:T(8,128)(2,1)}, u32[]{:S(2)}, u32[]{:S(2)}) collective-permute-start(bf16[128,704]{1,0:T(8,128)(2,1)S(1)} %fusion.26.refs_0_), channel_id=1, source_target_pairs={{0,6},{2,0},{4,2},{6,4},{1,7},{3,1},{5,3},{7,5},{8,14},{10,8},{12,... | collective-permute-start | bytes 540680 | tf_op jit(solution)/shard_map/ppermute | solution.py:265
  51.9 6.8 %collective-permute-start.7 = (bf16[128,704]{1,0:T(8,128)(2,1)S(1)}, bf16[128,704]{1,0:T(8,128)(2,1)S(1)}, u32[]{:S(2)}, u32[]{:S(2)}) collective-permute-start(bf16[128,704]{1,0:T(8,128)(2,1)S(1)} %fusion.26.refs_0_), channel_id=1, source_target_pairs={{0,1},{1,0},{2,3},{3,2},{4,5},{5,4},{6,7},{7,6},{8,9},{9,8},{10,11... | collective-permute-start | bytes 540680 | tf_op jit(solution)/shard_map/ppermute | solution.py:341
  58.7 2.3 %collective-permute-start.11 = (bf16[128,704]{1,0:T(8,128)(2,1)S(1)}, bf16[128,704]{1,0:T(8,128)(2,1)S(1)}, u32[]{:S(2)}, u32[]{:S(2)}) collective-permute-start(bf16[128,704]{1,0:T(8,128)(2,1)S(1)} %collective-permute-done.3.refs_4_), channel_id=1, source_target_pairs={{0,1},{1,0},{2,3},{3,2},{4,5},{5,4},{6,7},{7,6},{8,9},{9,8},{10,11... | collective-permute-start | bytes 540680 | tf_op jit(solution)/shard_map/ppermute | solution.py:341
  61.1 1.7 %collective-permute-start.8 = (bf16[128,704]{1,0:T(8,128)(2,1)}, bf16[128,704]{1,0:T(8,128)(2,1)}, u32[]{:S(2)}, u32[]{:S(2)}) collective-permute-start(bf16[128,704]{1,0:T(8,128)(2,1)} %collective-permute-done.refs_1_), channel_id=1, source_target_pairs={{0,1},{1,0},{2,3},{3,2},{4,5},{5,4},{6,7},{7,6},{8,9},{9,8},{10,11... | collective-permute-start | bytes 540680 | tf_op jit(solution)/shard_map/ppermute | solution.py:341
  65.9 4.5 %all-to-all-start.2 = ((bf16[16,64,256]{2,1,0:T(8,128)(2,1)}), bf16[16,64,256]{2,1,0:T(8,128)(2,1)S(1)}, u32[]{:S(2)}, u32[]{:S(2)}) async-start(bf16[16,64,256]{2,1,0:T(8,128)(2,1)} %reshape.383), calls=%async_computation.2 | async-start | bytes 1048576 | tf_op jit(solution)/shard_map/all_to_all | solution.py:339
  73.3 13.7 %attend.1 = (f32[128,2048]{1,0:T(8,128)}, bf16[2048,128]{1,0:T(8,128)(2,1)S(1)}) custom-call(s32[20]{0:T(128)S(1)} %concatenate.6.facts, bf16[128,704]{1,0:T(8,128)(2,1)S(1)} %fusion.26.refs_0_, bf16[128,704]{1,0:T(8,128)(2,1)} %collective-permute-done.refs_1_, bf16[128,704]{1,0:T(8,128)(2,1)} %collective-permute-done.1.refs_2_, ...), custom_call_target="tpu_custom_call" | custom-call | flops 4831838208 | bytes 8388608 | tf_op jit(solution)/shard_map/attend/pallas_call | solution.py:344
  87.8 5.2 %all-to-all-start.1 = ((f32[8,16,2048]{2,1,0:T(8,128)}), f32[8,16,2048]{2,1,0:T(8,128)S(1)}, u32[]{:S(2)}, u32[]{:S(2)}) async-start(f32[8,16,2048]{2,1,0:T(8,128)} %bitcast.32), calls=%async_computation.1 | async-start | bytes 2097152 | tf_op jit(solution)/shard_map/all_to_all | solution.py:365
  93.1 1.7 score.1
  94.8 14.1 %all-to-all-done.1.target_parts = f32[8,16,2048]{2,1,0:T(8,128)S(1)} async-done(((f32[8,16,2048]{2,1,0:T(8,128)}), f32[8,16,2048]{2,1,0:T(8,128)S(1)}, u32[]{:S(2)}, u32[]{:S(2)}) %all-to-all-start.1) | async-done | bytes 1048608 | tf_op jit(solution)/shard_map/all_to_all | solution.py:365
  108.9 4.1 %key_grad.1 = (f32[64,2048]{1,0:T(8,128)S(1)}, f32[16,1]{1,0:T(8,128)S(1)}, bf16[16,128,128]{2,1,0:T(8,128)(2,1)}) custom-call(s32[20]{0:T(128)S(1)} %concatenate.6.facts, f32[8,16,2048]{2,1,0:T(8,128)S(1)} %all-to-all-done.1.target_parts, f32[16,2048]{1,0:T(8,128)S(1)} %score.1, bf16[16,64,256]{2,1,0:T(8,128)(2,1)S(1)} %all-to-all-done.2.queries, ...), custom_call_target="tpu_custom_call" | custom-call | flops 1073741824 | bytes 4194304 | tf_op jit(solution)/shard_map/key_grad/pallas_call | solution.py:379
  113.0 4.2 %all-to-all-start.3 = ((bf16[16,128,128]{2,1,0:T(8,128)(2,1)}), bf16[16,128,128]{2,1,0:T(8,128)(2,1)S(1)}, u32[]{:S(2)}, u32[]{:S(2)}) async-start(bf16[16,128,128]{2,1,0:T(8,128)(2,1)} %get-tuple-element.45), calls=%async_computation.3 | async-start | bytes 1048576 | tf_op jit(solution)/shard_map/all_to_all | solution.py:408
  117.3 9.8 %all-to-all-done.3 = bf16[16,128,128]{2,1,0:T(8,128)(2,1)S(1)} async-done(((bf16[16,128,128]{2,1,0:T(8,128)(2,1)}), bf16[16,128,128]{2,1,0:T(8,128)(2,1)S(1)}, u32[]{:S(2)}, u32[]{:S(2)}) %all-to-all-start.3) | async-done | bytes 524320 | tf_op jit(solution)/shard_map/all_to_all | solution.py:408
  128.1 10.6 %all-to-all-start.4 = ((f32[16,24,128]{2,1,0:T(8,128)}), f32[16,24,128]{2,1,0:T(8,128)S(1)}, u32[]{:S(2)}, u32[]{:S(2)}) async-start(f32[16,24,128]{2,1,0:T(8,128)} %fusion.5), calls=%async_computation.4 | async-start | bytes 393216 | tf_op jit(solution)/shard_map/all_to_all | solution.py:413
  138.9 3.9 %query_grad.1 = f32[16,80,128]{2,1,0:T(8,128)} custom-call(f32[64,2048]{1,0:T(8,128)S(1)} %get-tuple-element.42.score_grad, f32[16,1]{1,0:T(8,128)S(1)} %get-tuple-element.43.loss, bf16[16,64,256]{2,1,0:T(8,128)(2,1)S(1)} %all-to-all-done.2.queries, bf16[2048,128]{1,0:T(8,128)(2,1)S(1)} %copy-done.13), custom_call_target="tpu_custom_call" | custom-call | flops 1073741824 | bytes 4194304 | tf_op jit(solution)/shard_map/query_grad/pallas_call | solution.py:396
  142.8 6.6 %all-to-all-done.4 = f32[16,24,128]{2,1,0:T(8,128)S(1)} async-done(((f32[16,24,128]{2,1,0:T(8,128)}), f32[16,24,128]{2,1,0:T(8,128)S(1)}, u32[]{:S(2)}, u32[]{:S(2)}) %all-to-all-start.4) | async-done | bytes 196640 | tf_op jit(solution)/shard_map/all_to_all | solution.py:413
  150.4 6.2 %all-to-all-start.5 = ((f32[16,80,128]{2,1,0:T(8,128)}), f32[16,80,128]{2,1,0:T(8,128)S(1)}, u32[]{:S(2)}, u32[]{:S(2)}) async-start(f32[16,80,128]{2,1,0:T(8,128)} %constant_dynamic-update-slice_fusion), calls=%async_computation.5 | async-start | bytes 1310720 | tf_op jit(solution)/shard_map/all_to_all | solution.py:423
  156.7 11.9 %all-to-all-done.5 = f32[16,80,128]{2,1,0:T(8,128)S(1)} async-done(((f32[16,80,128]{2,1,0:T(8,128)}), f32[16,80,128]{2,1,0:T(8,128)S(1)}, u32[]{:S(2)}, u32[]{:S(2)}) %all-to-all-start.5) | async-done | bytes 655392 | tf_op jit(solution)/shard_map/all_to_all | solution.py:423
  (125 shorter events, 34.9 us)
Async XLA Ops:
  0.6 36.5 %copy-start = (f32[256]{0:T(256)S(1)}, f32[256]{0:T(256)}, u32[]{:S(2)}) copy-start(f32[256]{0:T(256)} %param.13) | copy-start | bytes 3076
  6.1 31.7 %all-to-all-start = ((bf16[16,24,704]{2,1,0:T(8,128)(2,1)}), bf16[16,24,704]{2,1,0:T(8,128)(2,1)S(1)}, u32[]{:S(2)}, u32[]{:S(2)}) async-start(bf16[16,24,704]{2,1,0:T(8,128)(2,1)} %bitcast.3), calls=%async_computation | async-start | bytes 1179648 | tf_op jit(solution)/shard_map/all_to_all | solution.py:277
  19.3 30.0 %collective-permute-start.15 = (bf16[8,576,128]{2,1,0:T(8,128)(2,1)}, bf16[8,576,128]{2,1,0:T(8,128)(2,1)}, u32[]{:S(2)}, u32[]{:S(2)}) collective-permute-start(bf16[8,576,128]{2,1,0:T(8,128)(2,1)} %dynamic-slice_bitcast_fusion), channel_id=1, source_target_pairs={{0,1},{1,0},{2,3},{3,2},{4,5},{5,4},{6,7},{7,6},{8,9},{9,8},{10,11... | collective-permute-start | bytes 3538952 | tf_op jit(solution)/shard_map/ppermute | solution.py:281
  40.0 5.0 %collective-permute-start.3 = (bf16[128,704]{1,0:T(8,128)(2,1)S(1)}, bf16[128,704]{1,0:T(8,128)(2,1)S(1)}, u32[]{:S(2)}, u32[]{:S(2)}) collective-permute-start(bf16[128,704]{1,0:T(8,128)(2,1)S(1)} %fusion.26.refs_0_), channel_id=1, source_target_pairs={{0,8},{8,0},{1,9},{9,1},{2,10},{10,2},{3,11},{11,3},{4,12},{12,4},... | collective-permute-start | bytes 540680 | tf_op jit(solution)/shard_map/ppermute | solution.py:335
  40.5 9.1 %collective-permute-start.2 = (bf16[128,704]{1,0:T(8,128)(2,1)S(1)}, bf16[128,704]{1,0:T(8,128)(2,1)S(1)}, u32[]{:S(2)}, u32[]{:S(2)}) collective-permute-start(bf16[128,704]{1,0:T(8,128)(2,1)S(1)} %fusion.26.refs_0_), channel_id=1, source_target_pairs={{0,4},{2,6},{4,0},{6,2},{1,5},{3,7},{5,1},{7,3},{8,12},{10,14},{12... | collective-permute-start | bytes 540680 | tf_op jit(solution)/shard_map/ppermute | solution.py:265
  45.0 6.9 %collective-permute-start.4 = (bf16[128,704]{1,0:T(8,128)(2,1)S(1)}, bf16[128,704]{1,0:T(8,128)(2,1)}, u32[]{:S(2)}, u32[]{:S(2)}) collective-permute-start(bf16[128,704]{1,0:T(8,128)(2,1)S(1)} %collective-permute-done.3.refs_4_), channel_id=1, source_target_pairs={{0,2},{2,4},{4,6},{6,0},{1,3},{3,5},{5,7},{7,1},{8,10},{10,12},{12... | collective-permute-start | bytes 540680 | tf_op jit(solution)/shard_map/ppermute | solution.py:265
  46.2 12.5 %collective-permute-start.5 = (bf16[128,704]{1,0:T(8,128)(2,1)S(1)}, bf16[128,704]{1,0:T(8,128)(2,1)}, u32[]{:S(2)}, u32[]{:S(2)}) collective-permute-start(bf16[128,704]{1,0:T(8,128)(2,1)S(1)} %collective-permute-done.3.refs_4_), channel_id=1, source_target_pairs={{0,6},{2,0},{4,2},{6,4},{1,7},{3,1},{5,3},{7,5},{8,14},{10,8},{12,... | collective-permute-start | bytes 540680 | tf_op jit(solution)/shard_map/ppermute | solution.py:265
  47.7 11.0 %collective-permute-start.6 = (bf16[128,704]{1,0:T(8,128)(2,1)S(1)}, bf16[128,704]{1,0:T(8,128)(2,1)}, u32[]{:S(2)}, u32[]{:S(2)}) collective-permute-start(bf16[128,704]{1,0:T(8,128)(2,1)S(1)} %collective-permute-done.3.refs_4_), channel_id=1, source_target_pairs={{0,4},{2,6},{4,0},{6,2},{1,5},{3,7},{5,1},{7,3},{8,12},{10,14},{12... | collective-permute-start | bytes 540680 | tf_op jit(solution)/shard_map/ppermute | solution.py:265
  49.2 11.8 %collective-permute-start = (bf16[128,704]{1,0:T(8,128)(2,1)S(1)}, bf16[128,704]{1,0:T(8,128)(2,1)}, u32[]{:S(2)}, u32[]{:S(2)}) collective-permute-start(bf16[128,704]{1,0:T(8,128)(2,1)S(1)} %fusion.26.refs_0_), channel_id=1, source_target_pairs={{0,2},{2,4},{4,6},{6,0},{1,3},{3,5},{5,7},{7,1},{8,10},{10,12},{12... | collective-permute-start | bytes 540680 | tf_op jit(solution)/shard_map/ppermute | solution.py:265
  49.5 13.3 %collective-permute-start.1 = (bf16[128,704]{1,0:T(8,128)(2,1)S(1)}, bf16[128,704]{1,0:T(8,128)(2,1)}, u32[]{:S(2)}, u32[]{:S(2)}) collective-permute-start(bf16[128,704]{1,0:T(8,128)(2,1)S(1)} %fusion.26.refs_0_), channel_id=1, source_target_pairs={{0,6},{2,0},{4,2},{6,4},{1,7},{3,1},{5,3},{7,5},{8,14},{10,8},{12,... | collective-permute-start | bytes 540680 | tf_op jit(solution)/shard_map/ppermute | solution.py:265
  51.9 10.9 %collective-permute-start.7 = (bf16[128,704]{1,0:T(8,128)(2,1)S(1)}, bf16[128,704]{1,0:T(8,128)(2,1)S(1)}, u32[]{:S(2)}, u32[]{:S(2)}) collective-permute-start(bf16[128,704]{1,0:T(8,128)(2,1)S(1)} %fusion.26.refs_0_), channel_id=1, source_target_pairs={{0,1},{1,0},{2,3},{3,2},{4,5},{5,4},{6,7},{7,6},{8,9},{9,8},{10,11... | collective-permute-start | bytes 540680 | tf_op jit(solution)/shard_map/ppermute | solution.py:341
  58.7 5.3 %collective-permute-start.10 = (bf16[128,704]{1,0:T(8,128)(2,1)S(1)}, bf16[128,704]{1,0:T(8,128)(2,1)S(1)}, u32[]{:S(2)}, u32[]{:S(2)}) collective-permute-start(bf16[128,704]{1,0:T(8,128)(2,1)S(1)} %collective-permute-done.2.refs_3_), channel_id=1, source_target_pairs={{0,1},{1,0},{2,3},{3,2},{4,5},{5,4},{6,7},{7,6},{8,9},{9,8},{10,11... | collective-permute-start | bytes 540680 | tf_op jit(solution)/shard_map/ppermute | solution.py:341
  58.7 5.9 %collective-permute-start.11 = (bf16[128,704]{1,0:T(8,128)(2,1)S(1)}, bf16[128,704]{1,0:T(8,128)(2,1)S(1)}, u32[]{:S(2)}, u32[]{:S(2)}) collective-permute-start(bf16[128,704]{1,0:T(8,128)(2,1)S(1)} %collective-permute-done.3.refs_4_), channel_id=1, source_target_pairs={{0,1},{1,0},{2,3},{3,2},{4,5},{5,4},{6,7},{7,6},{8,9},{9,8},{10,11... | collective-permute-start | bytes 540680 | tf_op jit(solution)/shard_map/ppermute | solution.py:341
  61.1 9.4 %collective-permute-start.8 = (bf16[128,704]{1,0:T(8,128)(2,1)}, bf16[128,704]{1,0:T(8,128)(2,1)}, u32[]{:S(2)}, u32[]{:S(2)}) collective-permute-start(bf16[128,704]{1,0:T(8,128)(2,1)} %collective-permute-done.refs_1_), channel_id=1, source_target_pairs={{0,1},{1,0},{2,3},{3,2},{4,5},{5,4},{6,7},{7,6},{8,9},{9,8},{10,11... | collective-permute-start | bytes 540680 | tf_op jit(solution)/shard_map/ppermute | solution.py:341
  62.8 7.6 %collective-permute-start.9 = (bf16[128,704]{1,0:T(8,128)(2,1)}, bf16[128,704]{1,0:T(8,128)(2,1)}, u32[]{:S(2)}, u32[]{:S(2)}) collective-permute-start(bf16[128,704]{1,0:T(8,128)(2,1)} %collective-permute-done.1.refs_2_), channel_id=1, source_target_pairs={{0,1},{1,0},{2,3},{3,2},{4,5},{5,4},{6,7},{7,6},{8,9},{9,8},{10,11... | collective-permute-start | bytes 540680 | tf_op jit(solution)/shard_map/ppermute | solution.py:341
  63.5 7.0 %collective-permute-start.12 = (bf16[128,704]{1,0:T(8,128)(2,1)}, bf16[128,704]{1,0:T(8,128)(2,1)}, u32[]{:S(2)}, u32[]{:S(2)}) collective-permute-start(bf16[128,704]{1,0:T(8,128)(2,1)} %collective-permute-done.4.refs_5_), channel_id=1, source_target_pairs={{0,1},{1,0},{2,3},{3,2},{4,5},{5,4},{6,7},{7,6},{8,9},{9,8},{10,11... | collective-permute-start | bytes 540680 | tf_op jit(solution)/shard_map/ppermute | solution.py:341
  64.7 5.8 %collective-permute-start.13 = (bf16[128,704]{1,0:T(8,128)(2,1)}, bf16[128,704]{1,0:T(8,128)(2,1)}, u32[]{:S(2)}, u32[]{:S(2)}) collective-permute-start(bf16[128,704]{1,0:T(8,128)(2,1)} %collective-permute-done.5.refs_6_), channel_id=1, source_target_pairs={{0,1},{1,0},{2,3},{3,2},{4,5},{5,4},{6,7},{7,6},{8,9},{9,8},{10,11... | collective-permute-start | bytes 540680 | tf_op jit(solution)/shard_map/ppermute | solution.py:341
  65.4 5.1 %collective-permute-start.14 = (bf16[128,704]{1,0:T(8,128)(2,1)}, bf16[128,704]{1,0:T(8,128)(2,1)}, u32[]{:S(2)}, u32[]{:S(2)}) collective-permute-start(bf16[128,704]{1,0:T(8,128)(2,1)} %collective-permute-done.6.refs_7_), channel_id=1, source_target_pairs={{0,1},{1,0},{2,3},{3,2},{4,5},{5,4},{6,7},{7,6},{8,9},{9,8},{10,11... | collective-permute-start | bytes 540680 | tf_op jit(solution)/shard_map/ppermute | solution.py:341
  65.9 21.9 %all-to-all-start.2 = ((bf16[16,64,256]{2,1,0:T(8,128)(2,1)}), bf16[16,64,256]{2,1,0:T(8,128)(2,1)S(1)}, u32[]{:S(2)}, u32[]{:S(2)}) async-start(bf16[16,64,256]{2,1,0:T(8,128)(2,1)} %reshape.383), calls=%async_computation.2 | async-start | bytes 1048576 | tf_op jit(solution)/shard_map/all_to_all | solution.py:339
  87.8 21.1 %all-to-all-start.1 = ((f32[8,16,2048]{2,1,0:T(8,128)}), f32[8,16,2048]{2,1,0:T(8,128)S(1)}, u32[]{:S(2)}, u32[]{:S(2)}) async-start(f32[8,16,2048]{2,1,0:T(8,128)} %bitcast.32), calls=%async_computation.1 | async-start | bytes 2097152 | tf_op jit(solution)/shard_map/all_to_all | solution.py:365
  94.8 22.4 %copy-start.15 = (bf16[128,384]{1,0:T(8,128)(2,1)S(1)}, bf16[128,384]{1,0:T(8,128)(2,1)}, u32[]{:S(2)}) copy-start(bf16[128,384]{1,0:T(8,128)(2,1)} %mul.166) | copy-start | bytes 294916
  113.0 14.1 %all-to-all-start.3 = ((bf16[16,128,128]{2,1,0:T(8,128)(2,1)}), bf16[16,128,128]{2,1,0:T(8,128)(2,1)S(1)}, u32[]{:S(2)}, u32[]{:S(2)}) async-start(bf16[16,128,128]{2,1,0:T(8,128)(2,1)} %get-tuple-element.45), calls=%async_computation.3 | async-start | bytes 1048576 | tf_op jit(solution)/shard_map/all_to_all | solution.py:408
  128.1 21.2 %all-to-all-start.4 = ((f32[16,24,128]{2,1,0:T(8,128)}), f32[16,24,128]{2,1,0:T(8,128)S(1)}, u32[]{:S(2)}, u32[]{:S(2)}) async-start(f32[16,24,128]{2,1,0:T(8,128)} %fusion.5), calls=%async_computation.4 | async-start | bytes 393216 | tf_op jit(solution)/shard_map/all_to_all | solution.py:413
  150.4 18.2 %all-to-all-start.5 = ((f32[16,80,128]{2,1,0:T(8,128)}), f32[16,80,128]{2,1,0:T(8,128)S(1)}, u32[]{:S(2)}, u32[]{:S(2)}) async-start(f32[16,80,128]{2,1,0:T(8,128)} %constant_dynamic-update-slice_fusion), calls=%async_computation.5 | async-start | bytes 1310720 | tf_op jit(solution)/shard_map/all_to_all | solution.py:423
  (18 other events, 64.7 us)

commit v3 on v1

--- a/solution.py
+++ b/solution.py
@@ -14,6 +14,7 @@
 QROWS = 16
 STRIPE = 8
 VMEM = 60 * 1024 * 1024
+SMALL_VMEM = 32 * 1024 * 1024
 
 SLOTS, CORE, FIRST = 16, 18, 19
 
@@ -259,6 +260,7 @@
     heads_rows = index_local * QROWS
     swap = [(0, 1), (1, 0)]
     params = pltpu.CompilerParams(vmem_limit_bytes=VMEM)
+    small = pltpu.CompilerParams(vmem_limit_bytes=SMALL_VMEM)
     vmem = pl.BlockSpec(memory_space=pltpu.VMEM)
     smem = pl.BlockSpec(memory_space=pltpu.SMEM)
 
@@ -336,9 +338,10 @@
 
     other = lax.ppermute(stripe, "yl", swap)
     pieces = [stripe] + [shifted(stripe, shift) for shift in (1, 3, 2)]
-    iq, *pieces = lax.optimization_barrier((iq, *pieces))
+    far_pieces = [shifted(other, shift) for shift in (1, 3, 2)]
+    iq, *far_pieces = lax.optimization_barrier((iq, *far_pieces))
     iq = lax.all_to_all(iq, ROWS, 0, 0, tiled=True)
-    pieces += [other] + [shifted(other, shift) for shift in (1, 3, 2)]
+    pieces += [other] + far_pieces
     pieces += [lax.ppermute(piece, "core", swap) for piece in pieces]
 
     count = 2 * main_local * TILE
@@ -377,11 +380,9 @@
 
     score = pl.pallas_call(
         score_kernel,
-        grid=(1,),
-        in_specs=[whole(iq.shape), whole((key_span, idx_width))],
-        out_specs=whole((QROWS, key_span)),
+        in_specs=[vmem] * 2,
         out_shape=jax.ShapeDtypeStruct((QROWS, key_span), f32),
-        compiler_params=params,
+        compiler_params=small,
         cost_estimate=pl.CostEstimate(
             flops=2 * rows_all * key_span * idx_width, bytes_accessed=2**20, transcendentals=0
         ),
@@ -390,23 +391,14 @@
 
     score_grad, loss, key_part = pl.pallas_call(
         key_grad_kernel,
-        grid=(1,),
-        in_specs=[smem]
-        + [whole((lanes // 2, QROWS, key_span)), whole((QROWS, key_span))]
-        + [whole(iq.shape), whole((key_span, idx_width))]
-        + [whole((1, key_span)), whole((QROWS, 1))],
-        out_specs=[
-            whole((heads_rows, key_span)),
-            whole((QROWS, 1)),
-            whole((lanes, idx_width, TILE)),
-        ],
+        in_specs=[smem] + [vmem] * 6,
         out_shape=[
             jax.ShapeDtypeStruct((heads_rows, key_span), f32),
             jax.ShapeDtypeStruct((QROWS, 1), f32),
             jax.ShapeDtypeStruct((lanes, idx_width, TILE), bf16),
         ],
         scratch_shapes=[pltpu.VMEM((rows_all, key_span), bf16)],
-        compiler_params=params,
+        compiler_params=small,
         cost_estimate=pl.CostEstimate(
             flops=4 * rows_all * key_span * idx_width, bytes_accessed=4 * 2**20, transcendentals=0
         ),
@@ -416,12 +408,9 @@
     packed_shape = (lanes, heads_rows + 2 * STRIPE, idx_width)
     packed = pl.pallas_call(
         query_grad_kernel,
-        grid=(1,),
-        in_specs=[whole((heads_rows, key_span)), whole((QROWS, 1))]
-        + [whole(iq.shape), whole((key_span, idx_width))],
-        out_specs=whole(packed_shape),
+        in_specs=[vmem] * 4,
         out_shape=jax.ShapeDtypeStruct(packed_shape, f32),
-        compiler_params=params,
+        compiler_params=small,
         cost_estimate=pl.CostEstimate(
             flops=4 * rows_all * key_span * idx_width, bytes_accessed=4 * 2**20, transcendentals=0
         ),

time: 165 us -> 159 us (0.964)
  Pallas kernels: 31.9 us -> 28.2 us
  starting transfers between devices: 57.4 us -> 60.3 us
  local copies, waits for them, and re-layouts: 13.3 us -> 10.7 us
  waiting for transfers between devices: 54.6 us -> 52.1 us
    ppermute x6, waiting for transfers between devices: 8.52 us -> 0.69 us  [shifted(): return lax.ppermute(value, 'x', ring)]
    pallas_call x3, Pallas kernels: 13.5 us -> 9.73 us  [the longest x1 4.14 us: body(): pl.pallas_call(key_grad_kernel, in_specs=[smem] + [vmem] * 6, out_shape=[...]
    all_to_all x1, waiting for transfers between devices: 11.7 us -> 14.1 us  [body(): target_parts = lax.all_to_all(target_part, ('yl', 'x'), 0, 0, tiled=True)]
    ppermute x6, starting transfers between devices: 7.27 us -> 9.63 us  [shifted(): return lax.ppermute(value, 'x', ring)]
  transfers between devices with their start and end apart: 22 -> 22, of which waited for: 8 -> 7; matrix products, arithmetic and copies ran while one was open for 7% -> 6% of each run, Pallas kernels for 14% -> 13%
where the time goes in v3:
time: 159 us; the launch traced here: 158 us
  starting transfers between devices  60.3 us (38%)
  waiting for transfers between devices  52.1 us (33%)
  Pallas kernels  28.2 us (18%)
  local copies, waits for them, and re-layouts  10.7 us (7%)
  other arithmetic  4.45 us (3%)
    pallas_call x1, Pallas kernels, body(): pl.pallas_call(attend_kernel, grid_spec=pltpu.PrefetchScalarGridSpec(num_...  15.1 us
    all_to_all x1, waiting for transfers between devices, body(): target_parts = lax.all_to_all(target_part, ('yl', 'x'), 0, 0, tiled=True)  14.1 us
    ppermute x8, starting transfers between devices, body(): pieces += [lax.ppermute(piece, 'core', swap) for piece in pieces]  12.2 us
    all_to_all x1, waiting for transfers between devices, body(): packed = lax.all_to_all(packed, ROWS, 0, 0, tiled=True)  11.9 us
    all_to_all x1, starting transfers between devices, body(): arrived = lax.all_to_all(send, CTX, 0, 0, tiled=True)  11.9 us
    all_to_all x1, waiting for transfers between devices, body(): key_sum = lax.all_to_all(key_part, HEAD, 0, 0, tiled=True)  9.84 us
    ppermute x6, starting transfers between devices, shifted(): return lax.ppermute(value, 'x', ring)  9.63 us
    all_to_all x1, waiting for transfers between devices, body(): arrived = lax.all_to_all(send, CTX, 0, 0, tiled=True)  7.6 us
  transfers between devices with their start and end apart: 22, of which 7 were waited for; matrix products, arithmetic and copies ran while one was open for 6% of the time, Pallas kernels for 13%

profile of v3, /device:TPU:1, one launch (start us, length us, event | category | flops | bytes accessed | tf_op | source)
XLA Modules:
  0.0 158.3 jit_solution(13690880406063119168)
XLA Ops:
  1.2 3.3 %stripes.1 = bf16[384,704]{1,0:T(8,128)(2,1)} custom-call(s32[2]{0:T(128)} %pad_add_fusion.where, s32[16,16]{1,0:T(8,128)} %selection.1, bf16[768,128]{1,0:T(8,128)(2,1)} %index_key.1, bf16[576,768]{1,0:T(8,128)(2,1)} %bitcast.77), custom_call_target="tpu_custom_call" | custom-call | tf_op jit(solution)/shard_map/stripes/pallas_call | solution.py:271
  4.6 11.9 %all-to-all-start = ((bf16[16,24,704]{2,1,0:T(8,128)(2,1)}), bf16[16,24,704]{2,1,0:T(8,128)(2,1)S(1)}, u32[]{:S(2)}, u32[]{:S(2)}) async-start(bf16[16,24,704]{2,1,0:T(8,128)(2,1)} %bitcast.74), calls=%async_computation | async-start | bytes 1179648 | tf_op jit(solution)/shard_map/all_to_all | solution.py:281
  16.5 1.4 dynamic-slice_bitcast_fusion
  22.2 1.8 %mul.166 = bf16[128,384]{1,0:T(8,128)(2,1)S(1)} reshape(bf16[16,8,48,8]{3,2,1,0:T(8,128)(2,1)S(1)} %broadcast_multiply_fusion) | data formatting | bytes 196608 | tf_op jit(solution)/shard_map/mul | solution.py:240
  27.3 7.6 %all-to-all-done = bf16[16,24,704]{2,1,0:T(8,128)(2,1)S(1)} async-done(((bf16[16,24,704]{2,1,0:T(8,128)(2,1)}), bf16[16,24,704]{2,1,0:T(8,128)(2,1)S(1)}, u32[]{:S(2)}, u32[]{:S(2)}) %all-to-all-start) | async-done | bytes 540704 | tf_op jit(solution)/shard_map/all_to_all | solution.py:281
  35.6 2.7 %collective-permute-start.2 = (bf16[128,704]{1,0:T(8,128)(2,1)S(1)}, bf16[128,704]{1,0:T(8,128)(2,1)S(1)}, u32[]{:S(2)}, u32[]{:S(2)}) collective-permute-start(bf16[128,704]{1,0:T(8,128)(2,1)S(1)} %fusion.26.refs_0_), channel_id=1, source_target_pairs={{0,4},{2,6},{4,0},{6,2},{1,5},{3,7},{5,1},{7,3},{8,12},{10,14},{12... | collective-permute-start | bytes 540680 | tf_op jit(solution)/shard_map/ppermute | solution.py:269
  41.0 1.5 collective-permute-start.5
  42.4 1.5 collective-permute-start.6
  44.3 2.4 %collective-permute-start.1 = (bf16[128,704]{1,0:T(8,128)(2,1)S(1)}, bf16[128,704]{1,0:T(8,128)(2,1)S(1)}, u32[]{:S(2)}, u32[]{:S(2)}) collective-permute-start(bf16[128,704]{1,0:T(8,128)(2,1)S(1)} %fusion.26.refs_0_), channel_id=1, source_target_pairs={{0,6},{2,0},{4,2},{6,4},{1,7},{3,1},{5,3},{7,5},{8,14},{10,8},{12,... | collective-permute-start | bytes 540680 | tf_op jit(solution)/shard_map/ppermute | solution.py:269
  47.3 7.6 %collective-permute-start.7 = (bf16[128,704]{1,0:T(8,128)(2,1)S(1)}, bf16[128,704]{1,0:T(8,128)(2,1)S(1)}, u32[]{:S(2)}, u32[]{:S(2)}) collective-permute-start(bf16[128,704]{1,0:T(8,128)(2,1)S(1)} %fusion.26.refs_0_), channel_id=1, source_target_pairs={{0,1},{1,0},{2,3},{3,2},{4,5},{5,4},{6,7},{7,6},{8,9},{9,8},{10,11... | collective-permute-start | bytes 540680 | tf_op jit(solution)/shard_map/ppermute | solution.py:345
  56.5 2.0 %collective-permute-start.8 = (bf16[128,704]{1,0:T(8,128)(2,1)S(1)}, bf16[128,704]{1,0:T(8,128)(2,1)S(1)}, u32[]{:S(2)}, u32[]{:S(2)}) collective-permute-start(bf16[128,704]{1,0:T(8,128)(2,1)S(1)} %collective-permute-done.refs_1_), channel_id=1, source_target_pairs={{0,1},{1,0},{2,3},{3,2},{4,5},{5,4},{6,7},{7,6},{8,9},{9,8},{10,11... | collective-permute-start | bytes 540680 | tf_op jit(solution)/shard_map/ppermute | solution.py:345
  59.6 4.6 %all-to-all-start.2 = ((bf16[16,64,256]{2,1,0:T(8,128)(2,1)}), bf16[16,64,256]{2,1,0:T(8,128)(2,1)S(1)}, u32[]{:S(2)}, u32[]{:S(2)}) async-start(bf16[16,64,256]{2,1,0:T(8,128)(2,1)} %reshape.383), calls=%async_computation.2 | async-start | bytes 1048576 | tf_op jit(solution)/shard_map/all_to_all | solution.py:343
  65.0 15.1 %attend.1 = (f32[128,2048]{1,0:T(8,128)}, bf16[2048,128]{1,0:T(8,128)(2,1)}) custom-call(s32[20]{0:T(128)} %concatenate.6.facts, bf16[128,704]{1,0:T(8,128)(2,1)} %copy-done.4, bf16[128,704]{1,0:T(8,128)(2,1)} %copy-done.12, bf16[128,704]{1,0:T(8,128)(2,1)} %copy-done.13, bf16[128,704]{1,0:T(8,128)(2,1)} %copy-done.8, bf16[128,704]{1,0:T(8,128)(2,1)} %copy-done.7, ...), custom_call_target="tpu_custom_call" | custom-call | flops 4831838208 | bytes 8388608 | tf_op jit(solution)/shard_map/attend/pallas_call | solution.py:348
  80.1 5.2 %all-to-all-start.1 = ((f32[8,16,2048]{2,1,0:T(8,128)}), f32[8,16,2048]{2,1,0:T(8,128)S(1)}, u32[]{:S(2)}, u32[]{:S(2)}) async-start(f32[8,16,2048]{2,1,0:T(8,128)} %bitcast.75), calls=%async_computation.1 | async-start | bytes 2097152 | tf_op jit(solution)/shard_map/all_to_all | solution.py:378
  85.4 1.7 %score.1 = f32[16,2048]{1,0:T(8,128)S(1)} custom-call(bf16[16,64,256]{2,1,0:T(8,128)(2,1)S(1)} %all-to-all-done.2.queries, bf16[2048,128]{1,0:T(8,128)(2,1)S(1)} %copy-done.2), custom_call_target="tpu_custom_call" | custom-call | flops 536870912 | bytes 1048576 | tf_op jit(solution)/shard_map/score/pallas_call | solution.py:381
  87.1 14.1 %all-to-all-done.1.target_parts = f32[8,16,2048]{2,1,0:T(8,128)S(1)} async-done(((f32[8,16,2048]{2,1,0:T(8,128)}), f32[8,16,2048]{2,1,0:T(8,128)S(1)}, u32[]{:S(2)}, u32[]{:S(2)}) %all-to-all-start.1) | async-done | bytes 1048608 | tf_op jit(solution)/shard_map/all_to_all | solution.py:378
  101.2 4.1 %key_grad.1 = (f32[64,2048]{1,0:T(8,128)S(1)}, f32[16,1]{1,0:T(8,128)S(1)}, bf16[16,128,128]{2,1,0:T(8,128)(2,1)}) custom-call(s32[20]{0:T(128)S(1)} %copy-done.1, f32[8,16,2048]{2,1,0:T(8,128)S(1)} %all-to-all-done.1.target_parts, f32[16,2048]{1,0:T(8,128)S(1)} %score.1, bf16[16,64,256]{2,1,0:T(8,128)(2,1)S(1)} %all-to-all-done.2.queries, ...), custom_call_target="tpu_custom_call" | custom-call | flops 1073741824 | bytes 4194304 | tf_op jit(solution)/shard_map/key_grad/pallas_call | solution.py:392
  105.3 4.2 %all-to-all-start.3 = ((bf16[16,128,128]{2,1,0:T(8,128)(2,1)}), bf16[16,128,128]{2,1,0:T(8,128)(2,1)S(1)}, u32[]{:S(2)}, u32[]{:S(2)}) async-start(bf16[16,128,128]{2,1,0:T(8,128)(2,1)} %get-tuple-element.45), calls=%async_computation.3 | async-start | bytes 1048576 | tf_op jit(solution)/shard_map/all_to_all | solution.py:421
  109.6 9.8 %all-to-all-done.3 = bf16[16,128,128]{2,1,0:T(8,128)(2,1)S(1)} async-done(((bf16[16,128,128]{2,1,0:T(8,128)(2,1)}), bf16[16,128,128]{2,1,0:T(8,128)(2,1)S(1)}, u32[]{:S(2)}, u32[]{:S(2)}) %all-to-all-start.3) | async-done | bytes 524320 | tf_op jit(solution)/shard_map/all_to_all | solution.py:421
  120.5 4.9 %all-to-all-start.4 = ((f32[16,24,128]{2,1,0:T(8,128)}), f32[16,24,128]{2,1,0:T(8,128)S(1)}, u32[]{:S(2)}, u32[]{:S(2)}) async-start(f32[16,24,128]{2,1,0:T(8,128)} %fusion.5), calls=%async_computation.4 | async-start | bytes 393216 | tf_op jit(solution)/shard_map/all_to_all | solution.py:426
  125.5 3.9 %query_grad.1 = f32[16,80,128]{2,1,0:T(8,128)} custom-call(f32[64,2048]{1,0:T(8,128)S(1)} %get-tuple-element.42.score_grad, f32[16,1]{1,0:T(8,128)S(1)} %get-tuple-element.43.loss, bf16[16,64,256]{2,1,0:T(8,128)(2,1)S(1)} %all-to-all-done.2.queries, bf16[2048,128]{1,0:T(8,128)(2,1)S(1)} %copy-done.2), custom_call_target="tpu_custom_call" | custom-call | flops 1073741824 | bytes 4194304 | tf_op jit(solution)/shard_map/query_grad/pallas_call | solution.py:409
  129.4 6.6 %all-to-all-done.4 = f32[16,24,128]{2,1,0:T(8,128)S(1)} async-done(((f32[16,24,128]{2,1,0:T(8,128)}), f32[16,24,128]{2,1,0:T(8,128)S(1)}, u32[]{:S(2)}, u32[]{:S(2)}) %all-to-all-start.4) | async-done | bytes 196640 | tf_op jit(solution)/shard_map/all_to_all | solution.py:426
  137.0 6.2 %all-to-all-start.5 = ((f32[16,80,128]{2,1,0:T(8,128)}), f32[16,80,128]{2,1,0:T(8,128)S(1)}, u32[]{:S(2)}, u32[]{:S(2)}) async-start(f32[16,80,128]{2,1,0:T(8,128)} %constant_dynamic-update-slice_fusion), calls=%async_computation.5 | async-start | bytes 1310720 | tf_op jit(solution)/shard_map/all_to_all | solution.py:436
  143.3 11.9 %all-to-all-done.5 = f32[16,80,128]{2,1,0:T(8,128)S(1)} async-done(((f32[16,80,128]{2,1,0:T(8,128)}), f32[16,80,128]{2,1,0:T(8,128)S(1)}, u32[]{:S(2)}, u32[]{:S(2)}) %all-to-all-start.5) | async-done | bytes 655392 | tf_op jit(solution)/shard_map/all_to_all | solution.py:436
  (123 shorter events, 21.2 us)
Async XLA Ops:
  0.6 26.6 %copy-start = (f32[256]{0:T(256)S(1)}, f32[256]{0:T(256)}, u32[]{:S(2)}) copy-start(f32[256]{0:T(256)} %param.13) | copy-start | bytes 3076
  4.6 30.3 %all-to-all-start = ((bf16[16,24,704]{2,1,0:T(8,128)(2,1)}), bf16[16,24,704]{2,1,0:T(8,128)(2,1)S(1)}, u32[]{:S(2)}, u32[]{:S(2)}) async-start(bf16[16,24,704]{2,1,0:T(8,128)(2,1)} %bitcast.74), calls=%async_computation | async-start | bytes 1179648 | tf_op jit(solution)/shard_map/all_to_all | solution.py:281
  17.9 26.1 %collective-permute-start.15 = (bf16[8,576,128]{2,1,0:T(8,128)(2,1)S(1)}, bf16[8,576,128]{2,1,0:T(8,128)(2,1)}, u32[]{:S(2)}, u32[]{:S(2)}) collective-permute-start(bf16[8,576,128]{2,1,0:T(8,128)(2,1)S(1)} %dynamic-slice_bitcast_fusion), channel_id=1, source_target_pairs={{0,1},{1,0},{2,3},{3,2},{4,5},{5,4},{6,7},{7,6},{8,9},{9,8},{10,11... | collective-permute-start | bytes 3538952 | tf_op jit(solution)/shard_map/ppermute | solution.py:285
  35.1 29.2 %copy-start.4 = (bf16[128,704]{1,0:T(8,128)(2,1)}, bf16[128,704]{1,0:T(8,128)(2,1)S(1)}, u32[]{:S(2)}) copy-start(bf16[128,704]{1,0:T(8,128)(2,1)S(1)} %fusion.26.refs_0_) | copy-start | bytes 540676
  35.1 4.6 %collective-permute-start.3 = (bf16[128,704]{1,0:T(8,128)(2,1)S(1)}, bf16[128,704]{1,0:T(8,128)(2,1)S(1)}, u32[]{:S(2)}, u32[]{:S(2)}) collective-permute-start(bf16[128,704]{1,0:T(8,128)(2,1)S(1)} %fusion.26.refs_0_), channel_id=1, source_target_pairs={{0,8},{8,0},{1,9},{9,1},{2,10},{10,2},{3,11},{11,3},{4,12},{12,4},... | collective-permute-start | bytes 540680 | tf_op jit(solution)/shard_map/ppermute | solution.py:339
  35.6 8.7 %collective-permute-start.2 = (bf16[128,704]{1,0:T(8,128)(2,1)S(1)}, bf16[128,704]{1,0:T(8,128)(2,1)S(1)}, u32[]{:S(2)}, u32[]{:S(2)}) collective-permute-start(bf16[128,704]{1,0:T(8,128)(2,1)S(1)} %fusion.26.refs_0_), channel_id=1, source_target_pairs={{0,4},{2,6},{4,0},{6,2},{1,5},{3,7},{5,1},{7,3},{8,12},{10,14},{12... | collective-permute-start | bytes 540680 | tf_op jit(solution)/shard_map/ppermute | solution.py:269
  39.7 7.6 %collective-permute-start.4 = (bf16[128,704]{1,0:T(8,128)(2,1)S(1)}, bf16[128,704]{1,0:T(8,128)(2,1)S(1)}, u32[]{:S(2)}, u32[]{:S(2)}) collective-permute-start(bf16[128,704]{1,0:T(8,128)(2,1)S(1)} %collective-permute-done.3.refs_4_), channel_id=1, source_target_pairs={{0,2},{2,4},{4,6},{6,0},{1,3},{3,5},{5,7},{7,1},{8,10},{10,12},{12... | collective-permute-start | bytes 540680 | tf_op jit(solution)/shard_map/ppermute | solution.py:269
  41.0 13.9 %collective-permute-start.5 = (bf16[128,704]{1,0:T(8,128)(2,1)S(1)}, bf16[128,704]{1,0:T(8,128)(2,1)S(1)}, u32[]{:S(2)}, u32[]{:S(2)}) collective-permute-start(bf16[128,704]{1,0:T(8,128)(2,1)S(1)} %collective-permute-done.3.refs_4_), channel_id=1, source_target_pairs={{0,6},{2,0},{4,2},{6,4},{1,7},{3,1},{5,3},{7,5},{8,14},{10,8},{12,... | collective-permute-start | bytes 540680 | tf_op jit(solution)/shard_map/ppermute | solution.py:269
  42.4 12.8 %collective-permute-start.6 = (bf16[128,704]{1,0:T(8,128)(2,1)S(1)}, bf16[128,704]{1,0:T(8,128)(2,1)S(1)}, u32[]{:S(2)}, u32[]{:S(2)}) collective-permute-start(bf16[128,704]{1,0:T(8,128)(2,1)S(1)} %collective-permute-done.3.refs_4_), channel_id=1, source_target_pairs={{0,4},{2,6},{4,0},{6,2},{1,5},{3,7},{5,1},{7,3},{8,12},{10,14},{12... | collective-permute-start | bytes 540680 | tf_op jit(solution)/shard_map/ppermute | solution.py:269
  44.0 12.6 %collective-permute-start = (bf16[128,704]{1,0:T(8,128)(2,1)S(1)}, bf16[128,704]{1,0:T(8,128)(2,1)S(1)}, u32[]{:S(2)}, u32[]{:S(2)}) collective-permute-start(bf16[128,704]{1,0:T(8,128)(2,1)S(1)} %fusion.26.refs_0_), channel_id=1, source_target_pairs={{0,2},{2,4},{4,6},{6,0},{1,3},{3,5},{5,7},{7,1},{8,10},{10,12},{12... | collective-permute-start | bytes 540680 | tf_op jit(solution)/shard_map/ppermute | solution.py:269
  44.3 14.3 %collective-permute-start.1 = (bf16[128,704]{1,0:T(8,128)(2,1)S(1)}, bf16[128,704]{1,0:T(8,128)(2,1)S(1)}, u32[]{:S(2)}, u32[]{:S(2)}) collective-permute-start(bf16[128,704]{1,0:T(8,128)(2,1)S(1)} %fusion.26.refs_0_), channel_id=1, source_target_pairs={{0,6},{2,0},{4,2},{6,4},{1,7},{3,1},{5,3},{7,5},{8,14},{10,8},{12,... | collective-permute-start | bytes 540680 | tf_op jit(solution)/shard_map/ppermute | solution.py:269
  47.3 11.3 %collective-permute-start.7 = (bf16[128,704]{1,0:T(8,128)(2,1)S(1)}, bf16[128,704]{1,0:T(8,128)(2,1)S(1)}, u32[]{:S(2)}, u32[]{:S(2)}) collective-permute-start(bf16[128,704]{1,0:T(8,128)(2,1)S(1)} %fusion.26.refs_0_), channel_id=1, source_target_pairs={{0,1},{1,0},{2,3},{3,2},{4,5},{5,4},{6,7},{7,6},{8,9},{9,8},{10,11... | collective-permute-start | bytes 540680 | tf_op jit(solution)/shard_map/ppermute | solution.py:345
  54.9 4.2 %collective-permute-start.10 = (bf16[128,704]{1,0:T(8,128)(2,1)S(1)}, bf16[128,704]{1,0:T(8,128)(2,1)S(1)}, u32[]{:S(2)}, u32[]{:S(2)}) collective-permute-start(bf16[128,704]{1,0:T(8,128)(2,1)S(1)} %collective-permute-done.2.refs_3_), channel_id=1, source_target_pairs={{0,1},{1,0},{2,3},{3,2},{4,5},{5,4},{6,7},{7,6},{8,9},{9,8},{10,11... | collective-permute-start | bytes 540680 | tf_op jit(solution)/shard_map/ppermute | solution.py:345
  55.2 4.0 %collective-permute-start.11 = (bf16[128,704]{1,0:T(8,128)(2,1)S(1)}, bf16[128,704]{1,0:T(8,128)(2,1)S(1)}, u32[]{:S(2)}, u32[]{:S(2)}) collective-permute-start(bf16[128,704]{1,0:T(8,128)(2,1)S(1)} %collective-permute-done.3.refs_4_), channel_id=1, source_target_pairs={{0,1},{1,0},{2,3},{3,2},{4,5},{5,4},{6,7},{7,6},{8,9},{9,8},{10,11... | collective-permute-start | bytes 540680 | tf_op jit(solution)/shard_map/ppermute | solution.py:345
  56.5 7.7 %collective-permute-start.8 = (bf16[128,704]{1,0:T(8,128)(2,1)S(1)}, bf16[128,704]{1,0:T(8,128)(2,1)S(1)}, u32[]{:S(2)}, u32[]{:S(2)}) collective-permute-start(bf16[128,704]{1,0:T(8,128)(2,1)S(1)} %collective-permute-done.refs_1_), channel_id=1, source_target_pairs={{0,1},{1,0},{2,3},{3,2},{4,5},{5,4},{6,7},{7,6},{8,9},{9,8},{10,11... | collective-permute-start | bytes 540680 | tf_op jit(solution)/shard_map/ppermute | solution.py:345
  58.5 5.7 %collective-permute-start.9 = (bf16[128,704]{1,0:T(8,128)(2,1)S(1)}, bf16[128,704]{1,0:T(8,128)(2,1)S(1)}, u32[]{:S(2)}, u32[]{:S(2)}) collective-permute-start(bf16[128,704]{1,0:T(8,128)(2,1)S(1)} %collective-permute-done.1.refs_2_), channel_id=1, source_target_pairs={{0,1},{1,0},{2,3},{3,2},{4,5},{5,4},{6,7},{7,6},{8,9},{9,8},{10,11... | collective-permute-start | bytes 540680 | tf_op jit(solution)/shard_map/ppermute | solution.py:345
  58.6 5.6 %collective-permute-start.12 = (bf16[128,704]{1,0:T(8,128)(2,1)S(1)}, bf16[128,704]{1,0:T(8,128)(2,1)}, u32[]{:S(2)}, u32[]{:S(2)}) collective-permute-start(bf16[128,704]{1,0:T(8,128)(2,1)S(1)} %collective-permute-done.4.refs_5_), channel_id=1, source_target_pairs={{0,1},{1,0},{2,3},{3,2},{4,5},{5,4},{6,7},{7,6},{8,9},{9,8},{10,11... | collective-permute-start | bytes 540680 | tf_op jit(solution)/shard_map/ppermute | solution.py:345
  59.1 5.2 %collective-permute-start.13 = (bf16[128,704]{1,0:T(8,128)(2,1)S(1)}, bf16[128,704]{1,0:T(8,128)(2,1)}, u32[]{:S(2)}, u32[]{:S(2)}) collective-permute-start(bf16[128,704]{1,0:T(8,128)(2,1)S(1)} %collective-permute-done.5.refs_6_), channel_id=1, source_target_pairs={{0,1},{1,0},{2,3},{3,2},{4,5},{5,4},{6,7},{7,6},{8,9},{9,8},{10,11... | collective-permute-start | bytes 540680 | tf_op jit(solution)/shard_map/ppermute | solution.py:345
  59.2 5.1 %collective-permute-start.14 = (bf16[128,704]{1,0:T(8,128)(2,1)S(1)}, bf16[128,704]{1,0:T(8,128)(2,1)}, u32[]{:S(2)}, u32[]{:S(2)}) collective-permute-start(bf16[128,704]{1,0:T(8,128)(2,1)S(1)} %collective-permute-done.6.refs_7_), channel_id=1, source_target_pairs={{0,1},{1,0},{2,3},{3,2},{4,5},{5,4},{6,7},{7,6},{8,9},{9,8},{10,11... | collective-permute-start | bytes 540680 | tf_op jit(solution)/shard_map/ppermute | solution.py:345
  59.6 20.5 %all-to-all-start.2 = ((bf16[16,64,256]{2,1,0:T(8,128)(2,1)}), bf16[16,64,256]{2,1,0:T(8,128)(2,1)S(1)}, u32[]{:S(2)}, u32[]{:S(2)}) async-start(bf16[16,64,256]{2,1,0:T(8,128)(2,1)} %reshape.383), calls=%async_computation.2 | async-start | bytes 1048576 | tf_op jit(solution)/shard_map/all_to_all | solution.py:343
  80.1 21.1 %all-to-all-start.1 = ((f32[8,16,2048]{2,1,0:T(8,128)}), f32[8,16,2048]{2,1,0:T(8,128)S(1)}, u32[]{:S(2)}, u32[]{:S(2)}) async-start(f32[8,16,2048]{2,1,0:T(8,128)} %bitcast.75), calls=%async_computation.1 | async-start | bytes 2097152 | tf_op jit(solution)/shard_map/all_to_all | solution.py:378
  105.3 14.2 %all-to-all-start.3 = ((bf16[16,128,128]{2,1,0:T(8,128)(2,1)}), bf16[16,128,128]{2,1,0:T(8,128)(2,1)S(1)}, u32[]{:S(2)}, u32[]{:S(2)}) async-start(bf16[16,128,128]{2,1,0:T(8,128)(2,1)} %get-tuple-element.45), calls=%async_computation.3 | async-start | bytes 1048576 | tf_op jit(solution)/shard_map/all_to_all | solution.py:421
  120.5 15.4 %all-to-all-start.4 = ((f32[16,24,128]{2,1,0:T(8,128)}), f32[16,24,128]{2,1,0:T(8,128)S(1)}, u32[]{:S(2)}, u32[]{:S(2)}) async-start(f32[16,24,128]{2,1,0:T(8,128)} %fusion.5), calls=%async_computation.4 | async-start | bytes 393216 | tf_op jit(solution)/shard_map/all_to_all | solution.py:426
  137.0 18.2 %all-to-all-start.5 = ((f32[16,80,128]{2,1,0:T(8,128)}), f32[16,80,128]{2,1,0:T(8,128)S(1)}, u32[]{:S(2)}, u32[]{:S(2)}) async-start(f32[16,80,128]{2,1,0:T(8,128)} %constant_dynamic-update-slice_fusion), calls=%async_computation.5 | async-start | bytes 1310720 | tf_op jit(solution)/shard_map/all_to_all | solution.py:436
  (17 other events, 157.3 us)

commit v4 on v3

--- a/solution.py
+++ b/solution.py
@@ -30,8 +30,8 @@
     return key_pos <= rows + query_first
 
 
-def stripes_kernel(where, selection, index_key, key_latent, send):
-    ctx, lane = where[0], where[1]
+def stripes_kernel(selection, index_key, key_latent, send):
+    ctx, lane = lax.axis_index(CTX), lax.axis_index(HEAD)
     rows, (blocks, slots) = send.shape[0], selection.shape
     per_block = OWNER_MOST * STRIPE
     tiles = index_key.shape[0] // TILE
@@ -270,11 +270,11 @@
 
     send = pl.pallas_call(
         stripes_kernel,
-        in_specs=[smem, vmem, vmem, vmem],
+        in_specs=[vmem] * 3,
         out_shape=jax.ShapeDtypeStruct((ctx_count * OWNER_MOST * STRIPE, width), bf16),
         compiler_params=params,
         name="stripes",
-    )(jnp.stack([ctx_index, lane]).astype(jnp.int32), selection, index_key, key_latent.T)
+    )(selection, index_key, key_latent.T)
     send, index_query, index_weight, main_query = lax.optimization_barrier(
         (send, index_query, index_weight, main_query)
     )
@@ -417,15 +417,14 @@
         name="query_grad",
     )(score_grad, loss, iq, index_keys)
 
-    exact = lax.Precision.HIGHEST
     key_sum = lax.all_to_all(key_part, HEAD, 0, 0, tiled=True)
     key_sum = jnp.sum(key_sum.astype(f32), axis=0)
     back = lax.dot_general(
-        got_rows.astype(f32), key_sum, (((0,), (1,)), ((), ())), precision=exact
+        got_rows, key_sum.astype(bf16), (((0,), (1,)), ((), ())), preferred_element_type=bf16
     )
     back = lax.all_to_all(back, CTX, 0, 0, tiled=True)
     own_blocks = lax.dot_general(
-        sent_rows.astype(f32), back, (((0,), (0,)), ((), ())), precision=exact
+        sent_rows, back, (((0,), (0,)), ((), ())), preferred_element_type=f32
     ).reshape(key_tiles, STRIPE, idx_width)
     order = jnp.arange(lanes)
     natural = order % (lanes // 2) * 2 + order // (lanes // 2)

time: 159 us -> 157 us (0.987)
  no operation moved by 1% of the time
where the time goes in v4:
time: 157 us
  starting transfers between devices  60 us (38%)
  waiting for transfers between devices  51.4 us (33%)
  Pallas kernels  28.4 us (18%)
  local copies, waits for them, and re-layouts  10.5 us (7%)
  other arithmetic  3.81 us (2%)
    pallas_call x1, Pallas kernels, body(): pl.pallas_call(attend_kernel, grid_spec=pltpu.PrefetchScalarGridSpec(num_...  15.1 us
    all_to_all x1, waiting for transfers between devices, body(): target_parts = lax.all_to_all(target_part, ('yl', 'x'), 0, 0, tiled=True)  14.1 us
    ppermute x8, starting transfers between devices, body(): pieces += [lax.ppermute(piece, 'core', swap) for piece in pieces]  12.2 us
    all_to_all x1, waiting for transfers between devices, body(): packed = lax.all_to_all(packed, ROWS, 0, 0, tiled=True)  11.9 us
    all_to_all x1, starting transfers between devices, body(): arrived = lax.all_to_all(send, CTX, 0, 0, tiled=True)  11.9 us
    all_to_all x1, waiting for transfers between devices, body(): key_sum = lax.all_to_all(key_part, HEAD, 0, 0, tiled=True)  9.83 us
    ppermute x6, starting transfers between devices, shifted(): return lax.ppermute(value, 'x', ring)  9.64 us
    all_to_all x1, waiting for transfers between devices, body(): arrived = lax.all_to_all(send, CTX, 0, 0, tiled=True)  7.85 us
  transfers between devices with their start and end apart: 22, of which 7 were waited for; matrix products, arithmetic and copies ran while one was open for 6% of the time, Pallas kernels for 13%

profile of v4, /device:TPU:1, one launch (start us, length us, event | category | flops | bytes accessed | tf_op | source)
XLA Modules:
  0.0 156.5 jit_solution(3602430309962883680)
XLA Ops:
  0.7 3.4 %stripes.1 = bf16[384,704]{1,0:T(8,128)(2,1)} custom-call(s32[16,16]{1,0:T(8,128)} %selection.1, bf16[768,128]{1,0:T(8,128)(2,1)} %index_key.1, bf16[576,768]{1,0:T(8,128)(2,1)} %bitcast.75), custom_call_target="tpu_custom_call" | custom-call | tf_op jit(solution)/shard_map/stripes/pallas_call | solution.py:271
  4.1 11.9 %all-to-all-start = ((bf16[16,24,704]{2,1,0:T(8,128)(2,1)}), bf16[16,24,704]{2,1,0:T(8,128)(2,1)S(1)}, u32[]{:S(2)}, u32[]{:S(2)}) async-start(bf16[16,24,704]{2,1,0:T(8,128)(2,1)} %bitcast.71), calls=%async_computation | async-start | bytes 1179648 | tf_op jit(solution)/shard_map/all_to_all | solution.py:281
  20.3 1.8 %mul.164 = bf16[128,384]{1,0:T(8,128)(2,1)S(1)} reshape(bf16[16,8,48,8]{3,2,1,0:T(8,128)(2,1)S(1)} %broadcast_multiply_fusion) | data formatting | bytes 196608 | tf_op jit(solution)/shard_map/mul | solution.py:240
  26.6 7.8 %all-to-all-done = bf16[16,24,704]{2,1,0:T(8,128)(2,1)S(1)} async-done(((bf16[16,24,704]{2,1,0:T(8,128)(2,1)}), bf16[16,24,704]{2,1,0:T(8,128)(2,1)S(1)}, u32[]{:S(2)}, u32[]{:S(2)}) %all-to-all-start) | async-done | bytes 540704 | tf_op jit(solution)/shard_map/all_to_all | solution.py:281
  35.2 2.7 %collective-permute-start.2 = (bf16[128,704]{1,0:T(8,128)(2,1)S(1)}, bf16[128,704]{1,0:T(8,128)(2,1)S(1)}, u32[]{:S(2)}, u32[]{:S(2)}) collective-permute-start(bf16[128,704]{1,0:T(8,128)(2,1)S(1)} %fusion.26.refs_0_), channel_id=1, source_target_pairs={{0,4},{2,6},{4,0},{6,2},{1,5},{3,7},{5,1},{7,3},{8,12},{10,14},{12... | collective-permute-start | bytes 540680 | tf_op jit(solution)/shard_map/ppermute | solution.py:269
  40.5 1.5 collective-permute-start.5
  42.0 1.5 collective-permute-start.6
  43.8 2.4 %collective-permute-start.1 = (bf16[128,704]{1,0:T(8,128)(2,1)S(1)}, bf16[128,704]{1,0:T(8,128)(2,1)S(1)}, u32[]{:S(2)}, u32[]{:S(2)}) collective-permute-start(bf16[128,704]{1,0:T(8,128)(2,1)S(1)} %fusion.26.refs_0_), channel_id=1, source_target_pairs={{0,6},{2,0},{4,2},{6,4},{1,7},{3,1},{5,3},{7,5},{8,14},{10,8},{12,... | collective-permute-start | bytes 540680 | tf_op jit(solution)/shard_map/ppermute | solution.py:269
  46.9 7.6 %collective-permute-start.7 = (bf16[128,704]{1,0:T(8,128)(2,1)S(1)}, bf16[128,704]{1,0:T(8,128)(2,1)S(1)}, u32[]{:S(2)}, u32[]{:S(2)}) collective-permute-start(bf16[128,704]{1,0:T(8,128)(2,1)S(1)} %fusion.26.refs_0_), channel_id=1, source_target_pairs={{0,1},{1,0},{2,3},{3,2},{4,5},{5,4},{6,7},{7,6},{8,9},{9,8},{10,11... | collective-permute-start | bytes 540680 | tf_op jit(solution)/shard_map/ppermute | solution.py:345
  54.5 1.5 collective-permute-start.11
  56.1 2.0 %collective-permute-start.8 = (bf16[128,704]{1,0:T(8,128)(2,1)S(1)}, bf16[128,704]{1,0:T(8,128)(2,1)S(1)}, u32[]{:S(2)}, u32[]{:S(2)}) collective-permute-start(bf16[128,704]{1,0:T(8,128)(2,1)S(1)} %collective-permute-done.refs_1_), channel_id=1, source_target_pairs={{0,1},{1,0},{2,3},{3,2},{4,5},{5,4},{6,7},{7,6},{8,9},{9,8},{10,11... | collective-permute-start | bytes 540680 | tf_op jit(solution)/shard_map/ppermute | solution.py:345
  59.1 4.6 %all-to-all-start.2 = ((bf16[16,64,256]{2,1,0:T(8,128)(2,1)}), bf16[16,64,256]{2,1,0:T(8,128)(2,1)S(1)}, u32[]{:S(2)}, u32[]{:S(2)}) async-start(bf16[16,64,256]{2,1,0:T(8,128)(2,1)} %reshape.383), calls=%async_computation.2 | async-start | bytes 1048576 | tf_op jit(solution)/shard_map/all_to_all | solution.py:343
  64.4 15.1 %attend.1 = (f32[128,2048]{1,0:T(8,128)}, bf16[2048,128]{1,0:T(8,128)(2,1)}) custom-call(s32[20]{0:T(128)} %concatenate.6.facts, bf16[128,704]{1,0:T(8,128)(2,1)} %copy-done.5, bf16[128,704]{1,0:T(8,128)(2,1)} %copy-done.13, bf16[128,704]{1,0:T(8,128)(2,1)} %copy-done.14, bf16[128,704]{1,0:T(8,128)(2,1)} %copy-done.9, bf16[128,704]{1,0:T(8,128)(2,1)} %copy-done.8, ...), custom_call_target="tpu_custom_call" | custom-call | flops 4831838208 | bytes 8388608 | tf_op jit(solution)/shard_map/attend/pallas_call | solution.py:348
  79.6 5.2 %all-to-all-start.1 = ((f32[8,16,2048]{2,1,0:T(8,128)}), f32[8,16,2048]{2,1,0:T(8,128)S(1)}, u32[]{:S(2)}, u32[]{:S(2)}) async-start(f32[8,16,2048]{2,1,0:T(8,128)} %bitcast.73), calls=%async_computation.1 | async-start | bytes 2097152 | tf_op jit(solution)/shard_map/all_to_all | solution.py:378
  84.9 1.7 %score.1 = f32[16,2048]{1,0:T(8,128)S(1)} custom-call(bf16[16,64,256]{2,1,0:T(8,128)(2,1)S(1)} %all-to-all-done.2.queries, bf16[2048,128]{1,0:T(8,128)(2,1)S(1)} %copy-done.2), custom_call_target="tpu_custom_call" | custom-call | flops 536870912 | bytes 1048576 | tf_op jit(solution)/shard_map/score/pallas_call | solution.py:381
  86.6 14.1 %all-to-all-done.1.target_parts = f32[8,16,2048]{2,1,0:T(8,128)S(1)} async-done(((f32[8,16,2048]{2,1,0:T(8,128)}), f32[8,16,2048]{2,1,0:T(8,128)S(1)}, u32[]{:S(2)}, u32[]{:S(2)}) %all-to-all-start.1) | async-done | bytes 1048608 | tf_op jit(solution)/shard_map/all_to_all | solution.py:378
  100.7 4.2 %key_grad.1 = (f32[64,2048]{1,0:T(8,128)S(1)}, f32[16,1]{1,0:T(8,128)S(1)}, bf16[16,128,128]{2,1,0:T(8,128)(2,1)}) custom-call(s32[20]{0:T(128)S(1)} %copy-done.1, f32[8,16,2048]{2,1,0:T(8,128)S(1)} %all-to-all-done.1.target_parts, f32[16,2048]{1,0:T(8,128)S(1)} %score.1, bf16[16,64,256]{2,1,0:T(8,128)(2,1)S(1)} %all-to-all-done.2.queries, ...), custom_call_target="tpu_custom_call" | custom-call | flops 1073741824 | bytes 4194304 | tf_op jit(solution)/shard_map/key_grad/pallas_call | solution.py:392
  104.8 4.2 %all-to-all-start.3 = ((bf16[16,128,128]{2,1,0:T(8,128)(2,1)}), bf16[16,128,128]{2,1,0:T(8,128)(2,1)S(1)}, u32[]{:S(2)}, u32[]{:S(2)}) async-start(bf16[16,128,128]{2,1,0:T(8,128)(2,1)} %get-tuple-element.45), calls=%async_computation.3 | async-start | bytes 1048576 | tf_op jit(solution)/shard_map/all_to_all | solution.py:420
  109.2 9.8 %all-to-all-done.3 = bf16[16,128,128]{2,1,0:T(8,128)(2,1)S(1)} async-done(((bf16[16,128,128]{2,1,0:T(8,128)(2,1)}), bf16[16,128,128]{2,1,0:T(8,128)(2,1)S(1)}, u32[]{:S(2)}, u32[]{:S(2)}) %all-to-all-start.3) | async-done | bytes 524320 | tf_op jit(solution)/shard_map/all_to_all | solution.py:420
  119.9 4.9 %all-to-all-start.4 = ((bf16[16,24,128]{2,1,0:T(8,128)(2,1)}), bf16[16,24,128]{2,1,0:T(8,128)(2,1)S(1)}, u32[]{:S(2)}, u32[]{:S(2)}) async-start(bf16[16,24,128]{2,1,0:T(8,128)(2,1)} %fusion.7), calls=%async_computation.4 | async-start | bytes 196608 | tf_op jit(solution)/shard_map/all_to_all | solution.py:425
  124.9 4.0 %query_grad.1 = f32[16,80,128]{2,1,0:T(8,128)} custom-call(f32[64,2048]{1,0:T(8,128)S(1)} %get-tuple-element.42.score_grad, f32[16,1]{1,0:T(8,128)S(1)} %get-tuple-element.43.loss, bf16[16,64,256]{2,1,0:T(8,128)(2,1)S(1)} %all-to-all-done.2.queries, bf16[2048,128]{1,0:T(8,128)(2,1)S(1)} %copy-done.2), custom_call_target="tpu_custom_call" | custom-call | flops 1073741824 | bytes 4194304 | tf_op jit(solution)/shard_map/query_grad/pallas_call | solution.py:409
  128.8 5.6 %all-to-all-done.4 = bf16[16,24,128]{2,1,0:T(8,128)(2,1)S(1)} async-done(((bf16[16,24,128]{2,1,0:T(8,128)(2,1)}), bf16[16,24,128]{2,1,0:T(8,128)(2,1)S(1)}, u32[]{:S(2)}, u32[]{:S(2)}) %all-to-all-start.4) | async-done | bytes 98336 | tf_op jit(solution)/shard_map/all_to_all | solution.py:425
  135.5 5.9 %all-to-all-start.5 = ((f32[16,80,128]{2,1,0:T(8,128)}), f32[16,80,128]{2,1,0:T(8,128)S(1)}, u32[]{:S(2)}, u32[]{:S(2)}) async-start(f32[16,80,128]{2,1,0:T(8,128)} %constant_dynamic-update-slice_fusion), calls=%async_computation.5 | async-start | bytes 1310720 | tf_op jit(solution)/shard_map/all_to_all | solution.py:435
  141.5 11.9 %all-to-all-done.5 = f32[16,80,128]{2,1,0:T(8,128)S(1)} async-done(((f32[16,80,128]{2,1,0:T(8,128)}), f32[16,80,128]{2,1,0:T(8,128)S(1)}, u32[]{:S(2)}, u32[]{:S(2)}) %all-to-all-start.5) | async-done | bytes 655392 | tf_op jit(solution)/shard_map/all_to_all | solution.py:435
  (122 shorter events, 20.0 us)
Async XLA Ops:
  0.6 25.9 %copy-start = (f32[256]{0:T(256)S(1)}, f32[256]{0:T(256)}, u32[]{:S(2)}) copy-start(f32[256]{0:T(256)} %param.13) | copy-start | bytes 3076
  4.1 30.3 %all-to-all-start = ((bf16[16,24,704]{2,1,0:T(8,128)(2,1)}), bf16[16,24,704]{2,1,0:T(8,128)(2,1)S(1)}, u32[]{:S(2)}, u32[]{:S(2)}) async-start(bf16[16,24,704]{2,1,0:T(8,128)(2,1)} %bitcast.71), calls=%async_computation | async-start | bytes 1179648 | tf_op jit(solution)/shard_map/all_to_all | solution.py:281
  17.2 26.3 %collective-permute-start.15 = (bf16[8,576,128]{2,1,0:T(8,128)(2,1)}, bf16[8,576,128]{2,1,0:T(8,128)(2,1)}, u32[]{:S(2)}, u32[]{:S(2)}) collective-permute-start(bf16[8,576,128]{2,1,0:T(8,128)(2,1)} %dynamic-slice_bitcast_fusion), channel_id=1, source_target_pairs={{0,1},{1,0},{2,3},{3,2},{4,5},{5,4},{6,7},{7,6},{8,9},{9,8},{10,11... | collective-permute-start | bytes 3538952 | tf_op jit(solution)/shard_map/ppermute | solution.py:285
  34.7 29.1 %copy-start.5 = (bf16[128,704]{1,0:T(8,128)(2,1)}, bf16[128,704]{1,0:T(8,128)(2,1)S(1)}, u32[]{:S(2)}) copy-start(bf16[128,704]{1,0:T(8,128)(2,1)S(1)} %fusion.26.refs_0_) | copy-start | bytes 540676
  34.7 4.6 %collective-permute-start.3 = (bf16[128,704]{1,0:T(8,128)(2,1)S(1)}, bf16[128,704]{1,0:T(8,128)(2,1)S(1)}, u32[]{:S(2)}, u32[]{:S(2)}) collective-permute-start(bf16[128,704]{1,0:T(8,128)(2,1)S(1)} %fusion.26.refs_0_), channel_id=1, source_target_pairs={{0,8},{8,0},{1,9},{9,1},{2,10},{10,2},{3,11},{11,3},{4,12},{12,4},... | collective-permute-start | bytes 540680 | tf_op jit(solution)/shard_map/ppermute | solution.py:339
  35.2 8.7 %collective-permute-start.2 = (bf16[128,704]{1,0:T(8,128)(2,1)S(1)}, bf16[128,704]{1,0:T(8,128)(2,1)S(1)}, u32[]{:S(2)}, u32[]{:S(2)}) collective-permute-start(bf16[128,704]{1,0:T(8,128)(2,1)S(1)} %fusion.26.refs_0_), channel_id=1, source_target_pairs={{0,4},{2,6},{4,0},{6,2},{1,5},{3,7},{5,1},{7,3},{8,12},{10,14},{12... | collective-permute-start | bytes 540680 | tf_op jit(solution)/shard_map/ppermute | solution.py:269
  39.3 7.6 %collective-permute-start.4 = (bf16[128,704]{1,0:T(8,128)(2,1)S(1)}, bf16[128,704]{1,0:T(8,128)(2,1)S(1)}, u32[]{:S(2)}, u32[]{:S(2)}) collective-permute-start(bf16[128,704]{1,0:T(8,128)(2,1)S(1)} %collective-permute-done.3.refs_4_), channel_id=1, source_target_pairs={{0,2},{2,4},{4,6},{6,0},{1,3},{3,5},{5,7},{7,1},{8,10},{10,12},{12... | collective-permute-start | bytes 540680 | tf_op jit(solution)/shard_map/ppermute | solution.py:269
  40.5 13.9 %collective-permute-start.5 = (bf16[128,704]{1,0:T(8,128)(2,1)S(1)}, bf16[128,704]{1,0:T(8,128)(2,1)S(1)}, u32[]{:S(2)}, u32[]{:S(2)}) collective-permute-start(bf16[128,704]{1,0:T(8,128)(2,1)S(1)} %collective-permute-done.3.refs_4_), channel_id=1, source_target_pairs={{0,6},{2,0},{4,2},{6,4},{1,7},{3,1},{5,3},{7,5},{8,14},{10,8},{12,... | collective-permute-start | bytes 540680 | tf_op jit(solution)/shard_map/ppermute | solution.py:269
  42.0 12.6 %collective-permute-start.6 = (bf16[128,704]{1,0:T(8,128)(2,1)S(1)}, bf16[128,704]{1,0:T(8,128)(2,1)S(1)}, u32[]{:S(2)}, u32[]{:S(2)}) collective-permute-start(bf16[128,704]{1,0:T(8,128)(2,1)S(1)} %collective-permute-done.3.refs_4_), channel_id=1, source_target_pairs={{0,4},{2,6},{4,0},{6,2},{1,5},{3,7},{5,1},{7,3},{8,12},{10,14},{12... | collective-permute-start | bytes 540680 | tf_op jit(solution)/shard_map/ppermute | solution.py:269
  43.5 12.6 %collective-permute-start = (bf16[128,704]{1,0:T(8,128)(2,1)S(1)}, bf16[128,704]{1,0:T(8,128)(2,1)S(1)}, u32[]{:S(2)}, u32[]{:S(2)}) collective-permute-start(bf16[128,704]{1,0:T(8,128)(2,1)S(1)} %fusion.26.refs_0_), channel_id=1, source_target_pairs={{0,2},{2,4},{4,6},{6,0},{1,3},{3,5},{5,7},{7,1},{8,10},{10,12},{12... | collective-permute-start | bytes 540680 | tf_op jit(solution)/shard_map/ppermute | solution.py:269
  43.8 14.3 %collective-permute-start.1 = (bf16[128,704]{1,0:T(8,128)(2,1)S(1)}, bf16[128,704]{1,0:T(8,128)(2,1)S(1)}, u32[]{:S(2)}, u32[]{:S(2)}) collective-permute-start(bf16[128,704]{1,0:T(8,128)(2,1)S(1)} %fusion.26.refs_0_), channel_id=1, source_target_pairs={{0,6},{2,0},{4,2},{6,4},{1,7},{3,1},{5,3},{7,5},{8,14},{10,8},{12,... | collective-permute-start | bytes 540680 | tf_op jit(solution)/shard_map/ppermute | solution.py:269
  46.9 11.3 %collective-permute-start.7 = (bf16[128,704]{1,0:T(8,128)(2,1)S(1)}, bf16[128,704]{1,0:T(8,128)(2,1)S(1)}, u32[]{:S(2)}, u32[]{:S(2)}) collective-permute-start(bf16[128,704]{1,0:T(8,128)(2,1)S(1)} %fusion.26.refs_0_), channel_id=1, source_target_pairs={{0,1},{1,0},{2,3},{3,2},{4,5},{5,4},{6,7},{7,6},{8,9},{9,8},{10,11... | collective-permute-start | bytes 540680 | tf_op jit(solution)/shard_map/ppermute | solution.py:345
  54.4 4.2 %collective-permute-start.10 = (bf16[128,704]{1,0:T(8,128)(2,1)S(1)}, bf16[128,704]{1,0:T(8,128)(2,1)S(1)}, u32[]{:S(2)}, u32[]{:S(2)}) collective-permute-start(bf16[128,704]{1,0:T(8,128)(2,1)S(1)} %collective-permute-done.2.refs_3_), channel_id=1, source_target_pairs={{0,1},{1,0},{2,3},{3,2},{4,5},{5,4},{6,7},{7,6},{8,9},{9,8},{10,11... | collective-permute-start | bytes 540680 | tf_op jit(solution)/shard_map/ppermute | solution.py:345
  54.5 4.2 %collective-permute-start.11 = (bf16[128,704]{1,0:T(8,128)(2,1)S(1)}, bf16[128,704]{1,0:T(8,128)(2,1)S(1)}, u32[]{:S(2)}, u32[]{:S(2)}) collective-permute-start(bf16[128,704]{1,0:T(8,128)(2,1)S(1)} %collective-permute-done.3.refs_4_), channel_id=1, source_target_pairs={{0,1},{1,0},{2,3},{3,2},{4,5},{5,4},{6,7},{7,6},{8,9},{9,8},{10,11... | collective-permute-start | bytes 540680 | tf_op jit(solution)/shard_map/ppermute | solution.py:345
  56.1 7.7 %collective-permute-start.8 = (bf16[128,704]{1,0:T(8,128)(2,1)S(1)}, bf16[128,704]{1,0:T(8,128)(2,1)S(1)}, u32[]{:S(2)}, u32[]{:S(2)}) collective-permute-start(bf16[128,704]{1,0:T(8,128)(2,1)S(1)} %collective-permute-done.refs_1_), channel_id=1, source_target_pairs={{0,1},{1,0},{2,3},{3,2},{4,5},{5,4},{6,7},{7,6},{8,9},{9,8},{10,11... | collective-permute-start | bytes 540680 | tf_op jit(solution)/shard_map/ppermute | solution.py:345
  58.1 5.7 %collective-permute-start.9 = (bf16[128,704]{1,0:T(8,128)(2,1)S(1)}, bf16[128,704]{1,0:T(8,128)(2,1)}, u32[]{:S(2)}, u32[]{:S(2)}) collective-permute-start(bf16[128,704]{1,0:T(8,128)(2,1)S(1)} %collective-permute-done.1.refs_2_), channel_id=1, source_target_pairs={{0,1},{1,0},{2,3},{3,2},{4,5},{5,4},{6,7},{7,6},{8,9},{9,8},{10,11... | collective-permute-start | bytes 540680 | tf_op jit(solution)/shard_map/ppermute | solution.py:345
  58.2 5.6 %collective-permute-start.12 = (bf16[128,704]{1,0:T(8,128)(2,1)S(1)}, bf16[128,704]{1,0:T(8,128)(2,1)}, u32[]{:S(2)}, u32[]{:S(2)}) collective-permute-start(bf16[128,704]{1,0:T(8,128)(2,1)S(1)} %collective-permute-done.4.refs_5_), channel_id=1, source_target_pairs={{0,1},{1,0},{2,3},{3,2},{4,5},{5,4},{6,7},{7,6},{8,9},{9,8},{10,11... | collective-permute-start | bytes 540680 | tf_op jit(solution)/shard_map/ppermute | solution.py:345
  58.6 5.2 %collective-permute-start.13 = (bf16[128,704]{1,0:T(8,128)(2,1)S(1)}, bf16[128,704]{1,0:T(8,128)(2,1)}, u32[]{:S(2)}, u32[]{:S(2)}) collective-permute-start(bf16[128,704]{1,0:T(8,128)(2,1)S(1)} %collective-permute-done.5.refs_6_), channel_id=1, source_target_pairs={{0,1},{1,0},{2,3},{3,2},{4,5},{5,4},{6,7},{7,6},{8,9},{9,8},{10,11... | collective-permute-start | bytes 540680 | tf_op jit(solution)/shard_map/ppermute | solution.py:345
  58.7 5.1 %collective-permute-start.14 = (bf16[128,704]{1,0:T(8,128)(2,1)S(1)}, bf16[128,704]{1,0:T(8,128)(2,1)}, u32[]{:S(2)}, u32[]{:S(2)}) collective-permute-start(bf16[128,704]{1,0:T(8,128)(2,1)S(1)} %collective-permute-done.6.refs_7_), channel_id=1, source_target_pairs={{0,1},{1,0},{2,3},{3,2},{4,5},{5,4},{6,7},{7,6},{8,9},{9,8},{10,11... | collective-permute-start | bytes 540680 | tf_op jit(solution)/shard_map/ppermute | solution.py:345
  59.1 20.5 %all-to-all-start.2 = ((bf16[16,64,256]{2,1,0:T(8,128)(2,1)}), bf16[16,64,256]{2,1,0:T(8,128)(2,1)S(1)}, u32[]{:S(2)}, u32[]{:S(2)}) async-start(bf16[16,64,256]{2,1,0:T(8,128)(2,1)} %reshape.383), calls=%async_computation.2 | async-start | bytes 1048576 | tf_op jit(solution)/shard_map/all_to_all | solution.py:343
  79.6 21.1 %all-to-all-start.1 = ((f32[8,16,2048]{2,1,0:T(8,128)}), f32[8,16,2048]{2,1,0:T(8,128)S(1)}, u32[]{:S(2)}, u32[]{:S(2)}) async-start(f32[8,16,2048]{2,1,0:T(8,128)} %bitcast.73), calls=%async_computation.1 | async-start | bytes 2097152 | tf_op jit(solution)/shard_map/all_to_all | solution.py:378
  104.8 14.2 %all-to-all-start.3 = ((bf16[16,128,128]{2,1,0:T(8,128)(2,1)}), bf16[16,128,128]{2,1,0:T(8,128)(2,1)S(1)}, u32[]{:S(2)}, u32[]{:S(2)}) async-start(bf16[16,128,128]{2,1,0:T(8,128)(2,1)} %get-tuple-element.45), calls=%async_computation.3 | async-start | bytes 1048576 | tf_op jit(solution)/shard_map/all_to_all | solution.py:420
  119.9 14.6 %all-to-all-start.4 = ((bf16[16,24,128]{2,1,0:T(8,128)(2,1)}), bf16[16,24,128]{2,1,0:T(8,128)(2,1)S(1)}, u32[]{:S(2)}, u32[]{:S(2)}) async-start(bf16[16,24,128]{2,1,0:T(8,128)(2,1)} %fusion.7), calls=%async_computation.4 | async-start | bytes 196608 | tf_op jit(solution)/shard_map/all_to_all | solution.py:425
  135.5 17.9 %all-to-all-start.5 = ((f32[16,80,128]{2,1,0:T(8,128)}), f32[16,80,128]{2,1,0:T(8,128)S(1)}, u32[]{:S(2)}, u32[]{:S(2)}) async-start(f32[16,80,128]{2,1,0:T(8,128)} %constant_dynamic-update-slice_fusion), calls=%async_computation.5 | async-start | bytes 1310720 | tf_op jit(solution)/shard_map/all_to_all | solution.py:435
  (17 other events, 172.2 us)

commit v5 on v4

--- a/solution.py
+++ b/solution.py
@@ -418,6 +418,7 @@
     )(score_grad, loss, iq, index_keys)
 
     key_sum = lax.all_to_all(key_part, HEAD, 0, 0, tiled=True)
+    key_sum, packed = lax.optimization_barrier((key_sum, packed))
     key_sum = jnp.sum(key_sum.astype(f32), axis=0)
     back = lax.dot_general(
         got_rows, key_sum.astype(bf16), (((0,), (1,)), ((), ())), preferred_element_type=bf16

time: 157 us -> 157 us (level)
    all_to_all x1, waiting for transfers between devices: 5.63 us -> 9.61 us  [body(): back = lax.all_to_all(back, CTX, 0, 0, tiled=True)]
    all_to_all x1, waiting for transfers between devices: 9.83 us -> 5.85 us  [body(): key_sum = lax.all_to_all(key_part, HEAD, 0, 0, tiled=True)]
where the time goes in v5:
time: 157 us
  starting transfers between devices  60 us (38%)
  waiting for transfers between devices  51.4 us (33%)
  Pallas kernels  28.4 us (18%)
  local copies, waits for them, and re-layouts  10.5 us (7%)
  other arithmetic  3.81 us (2%)
    pallas_call x1, Pallas kernels, body(): pl.pallas_call(attend_kernel, grid_spec=pltpu.PrefetchScalarGridSpec(num_...  15.1 us
    all_to_all x1, waiting for transfers between devices, body(): target_parts = lax.all_to_all(target_part, ('yl', 'x'), 0, 0, tiled=True)  14.1 us
    ppermute x8, starting transfers between devices, body(): pieces += [lax.ppermute(piece, 'core', swap) for piece in pieces]  12.2 us
    all_to_all x1, waiting for transfers between devices, body(): packed = lax.all_to_all(packed, ROWS, 0, 0, tiled=True)  11.9 us
    all_to_all x1, starting transfers between devices, body(): arrived = lax.all_to_all(send, CTX, 0, 0, tiled=True)  11.9 us
    ppermute x6, starting transfers between devices, shifted(): return lax.ppermute(value, 'x', ring)  9.64 us
    all_to_all x1, waiting for transfers between devices, body(): back = lax.all_to_all(back, CTX, 0, 0, tiled=True)  9.61 us
    all_to_all x1, waiting for transfers between devices, body(): arrived = lax.all_to_all(send, CTX, 0, 0, tiled=True)  7.85 us
  transfers between devices with their start and end apart: 22, of which 7 were waited for; matrix products, arithmetic and copies ran while one was open for 6% of the time, Pallas kernels for 13%

profile of v5, /device:TPU:1, one launch (start us, length us, event | category | flops | bytes accessed | tf_op | source)
XLA Modules:
  0.0 156.5 jit_solution(15175672819403574502)
XLA Ops:
  0.7 3.4 %stripes.1 = bf16[384,704]{1,0:T(8,128)(2,1)} custom-call(s32[16,16]{1,0:T(8,128)} %selection.1, bf16[768,128]{1,0:T(8,128)(2,1)} %index_key.1, bf16[576,768]{1,0:T(8,128)(2,1)} %bitcast.75), custom_call_target="tpu_custom_call" | custom-call | tf_op jit(solution)/shard_map/stripes/pallas_call | solution.py:271
  4.1 11.9 %all-to-all-start = ((bf16[16,24,704]{2,1,0:T(8,128)(2,1)}), bf16[16,24,704]{2,1,0:T(8,128)(2,1)S(1)}, u32[]{:S(2)}, u32[]{:S(2)}) async-start(bf16[16,24,704]{2,1,0:T(8,128)(2,1)} %bitcast.71), calls=%async_computation | async-start | bytes 1179648 | tf_op jit(solution)/shard_map/all_to_all | solution.py:281
  20.3 1.8 %mul.164 = bf16[128,384]{1,0:T(8,128)(2,1)S(1)} reshape(bf16[16,8,48,8]{3,2,1,0:T(8,128)(2,1)S(1)} %broadcast_multiply_fusion) | data formatting | bytes 196608 | tf_op jit(solution)/shard_map/mul | solution.py:240
  26.6 7.8 %all-to-all-done = bf16[16,24,704]{2,1,0:T(8,128)(2,1)S(1)} async-done(((bf16[16,24,704]{2,1,0:T(8,128)(2,1)}), bf16[16,24,704]{2,1,0:T(8,128)(2,1)S(1)}, u32[]{:S(2)}, u32[]{:S(2)}) %all-to-all-start) | async-done | bytes 540704 | tf_op jit(solution)/shard_map/all_to_all | solution.py:281
  35.2 2.7 %collective-permute-start.2 = (bf16[128,704]{1,0:T(8,128)(2,1)S(1)}, bf16[128,704]{1,0:T(8,128)(2,1)S(1)}, u32[]{:S(2)}, u32[]{:S(2)}) collective-permute-start(bf16[128,704]{1,0:T(8,128)(2,1)S(1)} %fusion.26.refs_0_), channel_id=1, source_target_pairs={{0,4},{2,6},{4,0},{6,2},{1,5},{3,7},{5,1},{7,3},{8,12},{10,14},{12... | collective-permute-start | bytes 540680 | tf_op jit(solution)/shard_map/ppermute | solution.py:269
  40.5 1.5 collective-permute-start.5
  42.0 1.5 collective-permute-start.6
  43.8 2.4 %collective-permute-start.1 = (bf16[128,704]{1,0:T(8,128)(2,1)S(1)}, bf16[128,704]{1,0:T(8,128)(2,1)S(1)}, u32[]{:S(2)}, u32[]{:S(2)}) collective-permute-start(bf16[128,704]{1,0:T(8,128)(2,1)S(1)} %fusion.26.refs_0_), channel_id=1, source_target_pairs={{0,6},{2,0},{4,2},{6,4},{1,7},{3,1},{5,3},{7,5},{8,14},{10,8},{12,... | collective-permute-start | bytes 540680 | tf_op jit(solution)/shard_map/ppermute | solution.py:269
  46.9 7.6 %collective-permute-start.7 = (bf16[128,704]{1,0:T(8,128)(2,1)S(1)}, bf16[128,704]{1,0:T(8,128)(2,1)S(1)}, u32[]{:S(2)}, u32[]{:S(2)}) collective-permute-start(bf16[128,704]{1,0:T(8,128)(2,1)S(1)} %fusion.26.refs_0_), channel_id=1, source_target_pairs={{0,1},{1,0},{2,3},{3,2},{4,5},{5,4},{6,7},{7,6},{8,9},{9,8},{10,11... | collective-permute-start | bytes 540680 | tf_op jit(solution)/shard_map/ppermute | solution.py:345
  54.5 1.5 collective-permute-start.11
  56.1 2.0 %collective-permute-start.8 = (bf16[128,704]{1,0:T(8,128)(2,1)S(1)}, bf16[128,704]{1,0:T(8,128)(2,1)S(1)}, u32[]{:S(2)}, u32[]{:S(2)}) collective-permute-start(bf16[128,704]{1,0:T(8,128)(2,1)S(1)} %collective-permute-done.refs_1_), channel_id=1, source_target_pairs={{0,1},{1,0},{2,3},{3,2},{4,5},{5,4},{6,7},{7,6},{8,9},{9,8},{10,11... | collective-permute-start | bytes 540680 | tf_op jit(solution)/shard_map/ppermute | solution.py:345
  59.1 4.6 %all-to-all-start.2 = ((bf16[16,64,256]{2,1,0:T(8,128)(2,1)}), bf16[16,64,256]{2,1,0:T(8,128)(2,1)S(1)}, u32[]{:S(2)}, u32[]{:S(2)}) async-start(bf16[16,64,256]{2,1,0:T(8,128)(2,1)} %reshape.383), calls=%async_computation.2 | async-start | bytes 1048576 | tf_op jit(solution)/shard_map/all_to_all | solution.py:343
  64.4 15.1 %attend.1 = (f32[128,2048]{1,0:T(8,128)}, bf16[2048,128]{1,0:T(8,128)(2,1)}) custom-call(s32[20]{0:T(128)} %concatenate.6.facts, bf16[128,704]{1,0:T(8,128)(2,1)} %copy-done.5, bf16[128,704]{1,0:T(8,128)(2,1)} %copy-done.13, bf16[128,704]{1,0:T(8,128)(2,1)} %copy-done.14, bf16[128,704]{1,0:T(8,128)(2,1)} %copy-done.9, bf16[128,704]{1,0:T(8,128)(2,1)} %copy-done.8, ...), custom_call_target="tpu_custom_call" | custom-call | flops 4831838208 | bytes 8388608 | tf_op jit(solution)/shard_map/attend/pallas_call | solution.py:348
  79.6 5.2 %all-to-all-start.1 = ((f32[8,16,2048]{2,1,0:T(8,128)}), f32[8,16,2048]{2,1,0:T(8,128)S(1)}, u32[]{:S(2)}, u32[]{:S(2)}) async-start(f32[8,16,2048]{2,1,0:T(8,128)} %bitcast.73), calls=%async_computation.1 | async-start | bytes 2097152 | tf_op jit(solution)/shard_map/all_to_all | solution.py:378
  84.9 1.7 %score.1 = f32[16,2048]{1,0:T(8,128)S(1)} custom-call(bf16[16,64,256]{2,1,0:T(8,128)(2,1)S(1)} %all-to-all-done.2.queries, bf16[2048,128]{1,0:T(8,128)(2,1)S(1)} %copy-done.2), custom_call_target="tpu_custom_call" | custom-call | flops 536870912 | bytes 1048576 | tf_op jit(solution)/shard_map/score/pallas_call | solution.py:381
  86.6 14.1 %all-to-all-done.1.target_parts = f32[8,16,2048]{2,1,0:T(8,128)S(1)} async-done(((f32[8,16,2048]{2,1,0:T(8,128)}), f32[8,16,2048]{2,1,0:T(8,128)S(1)}, u32[]{:S(2)}, u32[]{:S(2)}) %all-to-all-start.1) | async-done | bytes 1048608 | tf_op jit(solution)/shard_map/all_to_all | solution.py:378
  100.7 4.2 %key_grad.1 = (f32[64,2048]{1,0:T(8,128)S(1)}, f32[16,1]{1,0:T(8,128)S(1)}, bf16[16,128,128]{2,1,0:T(8,128)(2,1)}) custom-call(s32[20]{0:T(128)S(1)} %copy-done.1, f32[8,16,2048]{2,1,0:T(8,128)S(1)} %all-to-all-done.1.target_parts, f32[16,2048]{1,0:T(8,128)S(1)} %score.1, bf16[16,64,256]{2,1,0:T(8,128)(2,1)S(1)} %all-to-all-done.2.queries, ...), custom_call_target="tpu_custom_call" | custom-call | flops 1073741824 | bytes 4194304 | tf_op jit(solution)/shard_map/key_grad/pallas_call | solution.py:392
  104.8 4.2 %all-to-all-start.3 = ((bf16[16,128,128]{2,1,0:T(8,128)(2,1)}), bf16[16,128,128]{2,1,0:T(8,128)(2,1)S(1)}, u32[]{:S(2)}, u32[]{:S(2)}) async-start(bf16[16,128,128]{2,1,0:T(8,128)(2,1)} %get-tuple-element.44), calls=%async_computation.3 | async-start | bytes 1048576 | tf_op jit(solution)/shard_map/all_to_all | solution.py:420
  109.2 4.0 %query_grad.1 = f32[16,80,128]{2,1,0:T(8,128)} custom-call(f32[64,2048]{1,0:T(8,128)S(1)} %get-tuple-element.45.score_grad, f32[16,1]{1,0:T(8,128)S(1)} %get-tuple-element.46.loss, bf16[16,64,256]{2,1,0:T(8,128)(2,1)S(1)} %all-to-all-done.2.queries, bf16[2048,128]{1,0:T(8,128)(2,1)S(1)} %copy-done.2), custom_call_target="tpu_custom_call" | custom-call | flops 1073741824 | bytes 4194304 | tf_op jit(solution)/shard_map/query_grad/pallas_call | solution.py:409
  113.1 5.8 %all-to-all-done.3 = bf16[16,128,128]{2,1,0:T(8,128)(2,1)S(1)} async-done(((bf16[16,128,128]{2,1,0:T(8,128)(2,1)}), bf16[16,128,128]{2,1,0:T(8,128)(2,1)S(1)}, u32[]{:S(2)}, u32[]{:S(2)}) %all-to-all-start.3) | async-done | bytes 524320 | tf_op jit(solution)/shard_map/all_to_all | solution.py:420
  119.9 4.9 %all-to-all-start.4 = ((bf16[16,24,128]{2,1,0:T(8,128)(2,1)}), bf16[16,24,128]{2,1,0:T(8,128)(2,1)S(1)}, u32[]{:S(2)}, u32[]{:S(2)}) async-start(bf16[16,24,128]{2,1,0:T(8,128)(2,1)} %fusion.7), calls=%async_computation.4 | async-start | bytes 196608 | tf_op jit(solution)/shard_map/all_to_all | solution.py:426
  124.9 9.6 %all-to-all-done.4 = bf16[16,24,128]{2,1,0:T(8,128)(2,1)S(1)} async-done(((bf16[16,24,128]{2,1,0:T(8,128)(2,1)}), bf16[16,24,128]{2,1,0:T(8,128)(2,1)S(1)}, u32[]{:S(2)}, u32[]{:S(2)}) %all-to-all-start.4) | async-done | bytes 98336 | tf_op jit(solution)/shard_map/all_to_all | solution.py:426
  135.5 5.9 %all-to-all-start.5 = ((f32[16,80,128]{2,1,0:T(8,128)}), f32[16,80,128]{2,1,0:T(8,128)S(1)}, u32[]{:S(2)}, u32[]{:S(2)}) async-start(f32[16,80,128]{2,1,0:T(8,128)} %constant_dynamic-update-slice_fusion), calls=%async_computation.5 | async-start | bytes 1310720 | tf_op jit(solution)/shard_map/all_to_all | solution.py:436
  141.5 11.9 %all-to-all-done.5 = f32[16,80,128]{2,1,0:T(8,128)S(1)} async-done(((f32[16,80,128]{2,1,0:T(8,128)}), f32[16,80,128]{2,1,0:T(8,128)S(1)}, u32[]{:S(2)}, u32[]{:S(2)}) %all-to-all-start.5) | async-done | bytes 655392 | tf_op jit(solution)/shard_map/all_to_all | solution.py:436
  (122 shorter events, 20.0 us)
Async XLA Ops:
  0.6 25.9 %copy-start = (f32[256]{0:T(256)S(1)}, f32[256]{0:T(256)}, u32[]{:S(2)}) copy-start(f32[256]{0:T(256)} %param.13) | copy-start | bytes 3076
  4.1 30.3 %all-to-all-start = ((bf16[16,24,704]{2,1,0:T(8,128)(2,1)}), bf16[16,24,704]{2,1,0:T(8,128)(2,1)S(1)}, u32[]{:S(2)}, u32[]{:S(2)}) async-start(bf16[16,24,704]{2,1,0:T(8,128)(2,1)} %bitcast.71), calls=%async_computation | async-start | bytes 1179648 | tf_op jit(solution)/shard_map/all_to_all | solution.py:281
  17.2 26.3 %collective-permute-start.15 = (bf16[8,576,128]{2,1,0:T(8,128)(2,1)}, bf16[8,576,128]{2,1,0:T(8,128)(2,1)}, u32[]{:S(2)}, u32[]{:S(2)}) collective-permute-start(bf16[8,576,128]{2,1,0:T(8,128)(2,1)} %dynamic-slice_bitcast_fusion), channel_id=1, source_target_pairs={{0,1},{1,0},{2,3},{3,2},{4,5},{5,4},{6,7},{7,6},{8,9},{9,8},{10,11... | collective-permute-start | bytes 3538952 | tf_op jit(solution)/shard_map/ppermute | solution.py:285
  34.7 29.1 %copy-start.5 = (bf16[128,704]{1,0:T(8,128)(2,1)}, bf16[128,704]{1,0:T(8,128)(2,1)S(1)}, u32[]{:S(2)}) copy-start(bf16[128,704]{1,0:T(8,128)(2,1)S(1)} %fusion.26.refs_0_) | copy-start | bytes 540676
  34.7 4.6 %collective-permute-start.3 = (bf16[128,704]{1,0:T(8,128)(2,1)S(1)}, bf16[128,704]{1,0:T(8,128)(2,1)S(1)}, u32[]{:S(2)}, u32[]{:S(2)}) collective-permute-start(bf16[128,704]{1,0:T(8,128)(2,1)S(1)} %fusion.26.refs_0_), channel_id=1, source_target_pairs={{0,8},{8,0},{1,9},{9,1},{2,10},{10,2},{3,11},{11,3},{4,12},{12,4},... | collective-permute-start | bytes 540680 | tf_op jit(solution)/shard_map/ppermute | solution.py:339
  35.2 8.7 %collective-permute-start.2 = (bf16[128,704]{1,0:T(8,128)(2,1)S(1)}, bf16[128,704]{1,0:T(8,128)(2,1)S(1)}, u32[]{:S(2)}, u32[]{:S(2)}) collective-permute-start(bf16[128,704]{1,0:T(8,128)(2,1)S(1)} %fusion.26.refs_0_), channel_id=1, source_target_pairs={{0,4},{2,6},{4,0},{6,2},{1,5},{3,7},{5,1},{7,3},{8,12},{10,14},{12... | collective-permute-start | bytes 540680 | tf_op jit(solution)/shard_map/ppermute | solution.py:269
  39.3 7.6 %collective-permute-start.4 = (bf16[128,704]{1,0:T(8,128)(2,1)S(1)}, bf16[128,704]{1,0:T(8,128)(2,1)S(1)}, u32[]{:S(2)}, u32[]{:S(2)}) collective-permute-start(bf16[128,704]{1,0:T(8,128)(2,1)S(1)} %collective-permute-done.3.refs_4_), channel_id=1, source_target_pairs={{0,2},{2,4},{4,6},{6,0},{1,3},{3,5},{5,7},{7,1},{8,10},{10,12},{12... | collective-permute-start | bytes 540680 | tf_op jit(solution)/shard_map/ppermute | solution.py:269
  40.5 13.9 %collective-permute-start.5 = (bf16[128,704]{1,0:T(8,128)(2,1)S(1)}, bf16[128,704]{1,0:T(8,128)(2,1)S(1)}, u32[]{:S(2)}, u32[]{:S(2)}) collective-permute-start(bf16[128,704]{1,0:T(8,128)(2,1)S(1)} %collective-permute-done.3.refs_4_), channel_id=1, source_target_pairs={{0,6},{2,0},{4,2},{6,4},{1,7},{3,1},{5,3},{7,5},{8,14},{10,8},{12,... | collective-permute-start | bytes 540680 | tf_op jit(solution)/shard_map/ppermute | solution.py:269
  42.0 12.6 %collective-permute-start.6 = (bf16[128,704]{1,0:T(8,128)(2,1)S(1)}, bf16[128,704]{1,0:T(8,128)(2,1)S(1)}, u32[]{:S(2)}, u32[]{:S(2)}) collective-permute-start(bf16[128,704]{1,0:T(8,128)(2,1)S(1)} %collective-permute-done.3.refs_4_), channel_id=1, source_target_pairs={{0,4},{2,6},{4,0},{6,2},{1,5},{3,7},{5,1},{7,3},{8,12},{10,14},{12... | collective-permute-start | bytes 540680 | tf_op jit(solution)/shard_map/ppermute | solution.py:269
  43.5 12.6 %collective-permute-start = (bf16[128,704]{1,0:T(8,128)(2,1)S(1)}, bf16[128,704]{1,0:T(8,128)(2,1)S(1)}, u32[]{:S(2)}, u32[]{:S(2)}) collective-permute-start(bf16[128,704]{1,0:T(8,128)(2,1)S(1)} %fusion.26.refs_0_), channel_id=1, source_target_pairs={{0,2},{2,4},{4,6},{6,0},{1,3},{3,5},{5,7},{7,1},{8,10},{10,12},{12... | collective-permute-start | bytes 540680 | tf_op jit(solution)/shard_map/ppermute | solution.py:269
  43.8 14.3 %collective-permute-start.1 = (bf16[128,704]{1,0:T(8,128)(2,1)S(1)}, bf16[128,704]{1,0:T(8,128)(2,1)S(1)}, u32[]{:S(2)}, u32[]{:S(2)}) collective-permute-start(bf16[128,704]{1,0:T(8,128)(2,1)S(1)} %fusion.26.refs_0_), channel_id=1, source_target_pairs={{0,6},{2,0},{4,2},{6,4},{1,7},{3,1},{5,3},{7,5},{8,14},{10,8},{12,... | collective-permute-start | bytes 540680 | tf_op jit(solution)/shard_map/ppermute | solution.py:269
  46.9 11.3 %collective-permute-start.7 = (bf16[128,704]{1,0:T(8,128)(2,1)S(1)}, bf16[128,704]{1,0:T(8,128)(2,1)S(1)}, u32[]{:S(2)}, u32[]{:S(2)}) collective-permute-start(bf16[128,704]{1,0:T(8,128)(2,1)S(1)} %fusion.26.refs_0_), channel_id=1, source_target_pairs={{0,1},{1,0},{2,3},{3,2},{4,5},{5,4},{6,7},{7,6},{8,9},{9,8},{10,11... | collective-permute-start | bytes 540680 | tf_op jit(solution)/shard_map/ppermute | solution.py:345
  54.4 4.2 %collective-permute-start.10 = (bf16[128,704]{1,0:T(8,128)(2,1)S(1)}, bf16[128,704]{1,0:T(8,128)(2,1)S(1)}, u32[]{:S(2)}, u32[]{:S(2)}) collective-permute-start(bf16[128,704]{1,0:T(8,128)(2,1)S(1)} %collective-permute-done.2.refs_3_), channel_id=1, source_target_pairs={{0,1},{1,0},{2,3},{3,2},{4,5},{5,4},{6,7},{7,6},{8,9},{9,8},{10,11... | collective-permute-start | bytes 540680 | tf_op jit(solution)/shard_map/ppermute | solution.py:345
  54.5 4.2 %collective-permute-start.11 = (bf16[128,704]{1,0:T(8,128)(2,1)S(1)}, bf16[128,704]{1,0:T(8,128)(2,1)S(1)}, u32[]{:S(2)}, u32[]{:S(2)}) collective-permute-start(bf16[128,704]{1,0:T(8,128)(2,1)S(1)} %collective-permute-done.3.refs_4_), channel_id=1, source_target_pairs={{0,1},{1,0},{2,3},{3,2},{4,5},{5,4},{6,7},{7,6},{8,9},{9,8},{10,11... | collective-permute-start | bytes 540680 | tf_op jit(solution)/shard_map/ppermute | solution.py:345
  56.1 7.7 %collective-permute-start.8 = (bf16[128,704]{1,0:T(8,128)(2,1)S(1)}, bf16[128,704]{1,0:T(8,128)(2,1)S(1)}, u32[]{:S(2)}, u32[]{:S(2)}) collective-permute-start(bf16[128,704]{1,0:T(8,128)(2,1)S(1)} %collective-permute-done.refs_1_), channel_id=1, source_target_pairs={{0,1},{1,0},{2,3},{3,2},{4,5},{5,4},{6,7},{7,6},{8,9},{9,8},{10,11... | collective-permute-start | bytes 540680 | tf_op jit(solution)/shard_map/ppermute | solution.py:345
  58.1 5.7 %collective-permute-start.9 = (bf16[128,704]{1,0:T(8,128)(2,1)S(1)}, bf16[128,704]{1,0:T(8,128)(2,1)}, u32[]{:S(2)}, u32[]{:S(2)}) collective-permute-start(bf16[128,704]{1,0:T(8,128)(2,1)S(1)} %collective-permute-done.1.refs_2_), channel_id=1, source_target_pairs={{0,1},{1,0},{2,3},{3,2},{4,5},{5,4},{6,7},{7,6},{8,9},{9,8},{10,11... | collective-permute-start | bytes 540680 | tf_op jit(solution)/shard_map/ppermute | solution.py:345
  58.2 5.6 %collective-permute-start.12 = (bf16[128,704]{1,0:T(8,128)(2,1)S(1)}, bf16[128,704]{1,0:T(8,128)(2,1)}, u32[]{:S(2)}, u32[]{:S(2)}) collective-permute-start(bf16[128,704]{1,0:T(8,128)(2,1)S(1)} %collective-permute-done.4.refs_5_), channel_id=1, source_target_pairs={{0,1},{1,0},{2,3},{3,2},{4,5},{5,4},{6,7},{7,6},{8,9},{9,8},{10,11... | collective-permute-start | bytes 540680 | tf_op jit(solution)/shard_map/ppermute | solution.py:345
  58.6 5.2 %collective-permute-start.13 = (bf16[128,704]{1,0:T(8,128)(2,1)S(1)}, bf16[128,704]{1,0:T(8,128)(2,1)}, u32[]{:S(2)}, u32[]{:S(2)}) collective-permute-start(bf16[128,704]{1,0:T(8,128)(2,1)S(1)} %collective-permute-done.5.refs_6_), channel_id=1, source_target_pairs={{0,1},{1,0},{2,3},{3,2},{4,5},{5,4},{6,7},{7,6},{8,9},{9,8},{10,11... | collective-permute-start | bytes 540680 | tf_op jit(solution)/shard_map/ppermute | solution.py:345
  58.7 5.1 %collective-permute-start.14 = (bf16[128,704]{1,0:T(8,128)(2,1)S(1)}, bf16[128,704]{1,0:T(8,128)(2,1)}, u32[]{:S(2)}, u32[]{:S(2)}) collective-permute-start(bf16[128,704]{1,0:T(8,128)(2,1)S(1)} %collective-permute-done.6.refs_7_), channel_id=1, source_target_pairs={{0,1},{1,0},{2,3},{3,2},{4,5},{5,4},{6,7},{7,6},{8,9},{9,8},{10,11... | collective-permute-start | bytes 540680 | tf_op jit(solution)/shard_map/ppermute | solution.py:345
  59.1 20.5 %all-to-all-start.2 = ((bf16[16,64,256]{2,1,0:T(8,128)(2,1)}), bf16[16,64,256]{2,1,0:T(8,128)(2,1)S(1)}, u32[]{:S(2)}, u32[]{:S(2)}) async-start(bf16[16,64,256]{2,1,0:T(8,128)(2,1)} %reshape.383), calls=%async_computation.2 | async-start | bytes 1048576 | tf_op jit(solution)/shard_map/all_to_all | solution.py:343
  79.6 21.1 %all-to-all-start.1 = ((f32[8,16,2048]{2,1,0:T(8,128)}), f32[8,16,2048]{2,1,0:T(8,128)S(1)}, u32[]{:S(2)}, u32[]{:S(2)}) async-start(f32[8,16,2048]{2,1,0:T(8,128)} %bitcast.73), calls=%async_computation.1 | async-start | bytes 2097152 | tf_op jit(solution)/shard_map/all_to_all | solution.py:378
  104.8 14.2 %all-to-all-start.3 = ((bf16[16,128,128]{2,1,0:T(8,128)(2,1)}), bf16[16,128,128]{2,1,0:T(8,128)(2,1)S(1)}, u32[]{:S(2)}, u32[]{:S(2)}) async-start(bf16[16,128,128]{2,1,0:T(8,128)(2,1)} %get-tuple-element.44), calls=%async_computation.3 | async-start | bytes 1048576 | tf_op jit(solution)/shard_map/all_to_all | solution.py:420
  119.9 14.6 %all-to-all-start.4 = ((bf16[16,24,128]{2,1,0:T(8,128)(2,1)}), bf16[16,24,128]{2,1,0:T(8,128)(2,1)S(1)}, u32[]{:S(2)}, u32[]{:S(2)}) async-start(bf16[16,24,128]{2,1,0:T(8,128)(2,1)} %fusion.7), calls=%async_computation.4 | async-start | bytes 196608 | tf_op jit(solution)/shard_map/all_to_all | solution.py:426
  135.5 17.9 %all-to-all-start.5 = ((f32[16,80,128]{2,1,0:T(8,128)}), f32[16,80,128]{2,1,0:T(8,128)S(1)}, u32[]{:S(2)}, u32[]{:S(2)}) async-start(f32[16,80,128]{2,1,0:T(8,128)} %constant_dynamic-update-slice_fusion), calls=%async_computation.5 | async-start | bytes 1310720 | tf_op jit(solution)/shard_map/all_to_all | solution.py:436
  (17 other events, 172.2 us)
